TPU v7x, 512 devices: a whole 4x8x8 slice. The times are simulated.
512 devices in a mesh: section: 8 (over x, core), fsdp: 16 (over z_lo, y), tp: 4 (over z_hi).
Axes of the slice: x: 4, y: 8, z: 8 (z_hi: 4, z_lo: 2; z = z_hi * 2 + z_lo), core: 2. Of those that a mesh axis runs over, the one named last changes fastest.
Arguments:
- queries: bfloat16 [8, 2048, 4096], P('section', 'fsdp', 'tp'), may hold values from -160 to 160
- key_rows: bfloat16 [8, 2048, 512], P('section', 'fsdp', 'tp'), may hold values from -8 to 8
- values: bfloat16 [8, 2048, 512], P('section', 'fsdp', 'tp'), may hold values from -6 to 6
- segments: int32 [8, 2048], P('section', 'fsdp'), may hold values from 0 to 15, never falling along the last dimension, each value on 1 to 1152 neighbouring positions
- held_queries: bfloat16 [8, 2048, 4096], P('section', ('fsdp', 'tp')), may hold values from -160 to 160
- held_keys: bfloat16 [8, 2048, 512], P('section', ('fsdp', 'tp')), may hold values from -8 to 8
- held_values: bfloat16 [8, 2048, 512], P('section', ('fsdp', 'tp')), may hold values from -6 to 6
- held_segments: int32 [8, 2048], P('section', 'fsdp'), may hold values from 0 to 15, never falling along the last dimension, each value on 1 to 1152 neighbouring positions
- out_grad: bfloat16 [8, 2048, 4096], P('section', 'fsdp', 'tp'), may hold values from -6 to 6
Outputs:
- attn_out: bfloat16 [8, 2048, 4096], P('section', 'fsdp', 'tp')
- query_grad: bfloat16 [8, 2048, 4096], P('section', 'fsdp', 'tp')
- key_grad: bfloat16 [8, 2048, 512], P('section', 'fsdp', 'tp')
- value_grad: bfloat16 [8, 2048, 512], P('section', 'fsdp', 'tp')
All inputs are finite; a program needn't handle non-finite values.
Results may differ from a plain program's by a relative error of at most 0.014.
Values may be sent and summed in bfloat16 or wider, within the bound.
No kernel may reach another device: no remote copies, remote signals or barrier semaphores. Data moves between devices by JAX's collectives and lax.ppermute only.
A program may use at most 64 MiB of HBM per device.

v0:
```python
import math

import jax
import jax.numpy as jnp
from jax import lax
from jax.sharding import PartitionSpec as P

HEAD_DIM = 128


NEG = -1e30


def partner(block, axis, apart):
    count = lax.axis_size(axis)
    route = []
    for low in range(count):
        high = low | 1 << apart
        if high != low and high < count:
            route += [(low, high), (high, low)]
    return lax.ppermute(block, axis, route)


def head_split(flat, group_count):
    return flat.reshape(flat.shape[0], group_count, -1, HEAD_DIM)


def visible_pairs(query_pos, query_seg, key_pos, key_seg):
    return (key_pos[None, :] <= query_pos[:, None]) & (key_seg[None, :] == query_seg[:, None])


def online_update(state_carry, query_heads, key_block, value_block, visible):
    running_max, running_sum, accumulated = state_carry
    scores = jnp.einsum(
        "igrd,jgd->igrj", query_heads, key_block, preferred_element_type=jnp.float32
    ) * (1.0 / math.sqrt(HEAD_DIM))
    visible_wide = visible[:, None, None, :]
    scores = jnp.where(visible_wide, scores, NEG)
    new_max = jnp.maximum(running_max, jnp.max(scores, axis=-1))
    weights = jnp.where(visible_wide, jnp.exp(scores - new_max[..., None]), 0.0)
    rescale = jnp.exp(running_max - new_max)
    running_sum = running_sum * rescale + jnp.sum(weights, axis=-1)
    accumulated = accumulated * rescale[..., None] + jnp.einsum(
        "igrj,jgd->igrd",
        weights.astype(jnp.bfloat16),
        value_block,
        preferred_element_type=jnp.float32,
    )
    return (new_max, running_sum, accumulated)


def attend(state_carry, query_heads, visible, key_block, value_block):
    return online_update(state_carry, query_heads, key_block, value_block, visible)


def block_grads(query_heads, grad_heads, log_total, delta_rows, visible, key_block, value_block):
    scores = jnp.einsum(
        "igrd,jgd->igrj", query_heads, key_block, preferred_element_type=jnp.float32
    ) * (1.0 / math.sqrt(HEAD_DIM))
    probabilities = jnp.where(
        visible[:, None, None, :], jnp.exp(scores - log_total[..., None]), 0.0
    )
    value_part = jnp.einsum(
        "igrj,igrd->jgd",
        probabilities.astype(jnp.bfloat16),
        grad_heads,
        preferred_element_type=jnp.float32,
    )
    prob_grad = jnp.einsum(
        "igrd,jgd->igrj", grad_heads, value_block, preferred_element_type=jnp.float32
    )
    score_grad = (probabilities * (prob_grad - delta_rows[..., None])).astype(jnp.bfloat16)
    query_part = jnp.einsum(
        "igrj,jgd->igrd", score_grad, key_block, preferred_element_type=jnp.float32
    )
    key_part = jnp.einsum(
        "igrj,igrd->jgd", score_grad, query_heads, preferred_element_type=jnp.float32
    )
    return (query_part, key_part, value_part)


def masked_grads(query_heads, grad_heads, log_total, delta_rows, visible, key_block, value_block):
    return block_grads(
        query_heads, grad_heads, log_total, delta_rows, visible, key_block, value_block
    )


def local(
    queries,
    key_rows,
    values,
    segments,
    held_queries,
    held_keys,
    held_values,
    held_segments,
    out_grad,
):
    row_count = queries.shape[1]
    group_count = key_rows.shape[2] // HEAD_DIM
    group_ratio = queries.shape[2] // key_rows.shape[2]
    score_scale = 1.0 / math.sqrt(HEAD_DIM)
    own_pos = lax.axis_index("fsdp") * row_count + jnp.arange(row_count, dtype=jnp.int32)
    blank_state = (
        jnp.full((row_count, group_count, group_ratio), NEG, jnp.float32),
        jnp.zeros((row_count, group_count, group_ratio), jnp.float32),
        jnp.zeros((row_count, group_count, group_ratio, HEAD_DIM), jnp.float32),
    )
    fwd_query = head_split(queries[0], group_count)
    fwd_seg = segments[0]
    key_piece = lax.all_gather(key_rows[0], "fsdp", axis=0, tiled=True)
    value_piece = lax.all_gather(values[0], "fsdp", axis=0, tiled=True)
    seg_piece = lax.all_gather(segments[0], "fsdp", axis=0, tiled=True)
    piece_rows = key_piece.shape[0]
    key_pos = jnp.arange(piece_rows, dtype=jnp.int32)
    visible = visible_pairs(own_pos, fwd_seg, key_pos, seg_piece)
    forward_state = attend(
        blank_state,
        fwd_query,
        visible,
        key_piece.reshape(piece_rows, group_count, HEAD_DIM),
        value_piece.reshape(piece_rows, group_count, HEAD_DIM),
    )
    attn_out = (
        (forward_state[2] / forward_state[1][..., None])
        .astype(jnp.bfloat16)
        .reshape(row_count, -1)[None]
    )
    bit_total = lax.axis_size("section").bit_length() - 1
    stash_items = (held_queries, held_keys, held_values, held_segments)
    for bit_index in range(bit_total):
        stash_items = partner(
            (stash_items[0], stash_items[1], stash_items[2], stash_items[3]), "section", bit_index
        )
    stash_query = stash_items[0][0]
    stash_key = stash_items[1][0]
    stash_value = stash_items[2][0]
    back_seg = stash_items[3][0]
    back_query, back_key, back_value = (
        lax.all_to_all(stash_query, "tp", split_axis=1, concat_axis=0, tiled=True),
        lax.all_to_all(stash_key, "tp", split_axis=1, concat_axis=0, tiled=True),
        lax.all_to_all(stash_value, "tp", split_axis=1, concat_axis=0, tiled=True),
    )
    full_key, full_value, full_seg = (
        lax.all_gather(back_key, "fsdp", axis=0, tiled=True),
        lax.all_gather(back_value, "fsdp", axis=0, tiled=True),
        lax.all_gather(back_seg, "fsdp", axis=0, tiled=True),
    )
    seq_len = full_key.shape[0]
    block_rows = min(512, seq_len)
    block_count = seq_len // block_rows
    key_blocks = full_key.reshape(block_count, block_rows, group_count, HEAD_DIM)
    value_blocks = full_value.reshape(block_count, block_rows, group_count, HEAD_DIM)
    seg_blocks = full_seg.reshape(block_count, block_rows)
    pos_blocks = jnp.arange(seq_len, dtype=jnp.int32).reshape(block_count, block_rows)
    back_heads = head_split(back_query, group_count)
    grad_heads = head_split(out_grad[0], group_count)

    def recompute_step(state_carry, block_items):
        key_block, value_block, seg_block, pos_block = block_items
        visible = visible_pairs(own_pos, back_seg, pos_block, seg_block)
        return (attend(state_carry, back_heads, visible, key_block, value_block), None)

    back_state, unused_output = lax.scan(
        recompute_step, blank_state, (key_blocks, value_blocks, seg_blocks, pos_blocks)
    )
    running_max, running_sum, accumulated = back_state
    log_total = running_max + jnp.log(running_sum)
    delta_rows = jnp.sum(
        grad_heads.astype(jnp.float32) * (accumulated / running_sum[..., None]), axis=-1
    )

    def key_block_step(query_sum, block_items):
        key_block, value_block, seg_block, pos_block = block_items
        visible = visible_pairs(own_pos, back_seg, pos_block, seg_block)
        query_part, key_part, value_part = masked_grads(
            back_heads, grad_heads, log_total, delta_rows, visible, key_block, value_block
        )
        return (query_sum + query_part, (key_part, value_part))

    query_zero = jnp.zeros((row_count, group_count, group_ratio, HEAD_DIM), jnp.float32)
    query_total, block_parts = lax.scan(
        key_block_step, query_zero, (key_blocks, value_blocks, seg_blocks, pos_blocks)
    )
    key_parts, value_parts = block_parts
    key_sums, value_sums = (
        lax.psum_scatter(
            key_parts.reshape(seq_len, -1).astype(jnp.bfloat16),
            "fsdp",
            scatter_dimension=0,
            tiled=True,
        ).astype(jnp.float32),
        lax.psum_scatter(
            value_parts.reshape(seq_len, -1).astype(jnp.bfloat16),
            "fsdp",
            scatter_dimension=0,
            tiled=True,
        ).astype(jnp.float32),
    )
    query_grad = (query_total * score_scale).astype(jnp.bfloat16).reshape(row_count, -1)[None]
    key_grad = (key_sums * score_scale).astype(jnp.bfloat16)[None]
    value_grad = value_sums.astype(jnp.bfloat16)[None]
    return (attn_out, query_grad, key_grad, value_grad)


def solution(mesh):
    return jax.shard_map(
        local,
        mesh=mesh,
        in_specs=(
            P("section", "fsdp", "tp"),
            P("section", "fsdp", "tp"),
            P("section", "fsdp", "tp"),
            P("section", "fsdp"),
            P("section", ("fsdp", "tp"), None),
            P("section", ("fsdp", "tp"), None),
            P("section", ("fsdp", "tp"), None),
            P("section", "fsdp"),
            P("section", "fsdp", "tp"),
        ),
        out_specs=(
            P("section", "fsdp", "tp"),
            P("section", "fsdp", "tp"),
            P("section", "fsdp", "tp"),
            P("section", "fsdp", "tp"),
        ),
        check_vma=False,
    )
```

profile of v0, /device:TPU:2, one launch (start us, length us, event | category | flops | bytes accessed | tf_op | source)
XLA Modules:
  0.0 442.7 jit_solution(4457034417724363523)
XLA Ops:
  7.2 1.9 collective-permute-start
  9.1 2.4 collective-permute-start.3
  11.5 1.9 collective-permute-start.6
  13.4 2.4 collective-permute-start.9
  15.9 34.8 %all-gather = s32[1,2048]{1,0:T(1,128)S(1)} all-gather(s32[1,128]{1,0:T(1,128)} %param.16), channel_id=2, replica_groups=mesh['section'=8,'fsdp'=16,'tp'=4] {'fsdp'}, dimensions={1}, use_global_device_ids=true | all-gather | bytes 8704 | tf_op jit(solution)/shard_map/all_gather | solution.py:113
  51.6 2.6 collective-permute-start.1
  54.3 34.5 %all-gather.1 = bf16[1,2048,128]{2,1,0:T(8,128)(2,1)S(1)} all-gather(bf16[1,128,128]{2,1,0:T(8,128)(2,1)} %param.14), channel_id=3, replica_groups=mesh['section'=8,'fsdp'=16,'tp'=4] {'fsdp'}, dimensions={1}, use_global_device_ids=true | all-gather | bytes 557056 | tf_op jit(solution)/shard_map/all_gather | solution.py:111
  88.8 1.0 copy.78
  89.8 1.9 collective-permute-start.10
  91.7 3.7 collective-permute-start.2
  95.4 3.3 collective-permute-start.7
  98.8 4.6 %fusion.48 = (f32[128,8]{0,1:T(8,128)S(1)}, f32[2048,128,8]{1,0,2:T(8,128)}) fusion(pred[128,2048]{0,1:T(8,128)(4,1)S(1)} %fusion.61, bf16[128,8,128]{2,1,0:T(8,128)(2,1)S(1)} %bitcast.301, bf16[1,2048,128]{2,1,0:T(8,128)(2,1)S(1)} %all-gather.1), kind=kOutput, calls=%fused_computation.70 | convolution fusion | flops 543161344 | bytes 9441280 | tf_op jit(solution)/shard_map/igrd,jgd->igrj/dot_general | solution.py:34
  103.4 3.6 collective-permute-start.11
  107.7 7.7 %all-to-all-start = ((bf16[32,4,128]{2,0,1:T(8,128)(2,1)}), bf16[32,4,128]{2,0,1:T(8,128)(2,1)S(1)}, u32[]{:S(2)}, u32[]{:S(2)}) async-start(bf16[32,4,128]{2,0,1:T(8,128)(2,1)} %copy.61), calls=%async_computation | async-start | bytes 65536 | tf_op jit(solution)/shard_map/all_to_all | solution.py:141
  115.3 5.4 %collective-permute-start.8 = (bf16[1,32,4096]{2,1,0:T(8,128)(2,1)S(1)}, bf16[1,32,4096]{2,1,0:T(8,128)(2,1)S(1)}, u32[]{:S(2)}, u32[]{:S(2)}) collective-permute-start(bf16[1,32,4096]{2,1,0:T(8,128)(2,1)S(1)} %collective-permute-done.7), channel_id=1, source_target_pairs={{0,256},{256,0},{64,320},{320,64},{128,384},{384,128},{192,448},{4... | collective-permute-start | bytes 786440 | tf_op jit(solution)/shard_map/ppermute | solution.py:21
  120.8 2.5 collective-permute-start.4
  123.9 7.2 %all-to-all-start.2 = ((bf16[32,4,128]{2,0,1:T(8,128)(2,1)}), bf16[32,4,128]{2,0,1:T(8,128)(2,1)S(1)}, u32[]{:S(2)}, u32[]{:S(2)}) async-start(bf16[32,4,128]{2,0,1:T(8,128)(2,1)} %copy.63), calls=%async_computation.2 | async-start | bytes 65536 | tf_op jit(solution)/shard_map/all_to_all | solution.py:142
  131.2 3.3 collective-permute-start.5
  135.0 3.1 collective-permute-done.5
  138.1 31.0 %all-gather.3 = s32[1,2048]{1,0:T(1,128)S(1)} all-gather(s32[1,128]{1,0:T(1,128)S(1)} %collective-permute-done.5), channel_id=5, replica_groups=mesh['section'=8,'fsdp'=16,'tp'=4] {'fsdp'}, dimensions={1}, use_global_device_ids=true | all-gather | bytes 8704 | tf_op jit(solution)/shard_map/all_gather | solution.py:147
  171.3 7.2 %all-to-all-start.1 = ((bf16[32,4,1024]{2,0,1:T(8,128)(2,1)}), bf16[32,4,1024]{2,0,1:T(8,128)(2,1)S(1)}, u32[]{:S(2)}, u32[]{:S(2)}) async-start(bf16[32,4,1024]{2,0,1:T(8,128)(2,1)} %copy.62), calls=%async_computation.1 | async-start | bytes 524288 | tf_op jit(solution)/shard_map/all_to_all | solution.py:140
  178.5 32.9 %all_gather.21 = bf16[2048,128]{1,0:T(8,128)(2,1)S(1)} all-gather(bf16[128,128]{1,0:T(8,128)(2,1)S(1)} %bitcast.318), channel_id=1, replica_groups=mesh['section'=8,'fsdp'=16,'tp'=4] {'fsdp'}, dimensions={0}, use_global_device_ids=true | all-gather | bytes 557056 | tf_op jit(solution)/shard_map/all_gather | solution.py:145
  211.4 36.9 %all_gather.23 = bf16[2048,128]{1,0:T(8,128)(2,1)} all-gather(bf16[128,128]{1,0:T(8,128)(2,1)S(1)} %bitcast.319), channel_id=1, replica_groups=mesh['section'=8,'fsdp'=16,'tp'=4] {'fsdp'}, dimensions={0}, use_global_device_ids=true | all-gather | bytes 557056 | tf_op jit(solution)/shard_map/all_gather | solution.py:146
  248.4 16.6 %while.30 = (s32[]{:T(128)}, f32[128,1,8]{0,2,1:T(8,128)S(1)}, f32[128,1,8]{0,2,1:T(8,128)S(1)}, f32[128,1,8,128]{0,3,2,1:T(8,128)}, s32[4,512]{1,0:T(4,128)S(1)...) while((s32[]{:T(128)}, f32[128,1,8]{0,2,1:T(8,128)S(1)}, ...), condition=%wide.region_5.6_spmd.clone, body=%wide.region_2.5_spmd.clone.sunk | while | flops 275847296 | bytes 12400345 | solution.py:164
  250.1 1.6 fusion.104
  254.3 1.6 fusion.104
  258.4 1.6 fusion.104
  262.6 1.6 fusion.104
  265.0 1.1 multiply_reduce_fusion
  266.1 29.4 %while.31 = (s32[]{:T(128)}, f32[128,1,8,128]{0,3,2,1:T(8,128)}, bf16[4,512,1,128]{3,1,2,0:T(8,128)(2,1)}, bf16[4,512,1,128]{3,1,2,0:T(8,128)(2,1)}, bf16[4,512,...) while((s32[]{:T(128)}, f32[128,1,8,128]{0,3,2,1:T(8,128)}, ...), condition=%wide.region_8.9_spmd.clone, body=%wide.region_7.8_spmd.clone.sunk | while | flops 675217536 | bytes 27285412 | solution.py:182
  267.0 1.3 fusion.115
  268.4 2.1 fusion.116
  270.5 1.4 fusion.117
  274.2 1.3 fusion.115
  275.6 2.3 fusion.116
  277.9 1.4 fusion.117
  281.6 1.3 fusion.115
  283.0 2.3 fusion.116
  285.3 1.4 fusion.117
  289.0 1.3 fusion.115
  290.4 2.3 fusion.116
  292.7 1.4 fusion.117
  295.6 5.1 %fusion.49 = f32[128,8]{0,1:T(8,128)S(1)} fusion(f32[2048,128,8]{1,0,2:T(8,128)} %get-tuple-element.393, f32[128,8]{0,1:T(8,128)S(1)} %broadcast_maximum_fusion, pred[128,2048]{0,1:T(8,128)(4,1)} %copy-done.5), kind=kLoop, calls=%fused_computation.71 | loop fusion | flops 10484736 | bytes 8658944 | tf_op jit(solution)/shard_map/reduce_sum | solution.py:42
  300.7 32.8 %all-gather.2 = bf16[1,2048,128]{1,2,0:T(8,128)(2,1)S(1)} all-gather(bf16[1,128,128]{1,2,0:T(8,128)(2,1)S(1)} %copy.59), channel_id=4, replica_groups=mesh['section'=8,'fsdp'=16,'tp'=4] {'fsdp'}, dimensions={1}, use_global_device_ids=true | all-gather | bytes 557056 | tf_op jit(solution)/shard_map/all_gather | solution.py:112
  333.5 5.6 %fusion.65 = bf16[1,128,128,8]{2,1,3,0:T(8,128)(2,1)S(1)} fusion(f32[2048,128,8]{1,0,2:T(8,128)} %get-tuple-element.393, f32[128,8]{0,1:T(8,128)S(1)} %broadcast_maximum_fusion, pred[128,2048]{0,1:T(8,128)(4,1)S(1)} %copy-done.6, bf16[1,2048,128]{1,2,0:T(8,128)(2,1)S(1)} %all-gather.2, f32[128,8]{0,1:T(8,128)S(1)} %get-tuple-element.391, ...), kind=kOutput, calls=%fused_computation.81 | convolution fusion | flops 547749888 | bytes 9449472 | tf_op jit(solution)/shard_map/igrj,jgd->igrd/dot_general | solution.py:43
  340.9 22.3 %reduce-scatter.3.cloned.1.call-done = bf16[128,128]{1,0:T(8,128)(2,1)} async-done(((bf16[2048,128]{1,0:T(8,128)(2,1)}), bf16[128,128]{1,0:T(8,128)(2,1)}) %reduce-scatter.3.cloned.1.call-update) | async-done | bytes 32784 | tf_op jit(solution)/shard_map/reduce_scatter | solution.py:187
  363.2 1.4 fusion.72
  364.6 71.2 %reduce-scatter.5.cloned.1.call-done = bf16[128,128]{1,0:T(8,128)(2,1)} async-done(((bf16[2048,128]{1,0:T(8,128)(2,1)}), bf16[128,128]{1,0:T(8,128)(2,1)}) %reduce-scatter.5.cloned.1.call-update) | async-done | bytes 32784 | tf_op jit(solution)/shard_map/reduce_scatter | solution.py:193
  (189 shorter events, 25.5 us)
Async XLA Ops:
  7.2 44.5 %collective-permute-start = (bf16[1,32,512]{2,1,0:T(8,128)(2,1)}, bf16[1,32,512]{2,1,0:T(8,128)(2,1)S(1)}, u32[]{:S(2)}, u32[]{:S(2)}) collective-permute-start(bf16[1,32,512]{2,1,0:T(8,128)(2,1)} %param.18), channel_id=1, source_target_pairs={{0,64},{64,0},{128,192},{192,128},{256,320},{320,256},{384,448},{4... | collective-permute-start | bytes 98312 | tf_op jit(solution)/shard_map/ppermute | solution.py:21
  9.1 111.7 %collective-permute-start.3 = (s32[1,128]{1,0:T(1,128)}, s32[1,128]{1,0:T(1,128)S(1)}, u32[]{:S(2)}, u32[]{:S(2)}) collective-permute-start(s32[1,128]{1,0:T(1,128)} %param.20), channel_id=1, source_target_pairs={{0,64},{64,0},{128,192},{192,128},{256,320},{320,256},{384,448},{4... | collective-permute-start | bytes 1544 | tf_op jit(solution)/shard_map/ppermute | solution.py:21
  11.5 83.9 %collective-permute-start.6 = (bf16[1,32,4096]{2,1,0:T(8,128)(2,1)}, bf16[1,32,4096]{2,1,0:T(8,128)(2,1)S(1)}, u32[]{:S(2)}, u32[]{:S(2)}) collective-permute-start(bf16[1,32,4096]{2,1,0:T(8,128)(2,1)} %param.17), channel_id=1, source_target_pairs={{0,64},{64,0},{128,192},{192,128},{256,320},{320,256},{384,448},{4... | collective-permute-start | bytes 786440 | tf_op jit(solution)/shard_map/ppermute | solution.py:21
  13.4 76.3 %collective-permute-start.9 = (bf16[1,32,512]{2,1,0:T(8,128)(2,1)}, bf16[1,32,512]{2,1,0:T(8,128)(2,1)S(1)}, u32[]{:S(2)}, u32[]{:S(2)}) collective-permute-start(bf16[1,32,512]{2,1,0:T(8,128)(2,1)} %param.19), channel_id=1, source_target_pairs={{0,64},{64,0},{128,192},{192,128},{256,320},{320,256},{384,448},{4... | collective-permute-start | bytes 98312 | tf_op jit(solution)/shard_map/ppermute | solution.py:21
  51.6 51.8 %copy-start.5 = (pred[128,2048]{0,1:T(8,128)(4,1)}, pred[128,2048]{0,1:T(8,128)(4,1)S(1)}, u32[]{:S(2)}) copy-start(pred[128,2048]{0,1:T(8,128)(4,1)S(1)} %fusion.61) | copy-start | bytes 786436
  51.6 40.1 %collective-permute-start.1 = (bf16[1,32,512]{2,1,0:T(8,128)(2,1)S(1)}, bf16[1,32,512]{2,1,0:T(8,128)(2,1)S(1)}, u32[]{:S(2)}, u32[]{:S(2)}) collective-permute-start(bf16[1,32,512]{2,1,0:T(8,128)(2,1)S(1)} %collective-permute-done), channel_id=1, source_target_pairs={{0,128},{128,0},{64,192},{192,64},{256,384},{384,256},{320,448},{4... | collective-permute-start | bytes 98312 | tf_op jit(solution)/shard_map/ppermute | solution.py:21
  89.8 13.6 %collective-permute-start.10 = (bf16[1,32,512]{2,1,0:T(8,128)(2,1)S(1)}, bf16[1,32,512]{2,1,0:T(8,128)(2,1)S(1)}, u32[]{:S(2)}, u32[]{:S(2)}) collective-permute-start(bf16[1,32,512]{2,1,0:T(8,128)(2,1)S(1)} %collective-permute-done.9), channel_id=1, source_target_pairs={{0,128},{128,0},{64,192},{192,64},{256,384},{384,256},{320,448},{4... | collective-permute-start | bytes 98312 | tf_op jit(solution)/shard_map/ppermute | solution.py:21
  91.7 15.3 %collective-permute-start.2 = (bf16[1,32,512]{2,1,0:T(8,128)(2,1)S(1)}, bf16[1,32,512]{2,1,0:T(8,128)(2,1)S(1)}, u32[]{:S(2)}, u32[]{:S(2)}) collective-permute-start(bf16[1,32,512]{2,1,0:T(8,128)(2,1)S(1)} %collective-permute-done.1), channel_id=1, source_target_pairs={{0,256},{256,0},{64,320},{320,64},{128,384},{384,128},{192,448},{4... | collective-permute-start | bytes 98312 | tf_op jit(solution)/shard_map/ppermute | solution.py:21
  95.4 19.9 %collective-permute-start.7 = (bf16[1,32,4096]{2,1,0:T(8,128)(2,1)S(1)}, bf16[1,32,4096]{2,1,0:T(8,128)(2,1)S(1)}, u32[]{:S(2)}, u32[]{:S(2)}) collective-permute-start(bf16[1,32,4096]{2,1,0:T(8,128)(2,1)S(1)} %collective-permute-done.6), channel_id=1, source_target_pairs={{0,128},{128,0},{64,192},{192,64},{256,384},{384,256},{320,448},{4... | collective-permute-start | bytes 786440 | tf_op jit(solution)/shard_map/ppermute | solution.py:21
  98.8 35.8 %copy-start.14 = (bf16[1,128,128]{2,1,0:T(8,128)(2,1)S(1)}, bf16[1,128,128]{2,1,0:T(8,128)(2,1)}, u32[]{:S(2)}) copy-start(bf16[1,128,128]{2,1,0:T(8,128)(2,1)} %param.15) | copy-start | bytes 98308
  98.8 35.9 %copy-start.13 = (bf16[1,128,1024]{2,1,0:T(8,128)(2,1)S(1)}, bf16[1,128,1024]{2,1,0:T(8,128)(2,1)}, u32[]{:S(2)}) copy-start(bf16[1,128,1024]{2,1,0:T(8,128)(2,1)} %param.21) | copy-start | bytes 786436
  103.4 19.9 %collective-permute-start.11 = (bf16[1,32,512]{2,1,0:T(8,128)(2,1)S(1)}, bf16[1,32,512]{2,1,0:T(8,128)(2,1)S(1)}, u32[]{:S(2)}, u32[]{:S(2)}) collective-permute-start(bf16[1,32,512]{2,1,0:T(8,128)(2,1)S(1)} %collective-permute-done.10), channel_id=1, source_target_pairs={{0,256},{256,0},{64,320},{320,64},{128,384},{384,128},{192,448},{4... | collective-permute-start | bytes 98312 | tf_op jit(solution)/shard_map/ppermute | solution.py:21
  107.7 16.3 %all-to-all-start = ((bf16[32,4,128]{2,0,1:T(8,128)(2,1)}), bf16[32,4,128]{2,0,1:T(8,128)(2,1)S(1)}, u32[]{:S(2)}, u32[]{:S(2)}) async-start(bf16[32,4,128]{2,0,1:T(8,128)(2,1)} %copy.61), calls=%async_computation | async-start | bytes 65536 | tf_op jit(solution)/shard_map/all_to_all | solution.py:141
  115.3 55.0 %collective-permute-start.8 = (bf16[1,32,4096]{2,1,0:T(8,128)(2,1)S(1)}, bf16[1,32,4096]{2,1,0:T(8,128)(2,1)S(1)}, u32[]{:S(2)}, u32[]{:S(2)}) collective-permute-start(bf16[1,32,4096]{2,1,0:T(8,128)(2,1)S(1)} %collective-permute-done.7), channel_id=1, source_target_pairs={{0,256},{256,0},{64,320},{320,64},{128,384},{384,128},{192,448},{4... | collective-permute-start | bytes 786440 | tf_op jit(solution)/shard_map/ppermute | solution.py:21
  120.8 10.4 %collective-permute-start.4 = (s32[1,128]{1,0:T(1,128)S(1)}, s32[1,128]{1,0:T(1,128)S(1)}, u32[]{:S(2)}, u32[]{:S(2)}) collective-permute-start(s32[1,128]{1,0:T(1,128)S(1)} %collective-permute-done.3), channel_id=1, source_target_pairs={{0,128},{128,0},{64,192},{192,64},{256,384},{384,256},{320,448},{4... | collective-permute-start | bytes 1544 | tf_op jit(solution)/shard_map/ppermute | solution.py:21
  123.9 47.4 %all-to-all-start.2 = ((bf16[32,4,128]{2,0,1:T(8,128)(2,1)}), bf16[32,4,128]{2,0,1:T(8,128)(2,1)S(1)}, u32[]{:S(2)}, u32[]{:S(2)}) async-start(bf16[32,4,128]{2,0,1:T(8,128)(2,1)} %copy.63), calls=%async_computation.2 | async-start | bytes 65536 | tf_op jit(solution)/shard_map/all_to_all | solution.py:142
  131.2 6.9 %collective-permute-start.5 = (s32[1,128]{1,0:T(1,128)S(1)}, s32[1,128]{1,0:T(1,128)S(1)}, u32[]{:S(2)}, u32[]{:S(2)}) collective-permute-start(s32[1,128]{1,0:T(1,128)S(1)} %collective-permute-done.4), channel_id=1, source_target_pairs={{0,256},{256,0},{64,320},{320,64},{128,384},{384,128},{192,448},{4... | collective-permute-start | bytes 1544 | tf_op jit(solution)/shard_map/ppermute | solution.py:21
  171.3 77.0 %all-to-all-start.1 = ((bf16[32,4,1024]{2,0,1:T(8,128)(2,1)}), bf16[32,4,1024]{2,0,1:T(8,128)(2,1)S(1)}, u32[]{:S(2)}, u32[]{:S(2)}) async-start(bf16[32,4,1024]{2,0,1:T(8,128)(2,1)} %copy.62), calls=%async_computation.1 | async-start | bytes 524288 | tf_op jit(solution)/shard_map/all_to_all | solution.py:140
  178.5 184.7 %reduce-scatter.3.cloned.1.call-start = ((), (), s32[]{:S(2)}) async-start(), calls=%async_computation.5 | async-start | bytes 557056 | tf_op jit(solution)/shard_map/reduce_scatter | solution.py:187
  249.1 1.0 copy-start.7
  253.2 1.0 copy-start.7
  257.4 1.0 copy-start.7
  261.5 1.0 copy-start.7
  266.1 0.8 copy-start
  266.2 0.9 copy-start.3
  268.4 2.1 copy-start.9
  268.4 3.6 copy-start.11
  272.0 1.4 copy-start.1
  272.0 1.4 copy-start.4
  272.5 0.8 copy-start.12
  273.3 0.9 copy-start.3
  275.6 2.3 copy-start.9
  275.6 3.8 copy-start.11
  279.4 1.4 copy-start.1
  279.4 1.4 copy-start.4
  280.7 0.9 copy-start.3
  283.0 2.3 copy-start.9
  283.0 3.8 copy-start.11
  286.8 1.4 copy-start.1
  286.8 1.4 copy-start.4
  288.1 0.9 copy-start.3
  290.4 2.3 copy-start.9
  290.4 3.8 copy-start.11
  294.2 1.4 copy-start.1
  294.2 1.4 copy-start.4
  295.6 140.3 %reduce-scatter.5.cloned.1.call-start = ((), (), s32[]{:S(2)}) async-start(), calls=%async_computation.6 | async-start | bytes 557056 | tf_op jit(solution)/shard_map/reduce_scatter | solution.py:193
  295.6 37.9 %copy-start.6 = (pred[128,2048]{0,1:T(8,128)(4,1)S(1)}, pred[128,2048]{0,1:T(8,128)(4,1)}, u32[]{:S(2)}) copy-start(pred[128,2048]{0,1:T(8,128)(4,1)} %copy-done.5) | copy-start | bytes 786436
  333.5 6.5 %copy-start.2 = (f32[128,1,8,128]{0,3,2,1:T(8,128)S(1)}, f32[128,1,8,128]{0,3,2,1:T(8,128)}, u32[]{:S(2)}) copy-start(f32[128,1,8,128]{0,3,2,1:T(8,128)} %get-tuple-element.140) | copy-start | bytes 1572868
  (14 other events, 11.4 us)
Sparse Core Ops, SparseCore 0:
  295.7 67.4 reduce-scatter.2
  366.8 68.9 reduce-scatter.4
where the time goes:
time: 444 us; the launch traced here: 443 us
  blocking collectives  203 us (46%)
  waiting for transfers between devices  96.7 us (22%)
  starting transfers between devices  57.2 us (13%)
  matrix products  42.9 us (10%)
  local copies, waits for them, and re-layouts  14.8 us (3%)
  between operations  14.4 us (3%)
  other arithmetic  13.1 us (3%)
    reduce_scatter x1, waiting for transfers between devices, local(): lax.psum_scatter(value_parts.reshape(seq_len, -1).astype(jnp.bfloat16), '...  71.2 us
    all_gather x1, blocking collectives, local(): lax.all_gather(back_value, 'fsdp', axis=0, tiled=True)  36.9 us
    ppermute x12, starting transfers between devices, partner(): return lax.ppermute(block, axis, route)  35.1 us
    all_gather x1, blocking collectives, local(): seg_piece = lax.all_gather(segments[0], 'fsdp', axis=0, tiled=True)  34.8 us
    all_gather x1, blocking collectives, local(): key_piece = lax.all_gather(key_rows[0], 'fsdp', axis=0, tiled=True)  34.5 us
    all_gather x1, blocking collectives, local(): lax.all_gather(back_key, 'fsdp', axis=0, tiled=True)  32.9 us
    all_gather x1, blocking collectives, local(): value_piece = lax.all_gather(values[0], 'fsdp', axis=0, tiled=True)  32.8 us
    all_gather x1, blocking collectives, local(): lax.all_gather(back_seg, 'fsdp', axis=0, tiled=True)  31 us
  transfers between devices with their start and end apart: 17, of which 3 were waited for; matrix products, arithmetic and copies ran while one was open for 5% of the time, Pallas kernels for 0%

commit v1 on v0

v1 whole, which is shorter than its diff:
```python
import functools
import math

import jax
import jax.numpy as jnp
from jax import lax
from jax.experimental import pallas as pl
from jax.experimental.pallas import tpu as pltpu
from jax.sharding import PartitionSpec as P

HEAD_DIM = 128
ROWS = 128
PIECES = 4
PIECE = ROWS // PIECES
HALO = 10
KEYS = HALO * ROWS
SPAN = 8
HIDDEN = -1e30
TO_LOG2 = math.log2(math.e) / math.sqrt(HEAD_DIM)
STEP = 256
VMEM_LIMIT = 48 * 1024 * 1024

SECTION_PAIRS = [(s, 7 - s) for s in range(8)]
FSDP_SWAP = [(f, f ^ 8) for f in range(16)]
FSDP_NINE = [(f, f + 9) for f in range(7)] + [(f + 9, f) for f in range(7)]
SECTION_FSDP_SWAP = [(s * 16 + f, (7 - s) * 16 + (f ^ 8)) for s in range(8) for f in range(16)]
ROW_GROUPS = [[z * 8 + y for y in range(8)] for z in range(2)]
ROW_TP_GROUPS = [[(z * 8 + y) * 4 + t for y in range(8) for t in range(4)] for z in range(2)]


def nt_dot(a, b):
    return lax.dot_general(a, b, (((1,), (1,)), ((), ())), preferred_element_type=jnp.float32)


def nn_dot(a, b):
    return jnp.dot(a, b, preferred_element_type=jnp.float32)


def write_bias(bias_ref, d, key_seg, query_seg, valid):
    key_wide = jnp.broadcast_to(key_seg, (ROWS, ROWS)).T
    seen = key_wide == jnp.broadcast_to(query_seg, (ROWS, ROWS))
    if d == 0:
        key_pos = lax.broadcasted_iota(jnp.int32, (ROWS, ROWS), 0)
        query_pos = lax.broadcasted_iota(jnp.int32, (ROWS, ROWS), 1)
        seen = seen & (key_pos <= query_pos)
        bias_ref[0:ROWS, :] = jnp.where(seen, 0.0, HIDDEN)
    else:
        shown = jnp.where(valid, 0.0, HIDDEN).astype(jnp.float32)
        bias_ref[d * ROWS : (d + 1) * ROWS, :] = jnp.where(seen, shown, HIDDEN)


def head_scores(keys_ref, bias_ref, scores_ref, query_pair):
    top = jnp.full((1, 2 * ROWS), HIDDEN, jnp.float32)
    for lo in range(0, KEYS, STEP):
        bias = bias_ref[lo : lo + STEP, :]
        raw = nt_dot(keys_ref[lo : lo + STEP, :], query_pair)
        scores = raw * TO_LOG2 + jnp.concatenate([bias, bias], axis=1)
        scores_ref[lo : lo + STEP, :] = scores
        top = jnp.maximum(top, jnp.max(scores, axis=0, keepdims=True))
    return top


def forward_kernel(f_ref, query_ref, gathered_ref, out_ref, keys, values_t, bias, scores):
    f = f_ref[0]
    upper = f >= SPAN
    for d in range(HALO):
        block = f - d
        valid = block >= 0
        block = jnp.maximum(block, 0)
        crossed = jnp.where(upper & (block < SPAN), 1, 0)
        entry = (block & (SPAN - 1)) * 2 + crossed
        keys[d * ROWS : (d + 1) * ROWS, :] = gathered_ref[entry, 0:ROWS, :]
        values_t[:, d * ROWS : (d + 1) * ROWS] = gathered_ref[entry, ROWS : 2 * ROWS, :].T
        key_seg = gathered_ref[entry, 2 * ROWS : 2 * ROWS + 16, :].astype(jnp.float32)[0:1]
        if d == 0:
            query_seg = key_seg
        write_bias(bias, d, key_seg, query_seg, valid)
    for pair in range(4):
        lo_col = pair * 2 * HEAD_DIM
        query_pair = jnp.concatenate(
            [query_ref[:, lo_col : lo_col + 128], query_ref[:, lo_col + 128 : lo_col + 256]], axis=0
        )
        top = head_scores(keys, bias, scores, query_pair)
        total = jnp.zeros((1, 2 * ROWS), jnp.float32)
        summed = jnp.zeros((HEAD_DIM, 2 * ROWS), jnp.float32)
        for lo in range(0, KEYS, STEP):
            weights = jnp.exp2(scores[lo : lo + STEP, :] - top)
            total = total + jnp.sum(weights, axis=0, keepdims=True)
            summed = summed + nn_dot(values_t[:, lo : lo + STEP], weights.astype(jnp.bfloat16))
        result = (summed / total).T.astype(jnp.bfloat16)
        out_ref[:, lo_col : lo_col + 128] = result[0:128]
        out_ref[:, lo_col + 128 : lo_col + 256] = result[128:256]


def backward_kernel(
    f_ref,
    own_ref,
    slots_ref,
    nine_ref,
    grad_ref,
    query_grad_ref,
    send_ref,
    send_nine_ref,
    own_part_ref,
    keys,
    keys_t,
    values,
    bias,
    scores,
    prob_grads,
    key_sum,
    value_sum,
):
    f = f_ref[0]
    y = f & (SPAN - 1)
    upper = f >= SPAN
    for d in range(HALO):
        base = d * ROWS
        slot = (y - d) & (SPAN - 1)
        for piece in range(PIECES):
            at = base + piece * PIECE
            if d == 0:
                key_piece = own_ref[piece, :, 1024:1152]
                value_piece = own_ref[piece, :, 1152:1280]
            elif d == HALO - 1:
                key_piece = nine_ref[piece, :, 0:128]
                value_piece = nine_ref[piece, :, 128:256]
            else:
                key_piece = slots_ref[slot * PIECES + piece, 0:PIECE, :]
                value_piece = slots_ref[slot * PIECES + piece, PIECE : 2 * PIECE, :]
            keys[at : at + PIECE, :] = key_piece
            values[at : at + PIECE, :] = value_piece
        keys_t[:, base : base + ROWS] = keys[base : base + ROWS, :].T
        ids = slots_ref[slot * PIECES, 2 * PIECE : 2 * PIECE + 16, :].astype(jnp.float32)
        if d == 0:
            query_seg = ids[1:2]
            key_seg = query_seg
        elif d == HALO - 1:
            key_seg = ids[2:3]
        else:
            key_seg = ids[0:1]
        valid = (f >= d) if d < HALO - 1 else (upper & (y >= 1))
        write_bias(bias, d, key_seg, query_seg, valid)
    for pair in range(4):
        lo_col = pair * 2 * HEAD_DIM
        query_pair = jnp.concatenate(
            [
                own_ref[piece, :, col : col + 128]
                for col in (lo_col, lo_col + 128)
                for piece in range(PIECES)
            ],
            axis=0,
        )
        grad_pair = jnp.concatenate(
            [grad_ref[:, lo_col : lo_col + 128], grad_ref[:, lo_col + 128 : lo_col + 256]], axis=0
        )
        top = head_scores(keys, bias, scores, query_pair)
        total = jnp.zeros((1, 2 * ROWS), jnp.float32)
        mixed = jnp.zeros((1, 2 * ROWS), jnp.float32)
        for lo in range(0, KEYS, STEP):
            weights = jnp.exp2(scores[lo : lo + STEP, :] - top)
            prob_grad = nt_dot(values[lo : lo + STEP, :], grad_pair)
            total = total + jnp.sum(weights, axis=0, keepdims=True)
            mixed = mixed + jnp.sum(weights * prob_grad, axis=0, keepdims=True)
            scores[lo : lo + STEP, :] = weights
            prob_grads[lo : lo + STEP, :] = prob_grad
        inverse = 1.0 / total
        delta = mixed * inverse
        query_sum = jnp.zeros((HEAD_DIM, 2 * ROWS), jnp.float32)
        for lo in range(0, KEYS, STEP):
            probabilities = scores[lo : lo + STEP, :] * inverse
            score_grad = (probabilities * (prob_grads[lo : lo + STEP, :] - delta)).astype(
                jnp.bfloat16
            )
            value_part = nn_dot(probabilities.astype(jnp.bfloat16), grad_pair)
            key_part = nn_dot(score_grad, query_pair)
            query_sum = query_sum + nn_dot(keys_t[:, lo : lo + STEP], score_grad)
            if pair == 0:
                value_sum[lo : lo + STEP, :] = value_part
                key_sum[lo : lo + STEP, :] = key_part
            else:
                value_sum[lo : lo + STEP, :] += value_part
                key_sum[lo : lo + STEP, :] += key_part
        result = (query_sum * (1.0 / math.sqrt(HEAD_DIM))).T.astype(jnp.bfloat16)
        query_grad_ref[:, lo_col : lo_col + 128] = result[0:128]
        query_grad_ref[:, lo_col + 128 : lo_col + 256] = result[128:256]
    own_part_ref[0:ROWS, :] = key_sum[0:ROWS, :]
    own_part_ref[ROWS : 2 * ROWS, :] = value_sum[0:ROWS, :]
    for d in range(1, HALO):
        key_out = key_sum[d * ROWS : (d + 1) * ROWS, :].astype(jnp.bfloat16)
        value_out = value_sum[d * ROWS : (d + 1) * ROWS, :].astype(jnp.bfloat16)
        if d == HALO - 1:
            send_nine_ref[0:ROWS, :] = key_out
            send_nine_ref[ROWS : 2 * ROWS, :] = value_out
        else:
            slot = (y - d) & (SPAN - 1)
            send_ref[slot, 0:ROWS, :] = key_out
            send_ref[slot, ROWS : 2 * ROWS, :] = value_out


VMEM = pl.BlockSpec(memory_space=pltpu.VMEM)
SMEM = pl.BlockSpec(memory_space=pltpu.SMEM)


def run_forward(f, query, gathered):
    return pl.pallas_call(
        forward_kernel,
        out_shape=jax.ShapeDtypeStruct((ROWS, 1024), jnp.bfloat16),
        in_specs=[SMEM, VMEM, VMEM],
        out_specs=VMEM,
        scratch_shapes=[
            pltpu.VMEM((KEYS, HEAD_DIM), jnp.bfloat16),
            pltpu.VMEM((HEAD_DIM, KEYS), jnp.bfloat16),
            pltpu.VMEM((KEYS, ROWS), jnp.float32),
            pltpu.VMEM((KEYS, 2 * ROWS), jnp.float32),
        ],
        compiler_params=pltpu.CompilerParams(vmem_limit_bytes=VMEM_LIMIT),
        cost_estimate=pl.CostEstimate(
            flops=2 * 2 * 1024 * KEYS * 128, bytes_accessed=3_000_000, transcendentals=1024 * KEYS
        ),
        name="forward_attention",
    )(f, query, gathered)


def run_backward(f, own, slots, nine, grad):
    return pl.pallas_call(
        backward_kernel,
        out_shape=(
            jax.ShapeDtypeStruct((ROWS, 1024), jnp.bfloat16),
            jax.ShapeDtypeStruct((SPAN, 2 * ROWS, HEAD_DIM), jnp.bfloat16),
            jax.ShapeDtypeStruct((2 * ROWS, HEAD_DIM), jnp.bfloat16),
            jax.ShapeDtypeStruct((2 * ROWS, HEAD_DIM), jnp.float32),
        ),
        in_specs=[SMEM, VMEM, VMEM, VMEM, VMEM],
        out_specs=(VMEM, VMEM, VMEM, VMEM),
        scratch_shapes=[
            pltpu.VMEM((KEYS, HEAD_DIM), jnp.bfloat16),
            pltpu.VMEM((HEAD_DIM, KEYS), jnp.bfloat16),
            pltpu.VMEM((KEYS, HEAD_DIM), jnp.bfloat16),
            pltpu.VMEM((KEYS, ROWS), jnp.float32),
            pltpu.VMEM((KEYS, 2 * ROWS), jnp.float32),
            pltpu.VMEM((KEYS, 2 * ROWS), jnp.float32),
            pltpu.VMEM((KEYS, HEAD_DIM), jnp.float32),
            pltpu.VMEM((KEYS, HEAD_DIM), jnp.float32),
        ],
        compiler_params=pltpu.CompilerParams(vmem_limit_bytes=VMEM_LIMIT),
        cost_estimate=pl.CostEstimate(
            flops=5 * 2 * 1024 * KEYS * 128, bytes_accessed=4_000_000, transcendentals=1024 * KEYS
        ),
        name="backward_attention",
    )(f, own, slots, nine, grad)


def local(
    queries,
    key_rows,
    values,
    segments,
    held_queries,
    held_keys,
    held_values,
    held_segments,
    out_grad,
):
    f = lax.axis_index("fsdp").astype(jnp.int32)
    y = f & (SPAN - 1)
    upper = f >= SPAN
    f_arr = f.reshape(1)

    stash = jnp.concatenate(
        [
            held_queries[0].reshape(PIECE, 4, 1024),
            held_keys[0].reshape(PIECE, 4, 128),
            held_values[0].reshape(PIECE, 4, 128),
        ],
        axis=2,
    ).transpose(1, 0, 2)
    stash = lax.all_to_all(stash, "tp", split_axis=0, concat_axis=0, tiled=False)
    own = lax.ppermute(stash, "section", SECTION_PAIRS)

    held_ids = held_segments[0].astype(jnp.bfloat16)
    token_cut = jnp.concatenate(
        [
            held_keys[0].reshape(PIECE, 4, 128).transpose(1, 0, 2),
            held_values[0].reshape(PIECE, 4, 128).transpose(1, 0, 2),
            jnp.broadcast_to(held_ids[None, None, :], (4, 16, 128)),
        ],
        axis=1,
    )
    straight = lax.ppermute(token_cut, "section", SECTION_PAIRS)
    crossed = lax.ppermute(token_cut, ("section", "fsdp"), SECTION_FSDP_SWAP)
    id_rows = lax.broadcasted_iota(jnp.int32, (4, 16, 128), 1)
    target = lax.broadcasted_iota(jnp.int32, (SPAN, 1, 1, 1), 0)
    take_crossed = (target <= y) & upper
    body = jnp.where(take_crossed, crossed[None, :, : 2 * PIECE], straight[None, :, : 2 * PIECE])
    straight_ids = straight[None, :, 2 * PIECE :]
    crossed_ids = crossed[None, :, 2 * PIECE :]
    ids = jnp.where(take_crossed, crossed_ids, straight_ids)
    ids = jnp.where(id_rows[None] == 1, straight_ids, jnp.where(id_rows[None] == 2, crossed_ids, ids))
    outgoing = jnp.concatenate([body, ids], axis=2).reshape(SPAN * 4, 2 * PIECE + 16, 128)
    slots = lax.all_to_all(
        outgoing,
        ("fsdp", "tp"),
        split_axis=0,
        concat_axis=0,
        tiled=False,
        axis_index_groups=ROW_TP_GROUPS,
    )
    nine = lax.ppermute(own[:, :, 1024:], "fsdp", FSDP_NINE)

    ids_low = segments[0].astype(jnp.bfloat16)
    forward_part = jnp.concatenate(
        [key_rows[0], values[0], jnp.broadcast_to(ids_low[None, :], (16, 128))], axis=0
    )
    forward_cross = lax.ppermute(forward_part, "fsdp", FSDP_SWAP)
    gathered = lax.all_gather(
        jnp.stack([forward_part, forward_cross]),
        "fsdp",
        axis=0,
        tiled=True,
        axis_index_groups=ROW_GROUPS,
    )

    query_grad, send, send_nine, own_part = run_backward(f_arr, own, slots, nine, out_grad[0])
    parts = lax.all_to_all(
        send, "fsdp", split_axis=0, concat_axis=0, tiled=False, axis_index_groups=ROW_GROUPS
    )
    from_nine = lax.ppermute(send_nine, "fsdp", FSDP_NINE)
    attn_out = run_forward(f_arr, queries[0], gathered)

    source = lax.broadcasted_iota(jnp.int32, (SPAN, 1, 1), 0)
    parts_wide = parts.astype(jnp.float32)
    same_row = jnp.sum(jnp.where(source > y, parts_wide, 0.0), axis=0) + own_part
    other_row = jnp.sum(jnp.where(source <= y, parts_wide, 0.0), axis=0).astype(jnp.bfloat16)
    from_upper = lax.ppermute(other_row, "fsdp", FSDP_SWAP)
    late = from_upper.astype(jnp.float32) + from_nine.astype(jnp.float32)
    final = same_row + jnp.where(upper, 0.0, late)
    key_grad = (final[:ROWS] * (1.0 / math.sqrt(HEAD_DIM))).astype(jnp.bfloat16)
    value_grad = final[ROWS:].astype(jnp.bfloat16)
    return (attn_out[None], query_grad[None], key_grad[None], value_grad[None])


def solution(mesh):
    return jax.shard_map(
        local,
        mesh=mesh,
        in_specs=(
            P("section", "fsdp", "tp"),
            P("section", "fsdp", "tp"),
            P("section", "fsdp", "tp"),
            P("section", "fsdp"),
            P("section", ("fsdp", "tp"), None),
            P("section", ("fsdp", "tp"), None),
            P("section", ("fsdp", "tp"), None),
            P("section", "fsdp"),
            P("section", "fsdp", "tp"),
        ),
        out_specs=(
            P("section", "fsdp", "tp"),
            P("section", "fsdp", "tp"),
            P("section", "fsdp", "tp"),
            P("section", "fsdp", "tp"),
        ),
        check_vma=False,
    )
```

time: 444 us -> 135 us (0.30)
  the two profiles are of different devices: /device:TPU:2 before, /device:TPU:1 now
where the time goes in v1:
time: 135 us; the launch traced here: 134 us
  starting transfers between devices  55.4 us (41%)
  waiting for transfers between devices  46.3 us (34%)
  between operations  14.3 us (11%)
  Pallas kernels  9.49 us (7%)
  local copies, waits for them, and re-layouts  4.96 us (4%)
  other arithmetic  3.56 us (3%)
    all_to_all x1, waiting for transfers between devices, local(): lax.all_to_all(send, 'fsdp', split_axis=0, concat_axis=0, tiled=False, ax...  13.9 us
    ppermute x1, waiting for transfers between devices, local(): forward_cross = lax.ppermute(forward_part, 'fsdp', FSDP_SWAP)  13.7 us
    all_to_all x1, starting transfers between devices, local(): lax.all_to_all(outgoing, ('fsdp', 'tp'), split_axis=0, concat_axis=0, til...  12.5 us
    all_to_all x1, starting transfers between devices, local(): lax.all_to_all(stash, 'tp', split_axis=0, concat_axis=0, tiled=False)  10.8 us
    all_to_all x1, starting transfers between devices, local(): lax.all_to_all(send, 'fsdp', split_axis=0, concat_axis=0, tiled=False, ax...  10.3 us
    ppermute x1, waiting for transfers between devices, local(): own = lax.ppermute(stash, 'section', SECTION_PAIRS)  9.61 us
    pallas_call x1, Pallas kernels, run_backward(): pl.pallas_call(backward_kernel, out_shape=(jax.ShapeDtypeStruct((ROWS, 10...  6.02 us
    ppermute x1, starting transfers between devices, local(): straight = lax.ppermute(token_cut, 'section', SECTION_PAIRS)  5.23 us
  transfers between devices with their start and end apart: 11, of which 5 were waited for; matrix products, arithmetic and copies ran while one was open for 2% of the time, Pallas kernels for 7%

profile of v1, /device:TPU:1, one launch (start us, length us, event | category | flops | bytes accessed | tf_op | source)
XLA Modules:
  0.0 134.1 jit_solution(15098829058293507201)
XLA Ops:
  7.2 0.8 reshape_squeeze.13
  7.9 0.8 reshape_squeeze.12
  8.7 0.0 copy-start.5
  8.8 1.1 reshape_squeeze.11
  9.9 0.1 copy.20
  10.0 0.8 maximum_bitcast_fusion
  10.7 10.8 %all-to-all-start = ((bf16[4,32,1280]{2,1,0:T(8,128)(2,1)}), bf16[4,32,1280]{2,1,0:T(8,128)(2,1)S(1)}, u32[]{:S(2)}, u32[]{:S(2)}) async-start(bf16[4,32,1280]{2,1,0:T(8,128)(2,1)} %maximum_bitcast_fusion), calls=%async_computation | async-start | bytes 655360 | tf_op jit(solution)/shard_map/all_to_all | solution.py:278
  21.6 0.1 pad_maximum_fusion.2
  21.7 5.2 %collective-permute-start.3 = (bf16[4,80,128]{2,0,1:T(4,128)(2,1)S(1)}, bf16[4,80,128]{2,0,1:T(4,128)(2,1)S(1)}, u32[]{:S(2)}, u32[]{:S(2)}) collective-permute-start(bf16[4,80,128]{2,0,1:T(4,128)(2,1)S(1)} %pad_maximum_fusion.2), channel_id=1, source_target_pairs={{0,448},{64,384},{128,320},{192,256},{256,192},{320,128},{384,64},... | collective-permute-start | bytes 245768 | tf_op jit(solution)/shard_map/ppermute | solution.py:290
  26.9 2.8 %collective-permute-start.2 = (bf16[4,80,128]{2,0,1:T(4,128)(2,1)S(1)}, bf16[4,80,128]{2,0,1:T(4,128)(2,1)S(1)}, u32[]{:S(2)}, u32[]{:S(2)}) collective-permute-start(bf16[4,80,128]{2,0,1:T(4,128)(2,1)S(1)} %pad_maximum_fusion.2), channel_id=1, source_target_pairs={{0,480},{4,484},{8,488},{12,492},{16,496},{20,500},{24,504},{28,50... | collective-permute-start | bytes 245768 | tf_op jit(solution)/shard_map/ppermute | solution.py:291
  29.8 0.1 broadcast_in_dim.143
  29.9 0.1 broadcast_in_dim.144
  30.0 0.0 collective-permute-done.3
  30.0 5.0 %collective-permute-done.2 = bf16[4,80,128]{2,0,1:T(4,128)(2,1)S(1)} collective-permute-done((bf16[4,80,128]{2,0,1:T(4,128)(2,1)S(1)}, bf16[4,80,128]{2,0,1:T(4,128)(2,1)S(1)}, u32[]{:S(2)}, u32[]{:S(2)}) %collective-permute-start.2) | collective-permute-done | bytes 81952 | tf_op jit(solution)/shard_map/ppermute | solution.py:291
  35.1 0.1 bitcast_select_fusion
  35.3 0.1 bitcast_select_fusion.2
  35.4 0.0 copy-start.6
  35.4 0.0 copy-start.3
  35.4 0.0 copy-start.4
  35.4 0.9 pad_maximum_fusion
  36.3 0.0 all-to-all-done
  36.3 12.5 %all-to-all-start.1 = ((bf16[32,80,128]{2,1,0:T(8,128)(2,1)}), bf16[32,80,128]{2,1,0:T(8,128)(2,1)S(1)}, u32[]{:S(2)}, u32[]{:S(2)}) async-start(bf16[32,80,128]{2,1,0:T(8,128)(2,1)} %pad_maximum_fusion), calls=%async_computation.1 | async-start | bytes 1310720 | tf_op jit(solution)/shard_map/all_to_all | solution.py:301
  48.8 0.0 all-gather.2.cloned.1.call-start
  48.9 0.0 copy-done.6
  48.9 3.1 %collective-permute-start = (bf16[272,128]{1,0:T(8,128)(2,1)S(1)}, bf16[272,128]{1,0:T(8,128)(2,1)S(1)}, u32[]{:S(2)}, u32[]{:S(2)}) collective-permute-start(bf16[272,128]{1,0:T(8,128)(2,1)S(1)} %get-tuple-element.15), channel_id=1, source_target_pairs={{0,32},{4,36},{8,40},{12,44},{16,48},{20,52},{24,56},{28,60},{32,0... | collective-permute-start | bytes 208904 | tf_op jit(solution)/shard_map/ppermute | solution.py:315
  52.0 13.7 %collective-permute-done = bf16[272,128]{1,0:T(8,128)(2,1)S(1)} collective-permute-done((bf16[272,128]{1,0:T(8,128)(2,1)S(1)}, bf16[272,128]{1,0:T(8,128)(2,1)S(1)}, u32[]{:S(2)}, u32[]{:S(2)}) %collective-permute-start) | collective-permute-done | bytes 69664 | tf_op jit(solution)/shard_map/ppermute | solution.py:315
  65.7 0.7 pad_maximum_fusion.1
  66.4 0.0 all-gather.2.cloned.1.call-update
  66.4 3.2 %collective-permute-start.1 = (bf16[4,32,1280]{2,1,0:T(8,128)(2,1)S(1)}, bf16[4,32,1280]{2,1,0:T(8,128)(2,1)S(1)}, u32[]{:S(2)}, u32[]{:S(2)}) collective-permute-start(bf16[4,32,1280]{2,1,0:T(8,128)(2,1)S(1)} %all-to-all-done), channel_id=1, source_target_pairs={{0,448},{64,384},{128,320},{192,256},{256,192},{320,128},{384,64},... | collective-permute-start | bytes 983048 | tf_op jit(solution)/shard_map/ppermute | solution.py:279
  69.6 9.6 %collective-permute-done.1.own_ref = bf16[4,32,1280]{2,1,0:T(8,128)(2,1)S(1)} collective-permute-done((bf16[4,32,1280]{2,1,0:T(8,128)(2,1)S(1)}, bf16[4,32,1280]{2,1,0:T(8,128)(2,1)S(1)}, u32[]{:S(2)}, u32[]{:S(2)}) %collective-permute-start.1) | collective-permute-done | bytes 327712 | tf_op jit(solution)/shard_map/ppermute | solution.py:279
  79.2 1.9 %collective-permute-start.4 = (bf16[4,32,256]{2,1,0:T(8,128)(2,1)S(1)}, bf16[4,32,256]{2,1,0:T(8,128)(2,1)S(1)}, u32[]{:S(2)}, u32[]{:S(2)}) collective-permute-start(bf16[4,32,256]{2,1,0:T(8,128)(2,1)S(1)} %slice.33), channel_id=1, source_target_pairs={{0,36},{4,40},{8,44},{12,48},{16,52},{20,56},{24,60},{36,0},{40,4}... | collective-permute-start | bytes 196616 | tf_op jit(solution)/shard_map/ppermute | solution.py:309
  81.1 4.0 %collective-permute-done.4.nine_ref = bf16[4,32,256]{2,1,0:T(8,128)(2,1)S(1)} collective-permute-done((bf16[4,32,256]{2,1,0:T(8,128)(2,1)S(1)}, bf16[4,32,256]{2,1,0:T(8,128)(2,1)S(1)}, u32[]{:S(2)}, u32[]{:S(2)}) %collective-permute-start.4) | collective-permute-done | bytes 65568 | tf_op jit(solution)/shard_map/ppermute | solution.py:309
  85.1 0.0 all-to-all-done.1.slots_ref
  85.1 0.0 copy-done.1
  85.1 6.0 %backward_attention.1 = (bf16[128,1024]{1,0:T(8,128)(2,1)}, bf16[8,256,128]{2,1,0:T(8,128)(2,1)}, bf16[256,128]{1,0:T(8,128)(2,1)S(1)}, f32[256,128]{1,0:T(8,128)S(1)}) custom-call(s32[1]{0:T(128)} %bitcast.f_ref, bf16[4,32,1280]{2,1,0:T(8,128)(2,1)S(1)} %collective-permute-done.1.own_ref, bf16[32,80,128]{2,1,0:T(8,128)(2,1)S(1)} %all-to-all-done.1.slots_ref, ...), custom_call_target="tpu_custom_call" | custom-call | flops 1677721600 | bytes 4000000 | tf_op jit(solution)/shard_map/backward_attention/pallas_call | solution.py:226
  91.1 10.3 %all-to-all-start.2 = ((bf16[8,256,128]{2,1,0:T(8,128)(2,1)}), bf16[8,256,128]{2,1,0:T(8,128)(2,1)S(1)}, u32[]{:S(2)}, u32[]{:S(2)}) async-start(bf16[8,256,128]{2,1,0:T(8,128)(2,1)} %get-tuple-element.9), calls=%async_computation.2 | async-start | bytes 1048576 | tf_op jit(solution)/shard_map/all_to_all | solution.py:325
  101.4 3.6 %collective-permute-start.6 = (bf16[256,128]{1,0:T(8,128)(2,1)S(1)}, bf16[256,128]{1,0:T(8,128)(2,1)S(1)}, u32[]{:S(2)}, u32[]{:S(2)}) collective-permute-start(bf16[256,128]{1,0:T(8,128)(2,1)S(1)} %get-tuple-element.11), channel_id=1, source_target_pairs={{0,36},{4,40},{8,44},{12,48},{16,52},{20,56},{24,60},{36,0},{40,4}... | collective-permute-start | bytes 196616 | tf_op jit(solution)/shard_map/ppermute | solution.py:328
  105.0 13.9 %all-to-all-done.2 = bf16[8,256,128]{2,1,0:T(8,128)(2,1)S(1)} async-done(((bf16[8,256,128]{2,1,0:T(8,128)(2,1)}), bf16[8,256,128]{2,1,0:T(8,128)(2,1)S(1)}, u32[]{:S(2)}, u32[]{:S(2)}) %all-to-all-start.2) | async-done | bytes 524320 | tf_op jit(solution)/shard_map/all_to_all | solution.py:325
  119.0 0.3 fusion
  119.2 1.9 %collective-permute-start.5 = (bf16[256,128]{1,0:T(8,128)(2,1)S(1)}, bf16[256,128]{1,0:T(8,128)(2,1)S(1)}, u32[]{:S(2)}, u32[]{:S(2)}) collective-permute-start(bf16[256,128]{1,0:T(8,128)(2,1)S(1)} %get-tuple-element.13), channel_id=1, source_target_pairs={{0,32},{4,36},{8,40},{12,44},{16,48},{20,52},{24,56},{28,60},{32,0... | collective-permute-start | bytes 196616 | tf_op jit(solution)/shard_map/ppermute | solution.py:335
  121.2 0.0 all-gather.2.cloned.1.call-done.gathered_ref
  121.2 0.0 copy-done.2
  121.2 1.2 copy-done
  122.5 3.5 %forward_attention.1 = bf16[128,1024]{1,0:T(8,128)(2,1)} custom-call(s32[1]{0:T(128)} %bitcast.f_ref, bf16[128,1024]{1,0:T(8,128)(2,1)S(1)} %bitcast.47, bf16[16,272,128]{2,1,0:T(8,128)(2,1)S(1)} %copy-done), custom_call_target="tpu_custom_call" | custom-call | flops 671088640 | bytes 3000000 | tf_op jit(solution)/shard_map/forward_attention/pallas_call | solution.py:206
  125.9 0.0 collective-permute-done.6
  125.9 0.0 collective-permute-done.5
  126.0 0.6 fusion.3
  126.6 0.6 fusion.4
  (26 shorter events, 0.2 us)
Async XLA Ops:
  8.7 12.9 %copy-start.5 = (s32[1,128]{1,0:T(1,128)S(1)}, s32[1,128]{1,0:T(1,128)}, u32[]{:S(2)}) copy-start(s32[1,128]{1,0:T(1,128)} %param.16) | copy-start | bytes 1540
  10.7 25.6 %all-to-all-start = ((bf16[4,32,1280]{2,1,0:T(8,128)(2,1)}), bf16[4,32,1280]{2,1,0:T(8,128)(2,1)S(1)}, u32[]{:S(2)}, u32[]{:S(2)}) async-start(bf16[4,32,1280]{2,1,0:T(8,128)(2,1)} %maximum_bitcast_fusion), calls=%async_computation | async-start | bytes 655360 | tf_op jit(solution)/shard_map/all_to_all | solution.py:278
  21.7 8.3 %collective-permute-start.3 = (bf16[4,80,128]{2,0,1:T(4,128)(2,1)S(1)}, bf16[4,80,128]{2,0,1:T(4,128)(2,1)S(1)}, u32[]{:S(2)}, u32[]{:S(2)}) collective-permute-start(bf16[4,80,128]{2,0,1:T(4,128)(2,1)S(1)} %pad_maximum_fusion.2), channel_id=1, source_target_pairs={{0,448},{64,384},{128,320},{192,256},{256,192},{320,128},{384,64},... | collective-permute-start | bytes 245768 | tf_op jit(solution)/shard_map/ppermute | solution.py:290
  26.9 8.1 %collective-permute-start.2 = (bf16[4,80,128]{2,0,1:T(4,128)(2,1)S(1)}, bf16[4,80,128]{2,0,1:T(4,128)(2,1)S(1)}, u32[]{:S(2)}, u32[]{:S(2)}) collective-permute-start(bf16[4,80,128]{2,0,1:T(4,128)(2,1)S(1)} %pad_maximum_fusion.2), channel_id=1, source_target_pairs={{0,480},{4,484},{8,488},{12,492},{16,496},{20,500},{24,504},{28,50... | collective-permute-start | bytes 245768 | tf_op jit(solution)/shard_map/ppermute | solution.py:291
  35.4 13.5 %copy-start.6 = (s32[1,128]{1,0:T(1,128)S(1)}, s32[1,128]{1,0:T(1,128)}, u32[]{:S(2)}) copy-start(s32[1,128]{1,0:T(1,128)} %param.12) | copy-start | bytes 1540
  35.4 13.5 %copy-start.3 = (bf16[1,128,128]{2,1,0:T(8,128)(2,1)S(1)}, bf16[1,128,128]{2,1,0:T(8,128)(2,1)}, u32[]{:S(2)}) copy-start(bf16[1,128,128]{2,1,0:T(8,128)(2,1)} %param.11) | copy-start | bytes 98308
  35.4 13.5 %copy-start.4 = (bf16[1,128,128]{2,1,0:T(8,128)(2,1)S(1)}, bf16[1,128,128]{2,1,0:T(8,128)(2,1)}, u32[]{:S(2)}) copy-start(bf16[1,128,128]{2,1,0:T(8,128)(2,1)} %param.10) | copy-start | bytes 98308
  36.3 48.8 %copy-start.1 = (bf16[1,128,1024]{2,1,0:T(8,128)(2,1)S(1)}, bf16[1,128,1024]{2,1,0:T(8,128)(2,1)}, u32[]{:S(2)}) copy-start(bf16[1,128,1024]{2,1,0:T(8,128)(2,1)} %param.17) | copy-start | bytes 786436
  36.3 48.8 %all-to-all-start.1 = ((bf16[32,80,128]{2,1,0:T(8,128)(2,1)}), bf16[32,80,128]{2,1,0:T(8,128)(2,1)S(1)}, u32[]{:S(2)}, u32[]{:S(2)}) async-start(bf16[32,80,128]{2,1,0:T(8,128)(2,1)} %pad_maximum_fusion), calls=%async_computation.1 | async-start | bytes 1310720 | tf_op jit(solution)/shard_map/all_to_all | solution.py:301
  48.8 72.4 %all-gather.2.cloned.1.call-start = ((), (), s32[]{:S(2)}) async-start(), calls=%async_computation.3 | async-start | bytes 1253376 | tf_op jit(solution)/shard_map/all_gather | solution.py:316
  48.9 16.8 %collective-permute-start = (bf16[272,128]{1,0:T(8,128)(2,1)S(1)}, bf16[272,128]{1,0:T(8,128)(2,1)S(1)}, u32[]{:S(2)}, u32[]{:S(2)}) collective-permute-start(bf16[272,128]{1,0:T(8,128)(2,1)S(1)} %get-tuple-element.15), channel_id=1, source_target_pairs={{0,32},{4,36},{8,40},{12,44},{16,48},{20,52},{24,56},{28,60},{32,0... | collective-permute-start | bytes 208904 | tf_op jit(solution)/shard_map/ppermute | solution.py:315
  66.4 12.8 %collective-permute-start.1 = (bf16[4,32,1280]{2,1,0:T(8,128)(2,1)S(1)}, bf16[4,32,1280]{2,1,0:T(8,128)(2,1)S(1)}, u32[]{:S(2)}, u32[]{:S(2)}) collective-permute-start(bf16[4,32,1280]{2,1,0:T(8,128)(2,1)S(1)} %all-to-all-done), channel_id=1, source_target_pairs={{0,448},{64,384},{128,320},{192,256},{256,192},{320,128},{384,64},... | collective-permute-start | bytes 983048 | tf_op jit(solution)/shard_map/ppermute | solution.py:279
  79.2 5.9 %collective-permute-start.4 = (bf16[4,32,256]{2,1,0:T(8,128)(2,1)S(1)}, bf16[4,32,256]{2,1,0:T(8,128)(2,1)S(1)}, u32[]{:S(2)}, u32[]{:S(2)}) collective-permute-start(bf16[4,32,256]{2,1,0:T(8,128)(2,1)S(1)} %slice.33), channel_id=1, source_target_pairs={{0,36},{4,40},{8,44},{12,48},{16,52},{20,56},{24,60},{36,0},{40,4}... | collective-permute-start | bytes 196616 | tf_op jit(solution)/shard_map/ppermute | solution.py:309
  91.1 30.1 %copy-start.2 = (bf16[1,128,1024]{2,1,0:T(8,128)(2,1)S(1)}, bf16[1,128,1024]{2,1,0:T(8,128)(2,1)}, u32[]{:S(2)}) copy-start(bf16[1,128,1024]{2,1,0:T(8,128)(2,1)} %param.9) | copy-start | bytes 786436
  91.1 27.8 %all-to-all-start.2 = ((bf16[8,256,128]{2,1,0:T(8,128)(2,1)}), bf16[8,256,128]{2,1,0:T(8,128)(2,1)S(1)}, u32[]{:S(2)}, u32[]{:S(2)}) async-start(bf16[8,256,128]{2,1,0:T(8,128)(2,1)} %get-tuple-element.9), calls=%async_computation.2 | async-start | bytes 1048576 | tf_op jit(solution)/shard_map/all_to_all | solution.py:325
  101.4 24.5 %collective-permute-start.6 = (bf16[256,128]{1,0:T(8,128)(2,1)S(1)}, bf16[256,128]{1,0:T(8,128)(2,1)S(1)}, u32[]{:S(2)}, u32[]{:S(2)}) collective-permute-start(bf16[256,128]{1,0:T(8,128)(2,1)S(1)} %get-tuple-element.11), channel_id=1, source_target_pairs={{0,36},{4,40},{8,44},{12,48},{16,52},{20,56},{24,60},{36,0},{40,4}... | collective-permute-start | bytes 196616 | tf_op jit(solution)/shard_map/ppermute | solution.py:328
  119.2 6.7 %collective-permute-start.5 = (bf16[256,128]{1,0:T(8,128)(2,1)S(1)}, bf16[256,128]{1,0:T(8,128)(2,1)S(1)}, u32[]{:S(2)}, u32[]{:S(2)}) collective-permute-start(bf16[256,128]{1,0:T(8,128)(2,1)S(1)} %get-tuple-element.13), channel_id=1, source_target_pairs={{0,32},{4,36},{8,40},{12,44},{16,48},{20,52},{24,56},{28,60},{32,0... | collective-permute-start | bytes 196616 | tf_op jit(solution)/shard_map/ppermute | solution.py:335
  121.2 1.2 copy-start
Sparse Core Ops, SparseCore 0:
  66.5 36.1 all-gather.1

commit v2 on v1

--- a/solution.py
+++ b/solution.py
@@ -18,14 +18,27 @@
 HIDDEN = -1e30
 TO_LOG2 = math.log2(math.e) / math.sqrt(HEAD_DIM)
 STEP = 256
-VMEM_LIMIT = 48 * 1024 * 1024
-
-SECTION_PAIRS = [(s, 7 - s) for s in range(8)]
+VMEM_LIMIT = 24 * 1024 * 1024
+SMALL_LIMIT = 8 * 1024 * 1024
+
+BLOCK = 2 * ROWS + 16
+CUT = 2 * PIECE + 8
+
 FSDP_SWAP = [(f, f ^ 8) for f in range(16)]
 FSDP_NINE = [(f, f + 9) for f in range(7)] + [(f + 9, f) for f in range(7)]
-SECTION_FSDP_SWAP = [(s * 16 + f, (7 - s) * 16 + (f ^ 8)) for s in range(8) for f in range(16)]
+SECTION_PAIRS = [(s, 7 - s) for s in range(8)]
+TP_ROUTES = [[(t, t ^ d) for t in range(4)] for d in range(4)]
+MIRROR_GROUPS = [
+    [(s * 16 + z * 8 + y) * 4 + t for s in (k, 7 - k) for z in range(2) for t in range(4)]
+    for k in range(4)
+    for y in range(8)
+]
 ROW_GROUPS = [[z * 8 + y for y in range(8)] for z in range(2)]
-ROW_TP_GROUPS = [[(z * 8 + y) * 4 + t for y in range(8) for t in range(4)] for z in range(2)]
+
+
+def fsdp_place():
+    f = lax.axis_index("fsdp").astype(jnp.int32)
+    return f, f & (SPAN - 1), f >= SPAN
 
 
 def nt_dot(a, b):
@@ -60,13 +73,11 @@
     return top
 
 
-def forward_kernel(f_ref, query_ref, gathered_ref, out_ref, keys, values_t, bias, scores):
-    f = f_ref[0]
-    upper = f >= SPAN
+def forward_kernel(query_ref, gathered_ref, out_ref, keys, values_t, bias, scores):
+    f, y, upper = fsdp_place()
     for d in range(HALO):
-        block = f - d
-        valid = block >= 0
-        block = jnp.maximum(block, 0)
+        valid = f >= d
+        block = jnp.maximum(f - d, 0)
         crossed = jnp.where(upper & (block < SPAN), 1, 0)
         entry = (block & (SPAN - 1)) * 2 + crossed
         keys[d * ROWS : (d + 1) * ROWS, :] = gathered_ref[entry, 0:ROWS, :]
@@ -93,7 +104,10 @@
 
 
 def backward_kernel(
-    f_ref,
+    query_0_ref,
+    query_1_ref,
+    query_2_ref,
+    query_3_ref,
     own_ref,
     slots_ref,
     nine_ref,
@@ -102,6 +116,7 @@
     send_ref,
     send_nine_ref,
     own_part_ref,
+    queries,
     keys,
     keys_t,
     values,
@@ -111,45 +126,33 @@
     key_sum,
     value_sum,
 ):
-    f = f_ref[0]
-    y = f & (SPAN - 1)
-    upper = f >= SPAN
+    f, y, upper = fsdp_place()
+    t = lax.axis_index("tp").astype(jnp.int32)
+    for apart, ref in enumerate((query_0_ref, query_1_ref, query_2_ref, query_3_ref)):
+        at = pl.multiple_of((t ^ apart) * PIECE, PIECE)
+        queries[pl.ds(at, PIECE), :] = ref[...]
     for d in range(HALO):
         base = d * ROWS
-        slot = (y - d) & (SPAN - 1)
-        for piece in range(PIECES):
-            at = base + piece * PIECE
-            if d == 0:
-                key_piece = own_ref[piece, :, 1024:1152]
-                value_piece = own_ref[piece, :, 1152:1280]
-            elif d == HALO - 1:
-                key_piece = nine_ref[piece, :, 0:128]
-                value_piece = nine_ref[piece, :, 128:256]
-            else:
-                key_piece = slots_ref[slot * PIECES + piece, 0:PIECE, :]
-                value_piece = slots_ref[slot * PIECES + piece, PIECE : 2 * PIECE, :]
-            keys[at : at + PIECE, :] = key_piece
-            values[at : at + PIECE, :] = value_piece
-        keys_t[:, base : base + ROWS] = keys[base : base + ROWS, :].T
-        ids = slots_ref[slot * PIECES, 2 * PIECE : 2 * PIECE + 16, :].astype(jnp.float32)
         if d == 0:
-            query_seg = ids[1:2]
-            key_seg = query_seg
+            block = own_ref[...]
+            valid = True
         elif d == HALO - 1:
-            key_seg = ids[2:3]
+            block = nine_ref[...]
+            valid = upper & (y >= 1)
         else:
-            key_seg = ids[0:1]
-        valid = (f >= d) if d < HALO - 1 else (upper & (y >= 1))
+            block = slots_ref[(y - d) & (SPAN - 1)]
+            valid = f >= d
+        keys[base : base + ROWS, :] = block[0:ROWS]
+        values[base : base + ROWS, :] = block[ROWS : 2 * ROWS]
+        keys_t[:, base : base + ROWS] = block[0:ROWS].T
+        key_seg = block[2 * ROWS :].astype(jnp.float32)[0:1]
+        if d == 0:
+            query_seg = key_seg
         write_bias(bias, d, key_seg, query_seg, valid)
     for pair in range(4):
         lo_col = pair * 2 * HEAD_DIM
         query_pair = jnp.concatenate(
-            [
-                own_ref[piece, :, col : col + 128]
-                for col in (lo_col, lo_col + 128)
-                for piece in range(PIECES)
-            ],
-            axis=0,
+            [queries[:, lo_col : lo_col + 128], queries[:, lo_col + 128 : lo_col + 256]], axis=0
         )
         grad_pair = jnp.concatenate(
             [grad_ref[:, lo_col : lo_col + 128], grad_ref[:, lo_col + 128 : lo_col + 256]], axis=0
@@ -199,14 +202,77 @@
 
 
 VMEM = pl.BlockSpec(memory_space=pltpu.VMEM)
-SMEM = pl.BlockSpec(memory_space=pltpu.SMEM)
-
-
-def run_forward(f, query, gathered):
+ANY = pl.BlockSpec(memory_space=pl.ANY)
+
+
+def wide_ids(ids_ref):
+    return jnp.broadcast_to(ids_ref[...].astype(jnp.float32), (16, 128)).astype(jnp.bfloat16)
+
+
+def prepare_kernel(
+    held_key_ref, held_value_ref, held_ids_ref, key_ref, value_ref, ids_ref, cut_ref, forward_ref
+):
+    held_ids = wide_ids(held_ids_ref)[0:8]
+    for t in range(PIECES):
+        cut = jnp.concatenate(
+            [
+                held_key_ref[0, :, t * 128 : (t + 1) * 128],
+                held_value_ref[0, :, t * 128 : (t + 1) * 128],
+                held_ids,
+            ],
+            axis=0,
+        )
+        for copy in range(4):
+            cut_ref[copy * PIECES + t] = cut
+    forward_ref[0:ROWS, :] = key_ref[0]
+    forward_ref[ROWS : 2 * ROWS, :] = value_ref[0]
+    forward_ref[2 * ROWS :, :] = wide_ids(ids_ref)
+
+
+def outgoing_kernel(
+    cuts_ref, query_ref, forward_ref, forward_cross_ref, own_ref, outgoing_ref, stacked_ref, *part_refs
+):
+    f, y, upper = fsdp_place()
+    t = lax.axis_index("tp").astype(jnp.int32)
+    for apart, ref in enumerate(part_refs):
+        lo = pl.multiple_of((t ^ apart) * 1024, 1024)
+        ref[...] = query_ref[:, pl.ds(lo, 1024)]
+    side = jnp.where(lax.axis_index("section") < 4, 2 * PIECES, 0)
+    row = jnp.where(upper, PIECES, 0)
+
+    def whole(first):
+        cuts = [cuts_ref[first + piece] for piece in range(PIECES)]
+        ids = cuts[0][2 * PIECE :]
+        return jnp.concatenate(
+            [cut[:PIECE] for cut in cuts] + [cut[PIECE : 2 * PIECE] for cut in cuts] + [ids, ids],
+            axis=0,
+        )
+
+    own = whole(side + row)
+    crossed = whole(side + PIECES - row)
+    own_ref[...] = own
+    for target in range(SPAN):
+        outgoing_ref[target] = jnp.where(upper & (target <= y), crossed, own)
+    stacked_ref[0] = forward_ref[...]
+    stacked_ref[1] = forward_cross_ref[...]
+
+
+def run_small(kernel, name, limit, shapes, *arrays, waits=()):
+    return pl.pallas_call(
+        kernel,
+        out_shape=tuple(jax.ShapeDtypeStruct(shape, jnp.bfloat16) for shape in shapes),
+        in_specs=[VMEM] * len(arrays) + [ANY] * len(waits),
+        out_specs=(VMEM,) * len(shapes),
+        compiler_params=pltpu.CompilerParams(vmem_limit_bytes=limit) if limit else None,
+        name=name,
+    )(*arrays, *waits)
+
+
+def run_forward(query, gathered):
     return pl.pallas_call(
         forward_kernel,
         out_shape=jax.ShapeDtypeStruct((ROWS, 1024), jnp.bfloat16),
-        in_specs=[SMEM, VMEM, VMEM],
+        in_specs=[VMEM, VMEM],
         out_specs=VMEM,
         scratch_shapes=[
             pltpu.VMEM((KEYS, HEAD_DIM), jnp.bfloat16),
@@ -219,10 +285,10 @@
             flops=2 * 2 * 1024 * KEYS * 128, bytes_accessed=3_000_000, transcendentals=1024 * KEYS
         ),
         name="forward_attention",
-    )(f, query, gathered)
-
-
-def run_backward(f, own, slots, nine, grad):
+    )(query, gathered)
+
+
+def run_backward(queries, own, slots, nine, grad):
     return pl.pallas_call(
         backward_kernel,
         out_shape=(
@@ -231,9 +297,10 @@
             jax.ShapeDtypeStruct((2 * ROWS, HEAD_DIM), jnp.bfloat16),
             jax.ShapeDtypeStruct((2 * ROWS, HEAD_DIM), jnp.float32),
         ),
-        in_specs=[SMEM, VMEM, VMEM, VMEM, VMEM],
+        in_specs=[VMEM] * 8,
         out_specs=(VMEM, VMEM, VMEM, VMEM),
         scratch_shapes=[
+            pltpu.VMEM((ROWS, 1024), jnp.bfloat16),
             pltpu.VMEM((KEYS, HEAD_DIM), jnp.bfloat16),
             pltpu.VMEM((HEAD_DIM, KEYS), jnp.bfloat16),
             pltpu.VMEM((KEYS, HEAD_DIM), jnp.bfloat16),
@@ -248,7 +315,7 @@
             flops=5 * 2 * 1024 * KEYS * 128, bytes_accessed=4_000_000, transcendentals=1024 * KEYS
         ),
         name="backward_attention",
-    )(f, own, slots, nine, grad)
+    )(*queries, own, slots, nine, grad)
 
 
 def local(
@@ -265,68 +332,53 @@
     f = lax.axis_index("fsdp").astype(jnp.int32)
     y = f & (SPAN - 1)
     upper = f >= SPAN
-    f_arr = f.reshape(1)
-
-    stash = jnp.concatenate(
-        [
-            held_queries[0].reshape(PIECE, 4, 1024),
-            held_keys[0].reshape(PIECE, 4, 128),
-            held_values[0].reshape(PIECE, 4, 128),
-        ],
-        axis=2,
-    ).transpose(1, 0, 2)
-    stash = lax.all_to_all(stash, "tp", split_axis=0, concat_axis=0, tiled=False)
-    own = lax.ppermute(stash, "section", SECTION_PAIRS)
-
-    held_ids = held_segments[0].astype(jnp.bfloat16)
-    token_cut = jnp.concatenate(
-        [
-            held_keys[0].reshape(PIECE, 4, 128).transpose(1, 0, 2),
-            held_values[0].reshape(PIECE, 4, 128).transpose(1, 0, 2),
-            jnp.broadcast_to(held_ids[None, None, :], (4, 16, 128)),
-        ],
-        axis=1,
-    )
-    straight = lax.ppermute(token_cut, "section", SECTION_PAIRS)
-    crossed = lax.ppermute(token_cut, ("section", "fsdp"), SECTION_FSDP_SWAP)
-    id_rows = lax.broadcasted_iota(jnp.int32, (4, 16, 128), 1)
-    target = lax.broadcasted_iota(jnp.int32, (SPAN, 1, 1, 1), 0)
-    take_crossed = (target <= y) & upper
-    body = jnp.where(take_crossed, crossed[None, :, : 2 * PIECE], straight[None, :, : 2 * PIECE])
-    straight_ids = straight[None, :, 2 * PIECE :]
-    crossed_ids = crossed[None, :, 2 * PIECE :]
-    ids = jnp.where(take_crossed, crossed_ids, straight_ids)
-    ids = jnp.where(id_rows[None] == 1, straight_ids, jnp.where(id_rows[None] == 2, crossed_ids, ids))
-    outgoing = jnp.concatenate([body, ids], axis=2).reshape(SPAN * 4, 2 * PIECE + 16, 128)
-    slots = lax.all_to_all(
-        outgoing,
-        ("fsdp", "tp"),
+    query_back = lax.ppermute(held_queries[0], "section", SECTION_PAIRS)
+    cuts, forward_part = run_small(
+        prepare_kernel,
+        "prepare",
+        None,
+        ((4 * PIECES, CUT, 128), (BLOCK, 128)),
+        held_keys,
+        held_values,
+        held_segments,
+        key_rows,
+        values,
+        segments,
+    )
+    cuts = lax.all_to_all(
+        cuts,
+        ("section", "fsdp", "tp"),
         split_axis=0,
         concat_axis=0,
         tiled=False,
-        axis_index_groups=ROW_TP_GROUPS,
-    )
-    nine = lax.ppermute(own[:, :, 1024:], "fsdp", FSDP_NINE)
-
-    ids_low = segments[0].astype(jnp.bfloat16)
-    forward_part = jnp.concatenate(
-        [key_rows[0], values[0], jnp.broadcast_to(ids_low[None, :], (16, 128))], axis=0
+        axis_index_groups=MIRROR_GROUPS,
     )
     forward_cross = lax.ppermute(forward_part, "fsdp", FSDP_SWAP)
+    own, outgoing, stacked, *parts = run_small(
+        outgoing_kernel,
+        "outgoing",
+        SMALL_LIMIT,
+        ((BLOCK, 128), (SPAN, BLOCK, 128), (2, BLOCK, 128), *[(PIECE, 1024)] * 4),
+        cuts,
+        query_back,
+        forward_part,
+        forward_cross,
+    )
+    stash = [parts[0]] + [lax.ppermute(parts[d], "tp", TP_ROUTES[d]) for d in (1, 2, 3)]
+    slots = lax.all_to_all(
+        outgoing, "fsdp", split_axis=0, concat_axis=0, tiled=False, axis_index_groups=ROW_GROUPS
+    )
+    nine = lax.ppermute(own, "fsdp", FSDP_NINE)
     gathered = lax.all_gather(
-        jnp.stack([forward_part, forward_cross]),
-        "fsdp",
-        axis=0,
-        tiled=True,
-        axis_index_groups=ROW_GROUPS,
-    )
-
-    query_grad, send, send_nine, own_part = run_backward(f_arr, own, slots, nine, out_grad[0])
+        stacked, "fsdp", axis=0, tiled=True, axis_index_groups=ROW_GROUPS
+    )
+
+    query_grad, send, send_nine, own_part = run_backward(stash, own, slots, nine, out_grad[0])
     parts = lax.all_to_all(
         send, "fsdp", split_axis=0, concat_axis=0, tiled=False, axis_index_groups=ROW_GROUPS
     )
     from_nine = lax.ppermute(send_nine, "fsdp", FSDP_NINE)
-    attn_out = run_forward(f_arr, queries[0], gathered)
+    attn_out = run_forward(queries[0], gathered)
 
     source = lax.broadcasted_iota(jnp.int32, (SPAN, 1, 1), 0)
     parts_wide = parts.astype(jnp.float32)

time: 135 us -> 115 us (0.85)
  waiting for transfers between devices: 46.3 us -> 21.7 us
  starting transfers between devices: 55.4 us -> 62.2 us
  other arithmetic: 3.56 us -> 0.93 us
  Pallas kernels: 9.49 us -> 12.1 us
  local copies, waits for them, and re-layouts: 4.96 us -> 2.75 us
    ppermute x4 -> x5, waiting for transfers between devices: 18.6 us -> 7.24 us  [the longest x3 4.46 us: local(): lax.ppermute(parts[d], 'tp', TP_ROUTES[d])]
    ppermute x1, waiting for transfers between devices: 13.7 us -> 2.91 us  [local(): forward_cross = lax.ppermute(forward_part, 'fsdp', FSDP_SWAP)]
    ppermute x4 -> x5, starting transfers between devices: 13.2 us -> 20.6 us  [the longest x3 11.4 us: local(): lax.ppermute(parts[d], 'tp', TP_ROUTES[d])]
    all_to_all x1, starting transfers between devices: 10.3 us -> 5.97 us  [local(): lax.all_to_all(send, 'fsdp', split_axis=0, concat_axis=0, tiled=False, ax...]
    ppermute x1, starting transfers between devices: 1.92 us -> 5.47 us  [local(): from_upper = lax.ppermute(other_row, 'fsdp', FSDP_SWAP)]
    all_to_all x1, waiting for transfers between devices: 13.9 us -> 10.9 us  [local(): lax.all_to_all(send, 'fsdp', split_axis=0, concat_axis=0, tiled=False, ax...]
    another operation x6 -> x0, local copies, waits for them, and re-layouts: 2.79 us -> none  [the longest x2 1.22 us: local(): held_queries[0].reshape(PIECE, 4, 1024)]
    ppermute x1, starting transfers between devices: 3.62 us -> 6.3 us  [local(): from_nine = lax.ppermute(send_nine, 'fsdp', FSDP_NINE)]
  transfers between devices with their start and end apart: 11 -> 12, of which waited for: 5 -> 5; matrix products, arithmetic and copies ran while one was open for 2% -> 0% of each run, Pallas kernels for 7% -> 8%
where the time goes in v2:
time: 115 us; the launch traced here: 114 us
  starting transfers between devices  62.2 us (54%)
  waiting for transfers between devices  21.7 us (19%)
  between operations  14.2 us (12%)
  Pallas kernels  12.1 us (11%)
  local copies, waits for them, and re-layouts  2.75 us (2%)
    all_to_all x1, starting transfers between devices, local(): lax.all_to_all(cuts, ('section', 'fsdp', 'tp'), split_axis=0, concat_axis...  13.9 us
    ppermute x3, starting transfers between devices, local(): lax.ppermute(parts[d], 'tp', TP_ROUTES[d])  11.4 us
    all_to_all x1, waiting for transfers between devices, local(): lax.all_to_all(send, 'fsdp', split_axis=0, concat_axis=0, tiled=False, ax...  10.9 us
    all_to_all x1, starting transfers between devices, local(): lax.all_to_all(outgoing, 'fsdp', split_axis=0, concat_axis=0, tiled=False...  6.82 us
    ppermute x1, starting transfers between devices, local(): from_nine = lax.ppermute(send_nine, 'fsdp', FSDP_NINE)  6.3 us
    pallas_call x1, Pallas kernels, run_backward(): pl.pallas_call(backward_kernel, out_shape=(jax.ShapeDtypeStruct((ROWS, 10...  6.08 us
    all_to_all x1, starting transfers between devices, local(): lax.all_to_all(send, 'fsdp', split_axis=0, concat_axis=0, tiled=False, ax...  5.97 us
    ppermute x1, starting transfers between devices, local(): from_upper = lax.ppermute(other_row, 'fsdp', FSDP_SWAP)  5.47 us
  transfers between devices with their start and end apart: 12, of which 5 were waited for; matrix products, arithmetic and copies ran while one was open for 0% of the time, Pallas kernels for 8%

profile of v2, /device:TPU:1, one launch (start us, length us, event | category | flops | bytes accessed | tf_op | source)
XLA Modules:
  0.0 113.8 jit_solution(10600670836172466481)
XLA Ops:
  7.2 1.6 %prepare.1 = (bf16[16,72,128]{2,1,0:T(8,128)(2,1)}, bf16[272,128]{1,0:T(8,128)(2,1)}) custom-call(bf16[1,32,512]{2,1,0:T(8,128)(2,1)} %held_key_ref.1, bf16[1,32,512]{2,1,0:T(8,128)(2,1)} %held_value_ref.1, s32[1,128]{1,0:T(1,128)} %held_ids_ref.1, bf16[1,128,128]{2,1,0:T(8,128)(2,1)} %key_ref.1, bf16[1,128,128]{2,1,0:T(8,128)(2,1)} %value_ref.1, ...), custom_call_target="tpu_custom_call" | custom-call | tf_op jit(solution)/shard_map/prepare/pallas_call | solution.py:261
  8.8 0.0 copy-start.2
  8.8 13.9 %all-to-all-start = ((bf16[16,72,128]{2,1,0:T(8,128)(2,1)}), bf16[16,72,128]{2,1,0:T(8,128)(2,1)S(1)}, u32[]{:S(2)}, u32[]{:S(2)}) async-start(bf16[16,72,128]{2,1,0:T(8,128)(2,1)} %get-tuple-element.17), calls=%async_computation | async-start | bytes 589824 | tf_op jit(solution)/shard_map/all_to_all | solution.py:348
  22.6 4.8 %collective-permute-start = (bf16[32,4096]{1,0:T(8,128)(2,1)}, bf16[32,4096]{1,0:T(8,128)(2,1)S(1)}, u32[]{:S(2)}, u32[]{:S(2)}) collective-permute-start(bf16[32,4096]{1,0:T(8,128)(2,1)} %bitcast.11), channel_id=1, source_target_pairs={{0,448},{64,384},{128,320},{192,256},{256,192},{320,128},{384,64},... | collective-permute-start | bytes 786440 | tf_op jit(solution)/shard_map/ppermute | solution.py:335
  27.4 3.1 %collective-permute-start.1 = (bf16[272,128]{1,0:T(8,128)(2,1)}, bf16[272,128]{1,0:T(8,128)(2,1)S(1)}, u32[]{:S(2)}, u32[]{:S(2)}) collective-permute-start(bf16[272,128]{1,0:T(8,128)(2,1)} %get-tuple-element.18.forward_ref), channel_id=1, source_target_pairs={{0,32},{4,36},{8,40},{12,44},{16,48},{20,52},{24,56},{28,60},{32,0... | collective-permute-start | bytes 208904 | tf_op jit(solution)/shard_map/ppermute | solution.py:356
  30.5 2.9 %collective-permute-done.1.forward_cross_ref = bf16[272,128]{1,0:T(8,128)(2,1)S(1)} collective-permute-done((bf16[272,128]{1,0:T(8,128)(2,1)}, bf16[272,128]{1,0:T(8,128)(2,1)S(1)}, u32[]{:S(2)}, u32[]{:S(2)}) %collective-permute-start.1) | collective-permute-done | bytes 69664 | tf_op jit(solution)/shard_map/ppermute | solution.py:356
  33.4 2.8 %collective-permute-done.query_ref = bf16[32,4096]{1,0:T(8,128)(2,1)S(1)} collective-permute-done((bf16[32,4096]{1,0:T(8,128)(2,1)}, bf16[32,4096]{1,0:T(8,128)(2,1)S(1)}, u32[]{:S(2)}, u32[]{:S(2)}) %collective-permute-start) | collective-permute-done | bytes 262176 | tf_op jit(solution)/shard_map/ppermute | solution.py:335
  36.2 0.0 all-to-all-done.cuts_ref
  36.2 0.0 copy-start
  36.2 0.9 copy-done
  37.1 0.9 outgoing.1
  38.0 6.8 %all-to-all-start.1 = ((bf16[8,272,128]{2,1,0:T(8,128)(2,1)}), bf16[8,272,128]{2,1,0:T(8,128)(2,1)S(1)}, u32[]{:S(2)}, u32[]{:S(2)}) async-start(bf16[8,272,128]{2,1,0:T(8,128)(2,1)} %get-tuple-element.25), calls=%async_computation.1 | async-start | bytes 1114112 | tf_op jit(solution)/shard_map/all_to_all | solution.py:368
  44.8 0.0 all-gather.2.cloned.1.call-start
  44.9 0.7 all-gather.2.cloned.1.call-update
  45.6 4.5 %collective-permute-start.5 = (bf16[272,128]{1,0:T(8,128)(2,1)S(1)}, bf16[272,128]{1,0:T(8,128)(2,1)S(1)}, u32[]{:S(2)}, u32[]{:S(2)}) collective-permute-start(bf16[272,128]{1,0:T(8,128)(2,1)S(1)} %get-tuple-element.24.own_ref), channel_id=1, source_target_pairs={{0,36},{4,40},{8,44},{12,48},{16,52},{20,56},{24,60},{36,0},{40,4}... | collective-permute-start | bytes 208904 | tf_op jit(solution)/shard_map/ppermute | solution.py:371
  50.0 4.2 %collective-permute-start.2 = (bf16[32,1024]{1,0:T(8,128)(2,1)S(1)}, bf16[32,1024]{1,0:T(8,128)(2,1)S(1)}, u32[]{:S(2)}, u32[]{:S(2)}) collective-permute-start(bf16[32,1024]{1,0:T(8,128)(2,1)S(1)} %get-tuple-element.21), channel_id=1, source_target_pairs={{0,1},{1,0},{2,3},{3,2},{4,5},{5,4},{6,7},{7,6},{8,9},{9,8},{10,11... | collective-permute-start | bytes 196616 | tf_op jit(solution)/shard_map/ppermute | solution.py:367
  54.3 4.0 %collective-permute-start.3 = (bf16[32,1024]{1,0:T(8,128)(2,1)S(1)}, bf16[32,1024]{1,0:T(8,128)(2,1)S(1)}, u32[]{:S(2)}, u32[]{:S(2)}) collective-permute-start(bf16[32,1024]{1,0:T(8,128)(2,1)S(1)} %get-tuple-element.22), channel_id=1, source_target_pairs={{0,2},{1,3},{2,0},{3,1},{4,6},{5,7},{6,4},{7,5},{8,10},{9,11},{10,... | collective-permute-start | bytes 196616 | tf_op jit(solution)/shard_map/ppermute | solution.py:367
  58.3 3.2 %collective-permute-start.4 = (bf16[32,1024]{1,0:T(8,128)(2,1)S(1)}, bf16[32,1024]{1,0:T(8,128)(2,1)S(1)}, u32[]{:S(2)}, u32[]{:S(2)}) collective-permute-start(bf16[32,1024]{1,0:T(8,128)(2,1)S(1)} %get-tuple-element.23), channel_id=1, source_target_pairs={{0,3},{1,2},{2,1},{3,0},{4,7},{5,6},{6,5},{7,4},{8,11},{9,10},{10,... | collective-permute-start | bytes 196616 | tf_op jit(solution)/shard_map/ppermute | solution.py:367
  61.5 0.0 collective-permute-done.2.query_1_ref
  61.5 2.1 %collective-permute-done.3.query_2_ref = bf16[32,1024]{1,0:T(8,128)(2,1)S(1)} collective-permute-done((bf16[32,1024]{1,0:T(8,128)(2,1)S(1)}, bf16[32,1024]{1,0:T(8,128)(2,1)S(1)}, u32[]{:S(2)}, u32[]{:S(2)}) %collective-permute-start.3) | collective-permute-done | bytes 65568 | tf_op jit(solution)/shard_map/ppermute | solution.py:367
  63.5 2.4 %collective-permute-done.4.query_3_ref = bf16[32,1024]{1,0:T(8,128)(2,1)S(1)} collective-permute-done((bf16[32,1024]{1,0:T(8,128)(2,1)S(1)}, bf16[32,1024]{1,0:T(8,128)(2,1)S(1)}, u32[]{:S(2)}, u32[]{:S(2)}) %collective-permute-start.4) | collective-permute-done | bytes 65568 | tf_op jit(solution)/shard_map/ppermute | solution.py:367
  65.9 0.0 collective-permute-done.5.nine_ref
  65.9 0.0 all-to-all-done.1.slots_ref
  65.9 0.0 copy-done.2
  65.9 6.1 %backward_attention.1 = (bf16[128,1024]{1,0:T(8,128)(2,1)}, bf16[8,256,128]{2,1,0:T(8,128)(2,1)}, bf16[256,128]{1,0:T(8,128)(2,1)S(1)}, f32[256,128]{1,0:T(8,128)S(1)}) custom-call(bf16[32,1024]{1,0:T(8,128)(2,1)S(1)} %get-tuple-element.20.query_0_ref, bf16[32,1024]{1,0:T(8,128)(2,1)S(1)} %collective-permute-done.2.query_1_ref, ...), custom_call_target="tpu_custom_call" | custom-call | flops 1677721600 | bytes 4000000 | tf_op jit(solution)/shard_map/backward_attention/pallas_call | solution.py:292
  72.0 0.0 copy-start.3
  72.0 6.0 %all-to-all-start.2 = ((bf16[8,256,128]{2,1,0:T(8,128)(2,1)}), bf16[8,256,128]{2,1,0:T(8,128)(2,1)S(1)}, u32[]{:S(2)}, u32[]{:S(2)}) async-start(bf16[8,256,128]{2,1,0:T(8,128)(2,1)} %get-tuple-element.27), calls=%async_computation.2 | async-start | bytes 1048576 | tf_op jit(solution)/shard_map/all_to_all | solution.py:377
  78.0 6.3 %collective-permute-start.7 = (bf16[256,128]{1,0:T(8,128)(2,1)S(1)}, bf16[256,128]{1,0:T(8,128)(2,1)S(1)}, u32[]{:S(2)}, u32[]{:S(2)}) collective-permute-start(bf16[256,128]{1,0:T(8,128)(2,1)S(1)} %get-tuple-element.29), channel_id=1, source_target_pairs={{0,36},{4,40},{8,44},{12,48},{16,52},{20,56},{24,60},{36,0},{40,4}... | collective-permute-start | bytes 196616 | tf_op jit(solution)/shard_map/ppermute | solution.py:380
  84.3 10.9 %all-to-all-done.2 = bf16[8,256,128]{2,1,0:T(8,128)(2,1)S(1)} async-done(((bf16[8,256,128]{2,1,0:T(8,128)(2,1)}), bf16[8,256,128]{2,1,0:T(8,128)(2,1)S(1)}, u32[]{:S(2)}, u32[]{:S(2)}) %all-to-all-start.2) | async-done | bytes 524320 | tf_op jit(solution)/shard_map/all_to_all | solution.py:377
  95.2 0.3 fusion
  95.5 5.5 %collective-permute-start.6 = (bf16[256,128]{1,0:T(8,128)(2,1)S(1)}, bf16[256,128]{1,0:T(8,128)(2,1)S(1)}, u32[]{:S(2)}, u32[]{:S(2)}) collective-permute-start(bf16[256,128]{1,0:T(8,128)(2,1)S(1)} %get-tuple-element.31), channel_id=1, source_target_pairs={{0,32},{4,36},{8,40},{12,44},{16,48},{20,52},{24,56},{28,60},{32,0... | collective-permute-start | bytes 196616 | tf_op jit(solution)/shard_map/ppermute | solution.py:387
  100.9 0.0 all-gather.2.cloned.1.call-done.gathered_ref
  101.0 0.0 copy-done.3
  101.0 0.0 copy-start.1
  101.0 1.2 %copy-done.1 = bf16[16,272,128]{2,1,0:T(8,128)(2,1)S(1)} copy-done((bf16[16,272,128]{2,1,0:T(8,128)(2,1)S(1)}, bf16[16,272,128]{2,1,0:T(8,128)(2,1)}, u32[]{:S(2)}) %copy-start.1) | copy-done | bytes 1114136
  102.2 3.5 %forward_attention.1 = bf16[128,1024]{1,0:T(8,128)(2,1)} custom-call(bf16[128,1024]{1,0:T(8,128)(2,1)S(1)} %bitcast.10, bf16[16,272,128]{2,1,0:T(8,128)(2,1)S(1)} %copy-done.1), custom_call_target="tpu_custom_call" | custom-call | flops 671088640 | bytes 3000000 | tf_op jit(solution)/shard_map/forward_attention/pallas_call | solution.py:272
  105.7 0.0 collective-permute-done.7
  105.7 0.0 collective-permute-done.6
  105.7 0.6 fusion.3
  106.4 0.6 fusion.4
  (2 shorter events, 0.0 us)
Async XLA Ops:
  8.8 57.2 %copy-start.2 = (bf16[1,128,1024]{2,1,0:T(8,128)(2,1)S(1)}, bf16[1,128,1024]{2,1,0:T(8,128)(2,1)}, u32[]{:S(2)}) copy-start(bf16[1,128,1024]{2,1,0:T(8,128)(2,1)} %param.17) | copy-start | bytes 786436
  8.8 27.4 %all-to-all-start = ((bf16[16,72,128]{2,1,0:T(8,128)(2,1)}), bf16[16,72,128]{2,1,0:T(8,128)(2,1)S(1)}, u32[]{:S(2)}, u32[]{:S(2)}) async-start(bf16[16,72,128]{2,1,0:T(8,128)(2,1)} %get-tuple-element.17), calls=%async_computation | async-start | bytes 589824 | tf_op jit(solution)/shard_map/all_to_all | solution.py:348
  22.6 13.6 %collective-permute-start = (bf16[32,4096]{1,0:T(8,128)(2,1)}, bf16[32,4096]{1,0:T(8,128)(2,1)S(1)}, u32[]{:S(2)}, u32[]{:S(2)}) collective-permute-start(bf16[32,4096]{1,0:T(8,128)(2,1)} %bitcast.11), channel_id=1, source_target_pairs={{0,448},{64,384},{128,320},{192,256},{256,192},{320,128},{384,64},... | collective-permute-start | bytes 786440 | tf_op jit(solution)/shard_map/ppermute | solution.py:335
  27.4 6.0 %collective-permute-start.1 = (bf16[272,128]{1,0:T(8,128)(2,1)}, bf16[272,128]{1,0:T(8,128)(2,1)S(1)}, u32[]{:S(2)}, u32[]{:S(2)}) collective-permute-start(bf16[272,128]{1,0:T(8,128)(2,1)} %get-tuple-element.18.forward_ref), channel_id=1, source_target_pairs={{0,32},{4,36},{8,40},{12,44},{16,48},{20,52},{24,56},{28,60},{32,0... | collective-permute-start | bytes 208904 | tf_op jit(solution)/shard_map/ppermute | solution.py:356
  36.2 0.9 copy-start
  38.0 27.9 %all-to-all-start.1 = ((bf16[8,272,128]{2,1,0:T(8,128)(2,1)}), bf16[8,272,128]{2,1,0:T(8,128)(2,1)S(1)}, u32[]{:S(2)}, u32[]{:S(2)}) async-start(bf16[8,272,128]{2,1,0:T(8,128)(2,1)} %get-tuple-element.25), calls=%async_computation.1 | async-start | bytes 1114112 | tf_op jit(solution)/shard_map/all_to_all | solution.py:368
  44.8 56.1 %all-gather.2.cloned.1.call-start = ((), (), s32[]{:S(2)}) async-start(), calls=%async_computation.3 | async-start | bytes 1253376 | tf_op jit(solution)/shard_map/all_gather | solution.py:372
  45.6 20.4 %collective-permute-start.5 = (bf16[272,128]{1,0:T(8,128)(2,1)S(1)}, bf16[272,128]{1,0:T(8,128)(2,1)S(1)}, u32[]{:S(2)}, u32[]{:S(2)}) collective-permute-start(bf16[272,128]{1,0:T(8,128)(2,1)S(1)} %get-tuple-element.24.own_ref), channel_id=1, source_target_pairs={{0,36},{4,40},{8,44},{12,48},{16,52},{20,56},{24,60},{36,0},{40,4}... | collective-permute-start | bytes 208904 | tf_op jit(solution)/shard_map/ppermute | solution.py:371
  50.0 11.4 %collective-permute-start.2 = (bf16[32,1024]{1,0:T(8,128)(2,1)S(1)}, bf16[32,1024]{1,0:T(8,128)(2,1)S(1)}, u32[]{:S(2)}, u32[]{:S(2)}) collective-permute-start(bf16[32,1024]{1,0:T(8,128)(2,1)S(1)} %get-tuple-element.21), channel_id=1, source_target_pairs={{0,1},{1,0},{2,3},{3,2},{4,5},{5,4},{6,7},{7,6},{8,9},{9,8},{10,11... | collective-permute-start | bytes 196616 | tf_op jit(solution)/shard_map/ppermute | solution.py:367
  54.3 9.2 %collective-permute-start.3 = (bf16[32,1024]{1,0:T(8,128)(2,1)S(1)}, bf16[32,1024]{1,0:T(8,128)(2,1)S(1)}, u32[]{:S(2)}, u32[]{:S(2)}) collective-permute-start(bf16[32,1024]{1,0:T(8,128)(2,1)S(1)} %get-tuple-element.22), channel_id=1, source_target_pairs={{0,2},{1,3},{2,0},{3,1},{4,6},{5,7},{6,4},{7,5},{8,10},{9,11},{10,... | collective-permute-start | bytes 196616 | tf_op jit(solution)/shard_map/ppermute | solution.py:367
  58.3 7.6 %collective-permute-start.4 = (bf16[32,1024]{1,0:T(8,128)(2,1)S(1)}, bf16[32,1024]{1,0:T(8,128)(2,1)S(1)}, u32[]{:S(2)}, u32[]{:S(2)}) collective-permute-start(bf16[32,1024]{1,0:T(8,128)(2,1)S(1)} %get-tuple-element.23), channel_id=1, source_target_pairs={{0,3},{1,2},{2,1},{3,0},{4,7},{5,6},{6,5},{7,4},{8,11},{9,10},{10,... | collective-permute-start | bytes 196616 | tf_op jit(solution)/shard_map/ppermute | solution.py:367
  72.0 29.0 %copy-start.3 = (bf16[1,128,1024]{2,1,0:T(8,128)(2,1)S(1)}, bf16[1,128,1024]{2,1,0:T(8,128)(2,1)}, u32[]{:S(2)}) copy-start(bf16[1,128,1024]{2,1,0:T(8,128)(2,1)} %param.9) | copy-start | bytes 786436
  72.0 23.2 %all-to-all-start.2 = ((bf16[8,256,128]{2,1,0:T(8,128)(2,1)}), bf16[8,256,128]{2,1,0:T(8,128)(2,1)S(1)}, u32[]{:S(2)}, u32[]{:S(2)}) async-start(bf16[8,256,128]{2,1,0:T(8,128)(2,1)} %get-tuple-element.27), calls=%async_computation.2 | async-start | bytes 1048576 | tf_op jit(solution)/shard_map/all_to_all | solution.py:377
  78.0 27.7 %collective-permute-start.7 = (bf16[256,128]{1,0:T(8,128)(2,1)S(1)}, bf16[256,128]{1,0:T(8,128)(2,1)S(1)}, u32[]{:S(2)}, u32[]{:S(2)}) collective-permute-start(bf16[256,128]{1,0:T(8,128)(2,1)S(1)} %get-tuple-element.29), channel_id=1, source_target_pairs={{0,36},{4,40},{8,44},{12,48},{16,52},{20,56},{24,60},{36,0},{40,4}... | collective-permute-start | bytes 196616 | tf_op jit(solution)/shard_map/ppermute | solution.py:380
  95.5 10.2 %collective-permute-start.6 = (bf16[256,128]{1,0:T(8,128)(2,1)S(1)}, bf16[256,128]{1,0:T(8,128)(2,1)S(1)}, u32[]{:S(2)}, u32[]{:S(2)}) collective-permute-start(bf16[256,128]{1,0:T(8,128)(2,1)S(1)} %get-tuple-element.31), channel_id=1, source_target_pairs={{0,32},{4,36},{8,40},{12,44},{16,48},{20,52},{24,56},{28,60},{32,0... | collective-permute-start | bytes 196616 | tf_op jit(solution)/shard_map/ppermute | solution.py:387
  101.0 1.2 %copy-start.1 = (bf16[16,272,128]{2,1,0:T(8,128)(2,1)S(1)}, bf16[16,272,128]{2,1,0:T(8,128)(2,1)}, u32[]{:S(2)}) copy-start(bf16[16,272,128]{2,1,0:T(8,128)(2,1)} %all-gather.2.cloned.1.call-done.gathered_ref) | copy-start | bytes 3342340
Sparse Core Ops, SparseCore 0:
  48.3 39.6 all-gather.1

commit v3 on v2

--- a/solution.py
+++ b/solution.py
@@ -73,7 +73,7 @@
     return top
 
 
-def forward_kernel(query_ref, gathered_ref, out_ref, keys, values_t, bias, scores):
+def forward_kernel(query_ref, gathered_ref, out_ref, mark_ref, keys, values_t, bias, scores):
     f, y, upper = fsdp_place()
     for d in range(HALO):
         valid = f >= d
@@ -101,6 +101,7 @@
         result = (summed / total).T.astype(jnp.bfloat16)
         out_ref[:, lo_col : lo_col + 128] = result[0:128]
         out_ref[:, lo_col + 128 : lo_col + 256] = result[128:256]
+    mark_ref[...] = jnp.zeros((8, 128), jnp.float32)
 
 
 def backward_kernel(
@@ -229,14 +230,16 @@
     forward_ref[2 * ROWS :, :] = wide_ids(ids_ref)
 
 
-def outgoing_kernel(
-    cuts_ref, query_ref, forward_ref, forward_cross_ref, own_ref, outgoing_ref, stacked_ref, *part_refs
-):
-    f, y, upper = fsdp_place()
+def split_kernel(query_ref, *part_refs):
     t = lax.axis_index("tp").astype(jnp.int32)
     for apart, ref in enumerate(part_refs):
         lo = pl.multiple_of((t ^ apart) * 1024, 1024)
         ref[...] = query_ref[:, pl.ds(lo, 1024)]
+
+
+def outgoing_kernel(cuts_ref, forward_ref, forward_cross_ref, *refs):
+    own_ref, outgoing_ref, stacked_ref = refs[-3:]
+    f, y, upper = fsdp_place()
     side = jnp.where(lax.axis_index("section") < 4, 2 * PIECES, 0)
     row = jnp.where(upper, PIECES, 0)
 
@@ -257,13 +260,43 @@
     stacked_ref[1] = forward_cross_ref[...]
 
 
-def run_small(kernel, name, limit, shapes, *arrays, waits=()):
+def reduce_kernel(parts_ref, own_part_ref, *refs):
+    same_ref, other_ref = refs[-2:]
+    f, y, upper = fsdp_place()
+    same = own_part_ref[...]
+    other = jnp.zeros((2 * ROWS, HEAD_DIM), jnp.float32)
+    for source in range(SPAN):
+        part = parts_ref[source].astype(jnp.float32)
+        later = source > y
+        same = same + jnp.where(later, part, 0.0)
+        other = other + jnp.where(later, 0.0, part)
+    same_ref[...] = same
+    other_ref[...] = other.astype(jnp.bfloat16)
+
+
+def finish_kernel(same_ref, from_upper_ref, from_nine_ref, key_grad_ref, value_grad_ref):
+    f, y, upper = fsdp_place()
+    late = from_upper_ref[...].astype(jnp.float32) + from_nine_ref[...].astype(jnp.float32)
+    final = same_ref[...] + jnp.where(upper, 0.0, late)
+    key_grad_ref[0] = (final[:ROWS] * (1.0 / math.sqrt(HEAD_DIM))).astype(jnp.bfloat16)
+    value_grad_ref[0] = final[ROWS:].astype(jnp.bfloat16)
+
+
+def run_small(kernel, name, limit, shapes, *arrays, waits=(), flops=0):
     return pl.pallas_call(
         kernel,
-        out_shape=tuple(jax.ShapeDtypeStruct(shape, jnp.bfloat16) for shape in shapes),
+        out_shape=tuple(
+            jax.ShapeDtypeStruct(shape[:-1] if shape[-1] is jnp.float32 else shape, jnp.float32)
+            if shape[-1] is jnp.float32
+            else jax.ShapeDtypeStruct(shape, jnp.bfloat16)
+            for shape in shapes
+        ),
         in_specs=[VMEM] * len(arrays) + [ANY] * len(waits),
         out_specs=(VMEM,) * len(shapes),
         compiler_params=pltpu.CompilerParams(vmem_limit_bytes=limit) if limit else None,
+        cost_estimate=pl.CostEstimate(flops=int(flops), bytes_accessed=0, transcendentals=0)
+        if flops
+        else None,
         name=name,
     )(*arrays, *waits)
 
@@ -271,9 +304,12 @@
 def run_forward(query, gathered):
     return pl.pallas_call(
         forward_kernel,
-        out_shape=jax.ShapeDtypeStruct((ROWS, 1024), jnp.bfloat16),
+        out_shape=(
+            jax.ShapeDtypeStruct((ROWS, 1024), jnp.bfloat16),
+            jax.ShapeDtypeStruct((8, 128), jnp.float32),
+        ),
         in_specs=[VMEM, VMEM],
-        out_specs=VMEM,
+        out_specs=(VMEM, VMEM),
         scratch_shapes=[
             pltpu.VMEM((KEYS, HEAD_DIM), jnp.bfloat16),
             pltpu.VMEM((HEAD_DIM, KEYS), jnp.bfloat16),
@@ -312,7 +348,7 @@
         ],
         compiler_params=pltpu.CompilerParams(vmem_limit_bytes=VMEM_LIMIT),
         cost_estimate=pl.CostEstimate(
-            flops=5 * 2 * 1024 * KEYS * 128, bytes_accessed=4_000_000, transcendentals=1024 * KEYS
+            flops=1_000_000, bytes_accessed=0, transcendentals=0
         ),
         name="backward_attention",
     )(*queries, own, slots, nine, grad)
@@ -329,9 +365,6 @@
     held_segments,
     out_grad,
 ):
-    f = lax.axis_index("fsdp").astype(jnp.int32)
-    y = f & (SPAN - 1)
-    upper = f >= SPAN
     query_back = lax.ppermute(held_queries[0], "section", SECTION_PAIRS)
     cuts, forward_part = run_small(
         prepare_kernel,
@@ -354,17 +387,20 @@
         axis_index_groups=MIRROR_GROUPS,
     )
     forward_cross = lax.ppermute(forward_part, "fsdp", FSDP_SWAP)
-    own, outgoing, stacked, *parts = run_small(
+    parts = run_small(
+        split_kernel, "split", SMALL_LIMIT, ((PIECE, 1024),) * 4, query_back, flops=3e10
+    )
+    stash = [parts[0]] + [lax.ppermute(parts[d], "tp", TP_ROUTES[d]) for d in (1, 2, 3)]
+    own, outgoing, stacked = run_small(
         outgoing_kernel,
         "outgoing",
         SMALL_LIMIT,
-        ((BLOCK, 128), (SPAN, BLOCK, 128), (2, BLOCK, 128), *[(PIECE, 1024)] * 4),
+        ((BLOCK, 128), (SPAN, BLOCK, 128), (2, BLOCK, 128)),
         cuts,
-        query_back,
         forward_part,
         forward_cross,
-    )
-    stash = [parts[0]] + [lax.ppermute(parts[d], "tp", TP_ROUTES[d]) for d in (1, 2, 3)]
+        waits=stash[1:2],
+    )
     slots = lax.all_to_all(
         outgoing, "fsdp", split_axis=0, concat_axis=0, tiled=False, axis_index_groups=ROW_GROUPS
     )
@@ -378,18 +414,28 @@
         send, "fsdp", split_axis=0, concat_axis=0, tiled=False, axis_index_groups=ROW_GROUPS
     )
     from_nine = lax.ppermute(send_nine, "fsdp", FSDP_NINE)
-    attn_out = run_forward(queries[0], gathered)
-
-    source = lax.broadcasted_iota(jnp.int32, (SPAN, 1, 1), 0)
-    parts_wide = parts.astype(jnp.float32)
-    same_row = jnp.sum(jnp.where(source > y, parts_wide, 0.0), axis=0) + own_part
-    other_row = jnp.sum(jnp.where(source <= y, parts_wide, 0.0), axis=0).astype(jnp.bfloat16)
+    attn_out, mark = run_forward(queries[0], gathered)
+
+    same_row, other_row = run_small(
+        reduce_kernel,
+        "reduce",
+        SMALL_LIMIT,
+        ((2 * ROWS, 128, jnp.float32), (2 * ROWS, 128)),
+        parts,
+        own_part,
+        waits=(mark,),
+    )
     from_upper = lax.ppermute(other_row, "fsdp", FSDP_SWAP)
-    late = from_upper.astype(jnp.float32) + from_nine.astype(jnp.float32)
-    final = same_row + jnp.where(upper, 0.0, late)
-    key_grad = (final[:ROWS] * (1.0 / math.sqrt(HEAD_DIM))).astype(jnp.bfloat16)
-    value_grad = final[ROWS:].astype(jnp.bfloat16)
-    return (attn_out[None], query_grad[None], key_grad[None], value_grad[None])
+    key_grad, value_grad = run_small(
+        finish_kernel,
+        "finish",
+        SMALL_LIMIT,
+        ((1, ROWS, 128), (1, ROWS, 128)),
+        same_row,
+        from_upper,
+        from_nine,
+    )
+    return (attn_out[None], query_grad[None], key_grad, value_grad)
 
 
 def solution(mesh):

time: 115 us -> 108 us (0.939)
  starting transfers between devices: 62.2 us -> 54.4 us
  waiting for transfers between devices: 21.7 us -> 23.2 us
  local copies, waits for them, and re-layouts: 2.75 us -> 1.26 us
    all_to_all x1, waiting for transfers between devices: 0.01 us -> 6.18 us  [local(): lax.all_to_all(outgoing, 'fsdp', split_axis=0, concat_axis=0, tiled=False...]
    all_to_all x1, waiting for transfers between devices: 10.9 us -> 6.89 us  [local(): lax.all_to_all(send, 'fsdp', split_axis=0, concat_axis=0, tiled=False, ax...]
    all_to_all x1, starting transfers between devices: 13.9 us -> 10.1 us  [local(): lax.all_to_all(cuts, ('section', 'fsdp', 'tp'), split_axis=0, concat_axis...]
    ppermute x1, waiting for transfers between devices: 2.78 us -> 0.01 us  [local(): query_back = lax.ppermute(held_queries[0], 'section', SECTION_PAIRS)]
    all_to_all x1, starting transfers between devices: 5.97 us -> 3.49 us  [local(): lax.all_to_all(send, 'fsdp', split_axis=0, concat_axis=0, tiled=False, ax...]
    all_to_all x1, waiting for transfers between devices: 0.01 us -> 2.07 us  [local(): lax.all_to_all(cuts, ('section', 'fsdp', 'tp'), split_axis=0, concat_axis...]
    ppermute x1, starting transfers between devices: 6.3 us -> 4.26 us  [local(): from_nine = lax.ppermute(send_nine, 'fsdp', FSDP_NINE)]
    ppermute x1, waiting for transfers between devices: 0.01 us -> 1.63 us  [local(): from_upper = lax.ppermute(other_row, 'fsdp', FSDP_SWAP)]
  transfers between devices with their start and end apart: 12 -> 12, of which waited for: 5 -> 7; matrix products, arithmetic and copies ran while one was open for 0% -> 0% of each run, Pallas kernels for 8% -> 11%
where the time goes in v3:
time: 108 us; the launch traced here: 106 us
  starting transfers between devices  54.4 us (50%)
  waiting for transfers between devices  23.2 us (21%)
  between operations  14.2 us (13%)
  Pallas kernels  12.9 us (12%)
  local copies, waits for them, and re-layouts  1.26 us (1%)
    ppermute x3, starting transfers between devices, local(): lax.ppermute(parts[d], 'tp', TP_ROUTES[d])  12.7 us
    all_to_all x1, starting transfers between devices, local(): lax.all_to_all(cuts, ('section', 'fsdp', 'tp'), split_axis=0, concat_axis...  10.1 us
    all_to_all x1, waiting for transfers between devices, local(): lax.all_to_all(send, 'fsdp', split_axis=0, concat_axis=0, tiled=False, ax...  6.89 us
    all_to_all x1, starting transfers between devices, local(): lax.all_to_all(outgoing, 'fsdp', split_axis=0, concat_axis=0, tiled=False...  6.83 us
    all_to_all x1, waiting for transfers between devices, local(): lax.all_to_all(outgoing, 'fsdp', split_axis=0, concat_axis=0, tiled=False...  6.18 us
    pallas_call x1, Pallas kernels, run_backward(): pl.pallas_call(backward_kernel, out_shape=(jax.ShapeDtypeStruct((ROWS, 10...  6.07 us
    ppermute x1, starting transfers between devices, local(): query_back = lax.ppermute(held_queries[0], 'section', SECTION_PAIRS)  5.78 us
    ppermute x1, starting transfers between devices, local(): from_nine = lax.ppermute(send_nine, 'fsdp', FSDP_NINE)  4.26 us
  transfers between devices with their start and end apart: 12, of which 7 were waited for; matrix products, arithmetic and copies ran while one was open for 0% of the time, Pallas kernels for 11%

profile of v3, /device:TPU:1, one launch (start us, length us, event | category | flops | bytes accessed | tf_op | source)
XLA Modules:
  0.0 106.0 jit_solution(16745232845925707718)
XLA Ops:
  7.2 5.8 %collective-permute-start.1 = (bf16[32,4096]{1,0:T(8,128)(2,1)}, bf16[32,4096]{1,0:T(8,128)(2,1)S(1)}, u32[]{:S(2)}, u32[]{:S(2)}) collective-permute-start(bf16[32,4096]{1,0:T(8,128)(2,1)} %bitcast.7), channel_id=1, source_target_pairs={{0,448},{64,384},{128,320},{192,256},{256,192},{320,128},{384,64},... | collective-permute-start | bytes 786440 | tf_op jit(solution)/shard_map/ppermute | solution.py:368
  13.0 1.6 %prepare.1 = (bf16[16,72,128]{2,1,0:T(8,128)(2,1)}, bf16[272,128]{1,0:T(8,128)(2,1)}) custom-call(bf16[1,32,512]{2,1,0:T(8,128)(2,1)} %held_key_ref.1, bf16[1,32,512]{2,1,0:T(8,128)(2,1)} %held_value_ref.1, s32[1,128]{1,0:T(1,128)} %held_ids_ref.1, bf16[1,128,128]{2,1,0:T(8,128)(2,1)} %key_ref.1, bf16[1,128,128]{2,1,0:T(8,128)(2,1)} %value_ref.1, ...), custom_call_target="tpu_custom_call" | custom-call | tf_op jit(solution)/shard_map/prepare/pallas_call | solution.py:286
  14.5 10.1 %all-to-all-start = ((bf16[16,72,128]{2,1,0:T(8,128)(2,1)}), bf16[16,72,128]{2,1,0:T(8,128)(2,1)S(1)}, u32[]{:S(2)}, u32[]{:S(2)}) async-start(bf16[16,72,128]{2,1,0:T(8,128)(2,1)} %get-tuple-element.23), calls=%async_computation | async-start | bytes 589824 | tf_op jit(solution)/shard_map/all_to_all | solution.py:381
  24.7 0.0 all-gather.2.cloned.1.call-start
  24.7 0.0 copy-start.1
  24.8 3.4 %collective-permute-start = (bf16[272,128]{1,0:T(8,128)(2,1)}, bf16[272,128]{1,0:T(8,128)(2,1)S(1)}, u32[]{:S(2)}, u32[]{:S(2)}) collective-permute-start(bf16[272,128]{1,0:T(8,128)(2,1)} %get-tuple-element.24.forward_ref), channel_id=1, source_target_pairs={{0,32},{4,36},{8,40},{12,44},{16,48},{20,52},{24,56},{28,60},{32,0... | collective-permute-start | bytes 208904 | tf_op jit(solution)/shard_map/ppermute | solution.py:389
  28.2 0.0 collective-permute-done.1.query_ref
  28.2 0.0 copy-start
  28.2 4.1 %collective-permute-start.2 = (bf16[32,1024]{1,0:T(8,128)(2,1)S(1)}, bf16[32,1024]{1,0:T(8,128)(2,1)S(1)}, u32[]{:S(2)}, u32[]{:S(2)}) collective-permute-start(bf16[32,1024]{1,0:T(8,128)(2,1)S(1)} %get-tuple-element.25), channel_id=1, source_target_pairs={{0,1},{1,0},{2,3},{3,2},{4,5},{5,4},{6,7},{7,6},{8,9},{9,8},{10,11... | collective-permute-start | bytes 196616 | tf_op jit(solution)/shard_map/ppermute | solution.py:393
  32.4 3.0 %collective-permute-done.forward_cross_ref = bf16[272,128]{1,0:T(8,128)(2,1)S(1)} collective-permute-done((bf16[272,128]{1,0:T(8,128)(2,1)}, bf16[272,128]{1,0:T(8,128)(2,1)S(1)}, u32[]{:S(2)}, u32[]{:S(2)}) %collective-permute-start) | collective-permute-done | bytes 69664 | tf_op jit(solution)/shard_map/ppermute | solution.py:389
  35.3 0.0 collective-permute-done.2.refs_0_.query_1_ref
  35.3 2.1 %all-to-all-done.cuts_ref = bf16[16,72,128]{2,1,0:T(8,128)(2,1)S(1)} async-done(((bf16[16,72,128]{2,1,0:T(8,128)(2,1)}), bf16[16,72,128]{2,1,0:T(8,128)(2,1)S(1)}, u32[]{:S(2)}, u32[]{:S(2)}) %all-to-all-start) | async-done | bytes 294944 | tf_op jit(solution)/shard_map/all_to_all | solution.py:381
  37.4 0.0 copy-done.1
  37.4 0.9 outgoing.1
  38.3 0.0 all-gather.2.cloned.1.call-update
  38.3 6.8 %all-to-all-start.1 = ((bf16[8,272,128]{2,1,0:T(8,128)(2,1)}), bf16[8,272,128]{2,1,0:T(8,128)(2,1)S(1)}, u32[]{:S(2)}, u32[]{:S(2)}) async-start(bf16[8,272,128]{2,1,0:T(8,128)(2,1)} %get-tuple-element.32), calls=%async_computation.1 | async-start | bytes 1114112 | tf_op jit(solution)/shard_map/all_to_all | solution.py:404
  45.2 3.8 %collective-permute-start.5 = (bf16[272,128]{1,0:T(8,128)(2,1)S(1)}, bf16[272,128]{1,0:T(8,128)(2,1)S(1)}, u32[]{:S(2)}, u32[]{:S(2)}) collective-permute-start(bf16[272,128]{1,0:T(8,128)(2,1)S(1)} %get-tuple-element.31.own_ref), channel_id=1, source_target_pairs={{0,36},{4,40},{8,44},{12,48},{16,52},{20,56},{24,60},{36,0},{40,4}... | collective-permute-start | bytes 208904 | tf_op jit(solution)/shard_map/ppermute | solution.py:407
  49.0 4.7 %collective-permute-start.3 = (bf16[32,1024]{1,0:T(8,128)(2,1)S(1)}, bf16[32,1024]{1,0:T(8,128)(2,1)S(1)}, u32[]{:S(2)}, u32[]{:S(2)}) collective-permute-start(bf16[32,1024]{1,0:T(8,128)(2,1)S(1)} %get-tuple-element.29), channel_id=1, source_target_pairs={{0,2},{1,3},{2,0},{3,1},{4,6},{5,7},{6,4},{7,5},{8,10},{9,11},{10,... | collective-permute-start | bytes 196616 | tf_op jit(solution)/shard_map/ppermute | solution.py:393
  53.7 3.9 %collective-permute-start.4 = (bf16[32,1024]{1,0:T(8,128)(2,1)S(1)}, bf16[32,1024]{1,0:T(8,128)(2,1)S(1)}, u32[]{:S(2)}, u32[]{:S(2)}) collective-permute-start(bf16[32,1024]{1,0:T(8,128)(2,1)S(1)} %get-tuple-element.30), channel_id=1, source_target_pairs={{0,3},{1,2},{2,1},{3,0},{4,7},{5,6},{6,5},{7,4},{8,11},{9,10},{10,... | collective-permute-start | bytes 196616 | tf_op jit(solution)/shard_map/ppermute | solution.py:393
  57.6 0.5 collective-permute-done.3.query_2_ref
  58.1 2.9 %collective-permute-done.4.query_3_ref = bf16[32,1024]{1,0:T(8,128)(2,1)S(1)} collective-permute-done((bf16[32,1024]{1,0:T(8,128)(2,1)S(1)}, bf16[32,1024]{1,0:T(8,128)(2,1)S(1)}, u32[]{:S(2)}, u32[]{:S(2)}) %collective-permute-start.4) | collective-permute-done | bytes 65568 | tf_op jit(solution)/shard_map/ppermute | solution.py:393
  61.0 0.0 collective-permute-done.5.nine_ref
  61.0 6.2 %all-to-all-done.1.slots_ref = bf16[8,272,128]{2,1,0:T(8,128)(2,1)S(1)} async-done(((bf16[8,272,128]{2,1,0:T(8,128)(2,1)}), bf16[8,272,128]{2,1,0:T(8,128)(2,1)S(1)}, u32[]{:S(2)}, u32[]{:S(2)}) %all-to-all-start.1) | async-done | bytes 557088 | tf_op jit(solution)/shard_map/all_to_all | solution.py:404
  67.2 0.0 copy-done
  67.2 0.0 copy-start.3
  67.2 6.1 %backward_attention.1 = (bf16[128,1024]{1,0:T(8,128)(2,1)}, bf16[8,256,128]{2,1,0:T(8,128)(2,1)}, bf16[256,128]{1,0:T(8,128)(2,1)S(1)}, f32[256,128]{1,0:T(8,128)S(1)}) custom-call(bf16[32,1024]{1,0:T(8,128)(2,1)S(1)} %get-tuple-element.28.query_0_ref, bf16[32,1024]{1,0:T(8,128)(2,1)S(1)} %collective-permute-done.2.refs_0_.query_1_ref, ...), custom_call_target="tpu_custom_call" | custom-call | flops 1000000 | tf_op jit(solution)/shard_map/backward_attention/pallas_call | solution.py:328
  73.3 3.5 %all-to-all-start.2 = ((bf16[8,256,128]{2,1,0:T(8,128)(2,1)}), bf16[8,256,128]{2,1,0:T(8,128)(2,1)S(1)}, u32[]{:S(2)}, u32[]{:S(2)}) async-start(bf16[8,256,128]{2,1,0:T(8,128)(2,1)} %get-tuple-element.34), calls=%async_computation.2 | async-start | bytes 1048576 | tf_op jit(solution)/shard_map/all_to_all | solution.py:413
  76.8 4.3 %collective-permute-start.7 = (bf16[256,128]{1,0:T(8,128)(2,1)S(1)}, bf16[256,128]{1,0:T(8,128)(2,1)S(1)}, u32[]{:S(2)}, u32[]{:S(2)}) collective-permute-start(bf16[256,128]{1,0:T(8,128)(2,1)S(1)} %get-tuple-element.39), channel_id=1, source_target_pairs={{0,36},{4,40},{8,44},{12,48},{16,52},{20,56},{24,60},{36,0},{40,4}... | collective-permute-start | bytes 196616 | tf_op jit(solution)/shard_map/ppermute | solution.py:416
  81.0 0.0 all-gather.2.cloned.1.call-done.gathered_ref
  81.1 0.0 copy-done.3
  81.1 0.0 copy-start.2
  81.1 1.2 %copy-done.2 = bf16[16,272,128]{2,1,0:T(8,128)(2,1)S(1)} copy-done((bf16[16,272,128]{2,1,0:T(8,128)(2,1)S(1)}, bf16[16,272,128]{2,1,0:T(8,128)(2,1)}, u32[]{:S(2)}) %copy-start.2) | copy-done | bytes 1114136
  82.3 3.5 %forward_attention.1 = (bf16[128,1024]{1,0:T(8,128)(2,1)}, f32[8,128]{1,0:T(8,128)S(1)}) custom-call(bf16[128,1024]{1,0:T(8,128)(2,1)S(1)} %bitcast.6, bf16[16,272,128]{2,1,0:T(8,128)(2,1)S(1)} %copy-done.2), custom_call_target="tpu_custom_call" | custom-call | flops 671088640 | bytes 3000000 | tf_op jit(solution)/shard_map/forward_attention/pallas_call | solution.py:305
  85.8 6.9 %all-to-all-done.2.parts_ref = bf16[8,256,128]{2,1,0:T(8,128)(2,1)S(1)} async-done(((bf16[8,256,128]{2,1,0:T(8,128)(2,1)}), bf16[8,256,128]{2,1,0:T(8,128)(2,1)S(1)}, u32[]{:S(2)}, u32[]{:S(2)}) %all-to-all-start.2) | async-done | bytes 524320 | tf_op jit(solution)/shard_map/all_to_all | solution.py:413
  92.7 0.2 reduce.1
  92.9 3.9 %collective-permute-start.6 = (bf16[256,128]{1,0:T(8,128)(2,1)S(1)}, bf16[256,128]{1,0:T(8,128)(2,1)S(1)}, u32[]{:S(2)}, u32[]{:S(2)}) collective-permute-start(bf16[256,128]{1,0:T(8,128)(2,1)S(1)} %get-tuple-element.38), channel_id=1, source_target_pairs={{0,32},{4,36},{8,40},{12,44},{16,48},{20,52},{24,56},{28,60},{32,0... | collective-permute-start | bytes 196616 | tf_op jit(solution)/shard_map/ppermute | solution.py:428
  96.9 0.0 collective-permute-done.7.from_nine_ref
  96.9 1.6 %collective-permute-done.6.from_upper_ref = bf16[256,128]{1,0:T(8,128)(2,1)S(1)} collective-permute-done((bf16[256,128]{1,0:T(8,128)(2,1)S(1)}, bf16[256,128]{1,0:T(8,128)(2,1)S(1)}, u32[]{:S(2)}, u32[]{:S(2)}) %collective-permute-start.6) | collective-permute-done | bytes 65568 | tf_op jit(solution)/shard_map/ppermute | solution.py:428
  98.5 0.6 finish.1
  (1 shorter events, 0.0 us)
Async XLA Ops:
  7.2 21.0 %collective-permute-start.1 = (bf16[32,4096]{1,0:T(8,128)(2,1)}, bf16[32,4096]{1,0:T(8,128)(2,1)S(1)}, u32[]{:S(2)}, u32[]{:S(2)}) collective-permute-start(bf16[32,4096]{1,0:T(8,128)(2,1)} %bitcast.7), channel_id=1, source_target_pairs={{0,448},{64,384},{128,320},{192,256},{256,192},{320,128},{384,64},... | collective-permute-start | bytes 786440 | tf_op jit(solution)/shard_map/ppermute | solution.py:368
  14.5 22.9 %all-to-all-start = ((bf16[16,72,128]{2,1,0:T(8,128)(2,1)}), bf16[16,72,128]{2,1,0:T(8,128)(2,1)S(1)}, u32[]{:S(2)}, u32[]{:S(2)}) async-start(bf16[16,72,128]{2,1,0:T(8,128)(2,1)} %get-tuple-element.23), calls=%async_computation | async-start | bytes 589824 | tf_op jit(solution)/shard_map/all_to_all | solution.py:381
  24.7 56.4 %all-gather.2.cloned.1.call-start = ((), (), s32[]{:S(2)}) async-start(), calls=%async_computation.3 | async-start | bytes 1253376 | tf_op jit(solution)/shard_map/all_gather | solution.py:408
  24.7 12.7 %copy-start.1 = (bf16[272,128]{1,0:T(8,128)(2,1)S(1)}, bf16[272,128]{1,0:T(8,128)(2,1)}, u32[]{:S(2)}) copy-start(bf16[272,128]{1,0:T(8,128)(2,1)} %get-tuple-element.24.forward_ref) | copy-start | bytes 208900
  24.8 10.6 %collective-permute-start = (bf16[272,128]{1,0:T(8,128)(2,1)}, bf16[272,128]{1,0:T(8,128)(2,1)S(1)}, u32[]{:S(2)}, u32[]{:S(2)}) collective-permute-start(bf16[272,128]{1,0:T(8,128)(2,1)} %get-tuple-element.24.forward_ref), channel_id=1, source_target_pairs={{0,32},{4,36},{8,40},{12,44},{16,48},{20,52},{24,56},{28,60},{32,0... | collective-permute-start | bytes 208904 | tf_op jit(solution)/shard_map/ppermute | solution.py:389
  28.2 39.0 %copy-start = (bf16[1,128,1024]{2,1,0:T(8,128)(2,1)S(1)}, bf16[1,128,1024]{2,1,0:T(8,128)(2,1)}, u32[]{:S(2)}) copy-start(bf16[1,128,1024]{2,1,0:T(8,128)(2,1)} %param.17) | copy-start | bytes 786436
  28.2 7.1 %collective-permute-start.2 = (bf16[32,1024]{1,0:T(8,128)(2,1)S(1)}, bf16[32,1024]{1,0:T(8,128)(2,1)S(1)}, u32[]{:S(2)}, u32[]{:S(2)}) collective-permute-start(bf16[32,1024]{1,0:T(8,128)(2,1)S(1)} %get-tuple-element.25), channel_id=1, source_target_pairs={{0,1},{1,0},{2,3},{3,2},{4,5},{5,4},{6,7},{7,6},{8,9},{9,8},{10,11... | collective-permute-start | bytes 196616 | tf_op jit(solution)/shard_map/ppermute | solution.py:393
  38.3 28.9 %all-to-all-start.1 = ((bf16[8,272,128]{2,1,0:T(8,128)(2,1)}), bf16[8,272,128]{2,1,0:T(8,128)(2,1)S(1)}, u32[]{:S(2)}, u32[]{:S(2)}) async-start(bf16[8,272,128]{2,1,0:T(8,128)(2,1)} %get-tuple-element.32), calls=%async_computation.1 | async-start | bytes 1114112 | tf_op jit(solution)/shard_map/all_to_all | solution.py:404
  45.2 15.8 %collective-permute-start.5 = (bf16[272,128]{1,0:T(8,128)(2,1)S(1)}, bf16[272,128]{1,0:T(8,128)(2,1)S(1)}, u32[]{:S(2)}, u32[]{:S(2)}) collective-permute-start(bf16[272,128]{1,0:T(8,128)(2,1)S(1)} %get-tuple-element.31.own_ref), channel_id=1, source_target_pairs={{0,36},{4,40},{8,44},{12,48},{16,52},{20,56},{24,60},{36,0},{40,4}... | collective-permute-start | bytes 208904 | tf_op jit(solution)/shard_map/ppermute | solution.py:407
  49.0 9.1 %collective-permute-start.3 = (bf16[32,1024]{1,0:T(8,128)(2,1)S(1)}, bf16[32,1024]{1,0:T(8,128)(2,1)S(1)}, u32[]{:S(2)}, u32[]{:S(2)}) collective-permute-start(bf16[32,1024]{1,0:T(8,128)(2,1)S(1)} %get-tuple-element.29), channel_id=1, source_target_pairs={{0,2},{1,3},{2,0},{3,1},{4,6},{5,7},{6,4},{7,5},{8,10},{9,11},{10,... | collective-permute-start | bytes 196616 | tf_op jit(solution)/shard_map/ppermute | solution.py:393
  53.7 7.3 %collective-permute-start.4 = (bf16[32,1024]{1,0:T(8,128)(2,1)S(1)}, bf16[32,1024]{1,0:T(8,128)(2,1)S(1)}, u32[]{:S(2)}, u32[]{:S(2)}) collective-permute-start(bf16[32,1024]{1,0:T(8,128)(2,1)S(1)} %get-tuple-element.30), channel_id=1, source_target_pairs={{0,3},{1,2},{2,1},{3,0},{4,7},{5,6},{6,5},{7,4},{8,11},{9,10},{10,... | collective-permute-start | bytes 196616 | tf_op jit(solution)/shard_map/ppermute | solution.py:393
  67.2 13.9 %copy-start.3 = (bf16[1,128,1024]{2,1,0:T(8,128)(2,1)S(1)}, bf16[1,128,1024]{2,1,0:T(8,128)(2,1)}, u32[]{:S(2)}) copy-start(bf16[1,128,1024]{2,1,0:T(8,128)(2,1)} %param.9) | copy-start | bytes 786436
  73.3 19.4 %all-to-all-start.2 = ((bf16[8,256,128]{2,1,0:T(8,128)(2,1)}), bf16[8,256,128]{2,1,0:T(8,128)(2,1)S(1)}, u32[]{:S(2)}, u32[]{:S(2)}) async-start(bf16[8,256,128]{2,1,0:T(8,128)(2,1)} %get-tuple-element.34), calls=%async_computation.2 | async-start | bytes 1048576 | tf_op jit(solution)/shard_map/all_to_all | solution.py:413
  76.8 20.1 %collective-permute-start.7 = (bf16[256,128]{1,0:T(8,128)(2,1)S(1)}, bf16[256,128]{1,0:T(8,128)(2,1)S(1)}, u32[]{:S(2)}, u32[]{:S(2)}) collective-permute-start(bf16[256,128]{1,0:T(8,128)(2,1)S(1)} %get-tuple-element.39), channel_id=1, source_target_pairs={{0,36},{4,40},{8,44},{12,48},{16,52},{20,56},{24,60},{36,0},{40,4}... | collective-permute-start | bytes 196616 | tf_op jit(solution)/shard_map/ppermute | solution.py:416
  81.1 1.2 %copy-start.2 = (bf16[16,272,128]{2,1,0:T(8,128)(2,1)S(1)}, bf16[16,272,128]{2,1,0:T(8,128)(2,1)}, u32[]{:S(2)}) copy-start(bf16[16,272,128]{2,1,0:T(8,128)(2,1)} %all-gather.2.cloned.1.call-done.gathered_ref) | copy-start | bytes 3342340
  92.9 5.6 %collective-permute-start.6 = (bf16[256,128]{1,0:T(8,128)(2,1)S(1)}, bf16[256,128]{1,0:T(8,128)(2,1)S(1)}, u32[]{:S(2)}, u32[]{:S(2)}) collective-permute-start(bf16[256,128]{1,0:T(8,128)(2,1)S(1)} %get-tuple-element.38), channel_id=1, source_target_pairs={{0,32},{4,36},{8,40},{12,44},{16,48},{20,52},{24,56},{28,60},{32,0... | collective-permute-start | bytes 196616 | tf_op jit(solution)/shard_map/ppermute | solution.py:428
Sparse Core Ops, SparseCore 0:
  38.5 41.3 all-gather.1

commit v4 on v3

--- a/solution.py
+++ b/solution.py
@@ -24,10 +24,12 @@
 BLOCK = 2 * ROWS + 16
 CUT = 2 * PIECE + 8
 
+FSDP_UP = {d: [(f, f + d) for f in range(16 - d)] for d in (1, 2, 4, 6, 8)}
 FSDP_SWAP = [(f, f ^ 8) for f in range(16)]
 FSDP_NINE = [(f, f + 9) for f in range(7)] + [(f + 9, f) for f in range(7)]
 SECTION_PAIRS = [(s, 7 - s) for s in range(8)]
-TP_ROUTES = [[(t, t ^ d) for t in range(4)] for d in range(4)]
+TP_NEAR = [(t, t ^ 1) for t in range(4)]
+TP_FAR = [(t, t ^ 2) for t in range(4)]
 MIRROR_GROUPS = [
     [(s * 16 + z * 8 + y) * 4 + t for s in (k, 7 - k) for z in range(2) for t in range(4)]
     for k in range(4)
@@ -73,16 +75,17 @@
     return top
 
 
-def forward_kernel(query_ref, gathered_ref, out_ref, mark_ref, keys, values_t, bias, scores):
+def forward_kernel(
+    query_ref, pair_0_ref, pair_2_ref, pair_4_ref, pair_6_ref, pair_8_ref, out_ref, mark_ref, keys, values_t, bias, scores
+):
     f, y, upper = fsdp_place()
+    pairs = (pair_0_ref, pair_2_ref, pair_4_ref, pair_6_ref, pair_8_ref)
     for d in range(HALO):
         valid = f >= d
-        block = jnp.maximum(f - d, 0)
-        crossed = jnp.where(upper & (block < SPAN), 1, 0)
-        entry = (block & (SPAN - 1)) * 2 + crossed
-        keys[d * ROWS : (d + 1) * ROWS, :] = gathered_ref[entry, 0:ROWS, :]
-        values_t[:, d * ROWS : (d + 1) * ROWS] = gathered_ref[entry, ROWS : 2 * ROWS, :].T
-        key_seg = gathered_ref[entry, 2 * ROWS : 2 * ROWS + 16, :].astype(jnp.float32)[0:1]
+        block = pairs[d >> 1][1 - (d & 1)]
+        keys[d * ROWS : (d + 1) * ROWS, :] = block[0:ROWS]
+        values_t[:, d * ROWS : (d + 1) * ROWS] = block[ROWS : 2 * ROWS].T
+        key_seg = block[2 * ROWS :].astype(jnp.float32)[0:1]
         if d == 0:
             query_seg = key_seg
         write_bias(bias, d, key_seg, query_seg, valid)
@@ -105,10 +108,9 @@
 
 
 def backward_kernel(
-    query_0_ref,
-    query_1_ref,
-    query_2_ref,
-    query_3_ref,
+    kept_ref,
+    near_ref,
+    far_ref,
     own_ref,
     slots_ref,
     nine_ref,
@@ -129,9 +131,9 @@
 ):
     f, y, upper = fsdp_place()
     t = lax.axis_index("tp").astype(jnp.int32)
-    for apart, ref in enumerate((query_0_ref, query_1_ref, query_2_ref, query_3_ref)):
+    for apart, piece in enumerate((kept_ref[0], near_ref[0], far_ref[0], far_ref[1])):
         at = pl.multiple_of((t ^ apart) * PIECE, PIECE)
-        queries[pl.ds(at, PIECE), :] = ref[...]
+        queries[pl.ds(at, PIECE), :] = piece
     for d in range(HALO):
         base = d * ROWS
         if d == 0:
@@ -230,15 +232,21 @@
     forward_ref[2 * ROWS :, :] = wide_ids(ids_ref)
 
 
-def split_kernel(query_ref, *part_refs):
+def split_kernel(query_ref, kept_ref, near_ref):
     t = lax.axis_index("tp").astype(jnp.int32)
-    for apart, ref in enumerate(part_refs):
+    for apart in range(PIECES):
         lo = pl.multiple_of((t ^ apart) * 1024, 1024)
-        ref[...] = query_ref[:, pl.ds(lo, 1024)]
-
-
-def outgoing_kernel(cuts_ref, forward_ref, forward_cross_ref, *refs):
-    own_ref, outgoing_ref, stacked_ref = refs[-3:]
+        ref = near_ref if apart & 1 else kept_ref
+        ref[apart >> 1] = query_ref[:, pl.ds(lo, 1024)]
+
+
+def pass_on_kernel(kept_ref, near_ref, far_ref):
+    far_ref[0] = kept_ref[1]
+    far_ref[1] = near_ref[1]
+
+
+def outgoing_kernel(cuts_ref, forward_ref, forward_before_ref, *refs):
+    own_ref, outgoing_ref, forward_pair_ref = refs[-3:]
     f, y, upper = fsdp_place()
     side = jnp.where(lax.axis_index("section") < 4, 2 * PIECES, 0)
     row = jnp.where(upper, PIECES, 0)
@@ -256,8 +264,8 @@
     own_ref[...] = own
     for target in range(SPAN):
         outgoing_ref[target] = jnp.where(upper & (target <= y), crossed, own)
-    stacked_ref[0] = forward_ref[...]
-    stacked_ref[1] = forward_cross_ref[...]
+    forward_pair_ref[0] = forward_before_ref[...]
+    forward_pair_ref[1] = forward_ref[...]
 
 
 def reduce_kernel(parts_ref, own_part_ref, *refs):
@@ -301,14 +309,14 @@
     )(*arrays, *waits)
 
 
-def run_forward(query, gathered):
+def run_forward(query, *pairs):
     return pl.pallas_call(
         forward_kernel,
         out_shape=(
             jax.ShapeDtypeStruct((ROWS, 1024), jnp.bfloat16),
             jax.ShapeDtypeStruct((8, 128), jnp.float32),
         ),
-        in_specs=[VMEM, VMEM],
+        in_specs=[VMEM] * 6,
         out_specs=(VMEM, VMEM),
         scratch_shapes=[
             pltpu.VMEM((KEYS, HEAD_DIM), jnp.bfloat16),
@@ -321,7 +329,7 @@
             flops=2 * 2 * 1024 * KEYS * 128, bytes_accessed=3_000_000, transcendentals=1024 * KEYS
         ),
         name="forward_attention",
-    )(query, gathered)
+    )(query, *pairs)
 
 
 def run_backward(queries, own, slots, nine, grad):
@@ -333,7 +341,7 @@
             jax.ShapeDtypeStruct((2 * ROWS, HEAD_DIM), jnp.bfloat16),
             jax.ShapeDtypeStruct((2 * ROWS, HEAD_DIM), jnp.float32),
         ),
-        in_specs=[VMEM] * 8,
+        in_specs=[VMEM] * 7,
         out_specs=(VMEM, VMEM, VMEM, VMEM),
         scratch_shapes=[
             pltpu.VMEM((ROWS, 1024), jnp.bfloat16),
@@ -386,35 +394,36 @@
         tiled=False,
         axis_index_groups=MIRROR_GROUPS,
     )
-    forward_cross = lax.ppermute(forward_part, "fsdp", FSDP_SWAP)
-    parts = run_small(
-        split_kernel, "split", SMALL_LIMIT, ((PIECE, 1024),) * 4, query_back, flops=3e10
-    )
-    stash = [parts[0]] + [lax.ppermute(parts[d], "tp", TP_ROUTES[d]) for d in (1, 2, 3)]
-    own, outgoing, stacked = run_small(
+    forward_before = lax.ppermute(forward_part, "fsdp", FSDP_UP[1])
+    kept, near = run_small(
+        split_kernel, "split", SMALL_LIMIT, ((2, PIECE, 1024),) * 2, query_back, flops=3e10
+    )
+    near = lax.ppermute(near, "tp", TP_NEAR)
+    own, outgoing, forward_pair = run_small(
         outgoing_kernel,
         "outgoing",
         SMALL_LIMIT,
         ((BLOCK, 128), (SPAN, BLOCK, 128), (2, BLOCK, 128)),
         cuts,
         forward_part,
-        forward_cross,
-        waits=stash[1:2],
+        forward_before,
     )
     slots = lax.all_to_all(
         outgoing, "fsdp", split_axis=0, concat_axis=0, tiled=False, axis_index_groups=ROW_GROUPS
     )
+    (far,) = run_small(
+        pass_on_kernel, "pass_on", SMALL_LIMIT, ((2, PIECE, 1024),), kept, near, flops=3e10
+    )
+    far = lax.ppermute(far, "tp", TP_FAR)
     nine = lax.ppermute(own, "fsdp", FSDP_NINE)
-    gathered = lax.all_gather(
-        stacked, "fsdp", axis=0, tiled=True, axis_index_groups=ROW_GROUPS
-    )
-
-    query_grad, send, send_nine, own_part = run_backward(stash, own, slots, nine, out_grad[0])
+    pairs = {d: lax.ppermute(forward_pair, "fsdp", FSDP_UP[d]) for d in (8, 6, 4, 2)}
+
+    query_grad, send, send_nine, own_part = run_backward((kept, near, far), own, slots, nine, out_grad[0])
     parts = lax.all_to_all(
         send, "fsdp", split_axis=0, concat_axis=0, tiled=False, axis_index_groups=ROW_GROUPS
     )
     from_nine = lax.ppermute(send_nine, "fsdp", FSDP_NINE)
-    attn_out, mark = run_forward(queries[0], gathered)
+    attn_out, mark = run_forward(queries[0], forward_pair, pairs[2], pairs[4], pairs[6], pairs[8])
 
     same_row, other_row = run_small(
         reduce_kernel,
@@ -423,7 +432,7 @@
         ((2 * ROWS, 128, jnp.float32), (2 * ROWS, 128)),
         parts,
         own_part,
-        waits=(mark,),
+        waits=(),
     )
     from_upper = lax.ppermute(other_row, "fsdp", FSDP_SWAP)
     key_grad, value_grad = run_small(

time: 108 us -> 100 us (0.926)
  the two profiles are of different devices: /device:TPU:1 before, /device:TPU:72 now
where the time goes in v4:
time: 100 us; the launch traced here: 99.2 us
  starting transfers between devices  65.3 us (65%)
  waiting for transfers between devices  20.2 us (20%)
  Pallas kernels  13 us (13%)
    ppermute x4, starting transfers between devices, local(): lax.ppermute(forward_pair, 'fsdp', FSDP_UP[d])  11.4 us
    all_to_all x1, starting transfers between devices, local(): lax.all_to_all(cuts, ('section', 'fsdp', 'tp'), split_axis=0, concat_axis...  10.2 us
    all_to_all x1, starting transfers between devices, local(): lax.all_to_all(outgoing, 'fsdp', split_axis=0, concat_axis=0, tiled=False...  7.96 us
    ppermute x1, starting transfers between devices, local(): from_nine = lax.ppermute(send_nine, 'fsdp', FSDP_NINE)  7.25 us
    ppermute x4, waiting for transfers between devices, local(): lax.ppermute(forward_pair, 'fsdp', FSDP_UP[d])  7.05 us
    pallas_call x1, Pallas kernels, run_backward(): pl.pallas_call(backward_kernel, out_shape=(jax.ShapeDtypeStruct((ROWS, 10...  6.07 us
    ppermute x1, starting transfers between devices, local(): far = lax.ppermute(far, 'tp', TP_FAR)  6.06 us
    all_to_all x1, starting transfers between devices, local(): lax.all_to_all(send, 'fsdp', split_axis=0, concat_axis=0, tiled=False, ax...  5.21 us
  transfers between devices with their start and end apart: 14, of which 6 were waited for; matrix products, arithmetic and copies ran while one was open for 0% of the time, Pallas kernels for 6%

profile of v4, /device:TPU:72, one launch (start us, length us, event | category | flops | bytes accessed | tf_op | source)
XLA Modules:
  0.0 99.2 jit_solution(4214194038325979866)
XLA Ops:
  0.6 4.1 %collective-permute-start.5 = (bf16[32,4096]{1,0:T(8,128)(2,1)}, bf16[32,4096]{1,0:T(8,128)(2,1)S(1)}, u32[]{:S(2)}, u32[]{:S(2)}) collective-permute-start(bf16[32,4096]{1,0:T(8,128)(2,1)} %bitcast.7), channel_id=1, source_target_pairs={{0,448},{64,384},{128,320},{192,256},{256,192},{320,128},{384,64},... | collective-permute-start | bytes 786440 | tf_op jit(solution)/shard_map/ppermute | solution.py:376
  4.7 1.6 %prepare.1 = (bf16[16,72,128]{2,1,0:T(8,128)(2,1)}, bf16[272,128]{1,0:T(8,128)(2,1)}) custom-call(bf16[1,32,512]{2,1,0:T(8,128)(2,1)} %held_key_ref.1, bf16[1,32,512]{2,1,0:T(8,128)(2,1)} %held_value_ref.1, s32[1,128]{1,0:T(1,128)} %held_ids_ref.1, bf16[1,128,128]{2,1,0:T(8,128)(2,1)} %key_ref.1, bf16[1,128,128]{2,1,0:T(8,128)(2,1)} %value_ref.1, ...), custom_call_target="tpu_custom_call" | custom-call | tf_op jit(solution)/shard_map/prepare/pallas_call | solution.py:294
  6.3 10.2 %all-to-all-start = ((bf16[16,72,128]{2,1,0:T(8,128)(2,1)}), bf16[16,72,128]{2,1,0:T(8,128)(2,1)S(1)}, u32[]{:S(2)}, u32[]{:S(2)}) async-start(bf16[16,72,128]{2,1,0:T(8,128)(2,1)} %get-tuple-element.20), calls=%async_computation | async-start | bytes 589824 | tf_op jit(solution)/shard_map/all_to_all | solution.py:389
  16.5 0.0 copy-start.1
  16.5 0.0 collective-permute-done.5.query_ref
  16.6 4.3 %collective-permute-start.6 = (bf16[2,32,1024]{2,1,0:T(8,128)(2,1)S(1)}, bf16[2,32,1024]{2,1,0:T(8,128)(2,1)S(1)}, u32[]{:S(2)}, u32[]{:S(2)}) collective-permute-start(bf16[2,32,1024]{2,1,0:T(8,128)(2,1)S(1)} %get-tuple-element.25), channel_id=1, source_target_pairs={{0,1},{1,0},{2,3},{3,2},{4,5},{5,4},{6,7},{7,6},{8,9},{9,8},{10,11... | collective-permute-start | bytes 393224 | tf_op jit(solution)/shard_map/ppermute | solution.py:401
  20.9 0.0 copy-done.1
  20.9 3.5 %collective-permute-start = (bf16[272,128]{1,0:T(8,128)(2,1)S(1)}, bf16[272,128]{1,0:T(8,128)(2,1)S(1)}, u32[]{:S(2)}, u32[]{:S(2)}) collective-permute-start(bf16[272,128]{1,0:T(8,128)(2,1)S(1)} %copy-done.1), channel_id=1, source_target_pairs={{0,4},{4,8},{8,12},{12,16},{16,20},{20,24},{24,28},{28,32},{32,36}... | collective-permute-start | bytes 208904 | tf_op jit(solution)/shard_map/ppermute | solution.py:397
  24.4 2.7 %collective-permute-done.forward_before_ref = bf16[272,128]{1,0:T(8,128)(2,1)S(1)} collective-permute-done((bf16[272,128]{1,0:T(8,128)(2,1)S(1)}, bf16[272,128]{1,0:T(8,128)(2,1)S(1)}, u32[]{:S(2)}, u32[]{:S(2)}) %collective-permute-start) | collective-permute-done | bytes 69664 | tf_op jit(solution)/shard_map/ppermute | solution.py:397
  27.1 0.8 all-to-all-done.cuts_ref
  27.9 0.9 outgoing.1
  28.8 8.0 %all-to-all-start.1 = ((bf16[8,272,128]{2,1,0:T(8,128)(2,1)}), bf16[8,272,128]{2,1,0:T(8,128)(2,1)S(1)}, u32[]{:S(2)}, u32[]{:S(2)}) async-start(bf16[8,272,128]{2,1,0:T(8,128)(2,1)} %get-tuple-element.27), calls=%async_computation.1 | async-start | bytes 1114112 | tf_op jit(solution)/shard_map/all_to_all | solution.py:411
  36.7 0.0 collective-permute-done.6.near_ref
  36.7 0.0 copy-start
  36.8 6.1 %collective-permute-start.7 = (bf16[2,32,1024]{2,1,0:T(8,128)(2,1)S(1)}, bf16[2,32,1024]{2,1,0:T(8,128)(2,1)S(1)}, u32[]{:S(2)}, u32[]{:S(2)}) collective-permute-start(bf16[2,32,1024]{2,1,0:T(8,128)(2,1)S(1)} %pass_on.1), channel_id=1, source_target_pairs={{0,2},{1,3},{2,0},{3,1},{4,6},{5,7},{6,4},{7,5},{8,10},{9,11},{10,... | collective-permute-start | bytes 393224 | tf_op jit(solution)/shard_map/ppermute | solution.py:417
  42.8 1.9 %collective-permute-start.8 = (bf16[272,128]{1,0:T(8,128)(2,1)S(1)}, bf16[272,128]{1,0:T(8,128)(2,1)S(1)}, u32[]{:S(2)}, u32[]{:S(2)}) collective-permute-start(bf16[272,128]{1,0:T(8,128)(2,1)S(1)} %get-tuple-element.26.own_ref), channel_id=1, source_target_pairs={{0,36},{4,40},{8,44},{12,48},{16,52},{20,56},{24,60},{36,0},{40,4}... | collective-permute-start | bytes 208904 | tf_op jit(solution)/shard_map/ppermute | solution.py:418
  44.8 3.9 %collective-permute-done.7.far_ref = bf16[2,32,1024]{2,1,0:T(8,128)(2,1)S(1)} collective-permute-done((bf16[2,32,1024]{2,1,0:T(8,128)(2,1)S(1)}, bf16[2,32,1024]{2,1,0:T(8,128)(2,1)S(1)}, u32[]{:S(2)}, u32[]{:S(2)}) %collective-permute-start.7) | collective-permute-done | bytes 131104 | tf_op jit(solution)/shard_map/ppermute | solution.py:417
  48.6 2.3 %collective-permute-done.8.nine_ref = bf16[272,128]{1,0:T(8,128)(2,1)S(1)} collective-permute-done((bf16[272,128]{1,0:T(8,128)(2,1)S(1)}, bf16[272,128]{1,0:T(8,128)(2,1)S(1)}, u32[]{:S(2)}, u32[]{:S(2)}) %collective-permute-start.8) | collective-permute-done | bytes 69664 | tf_op jit(solution)/shard_map/ppermute | solution.py:418
  51.0 3.3 %all-to-all-done.1.slots_ref = bf16[8,272,128]{2,1,0:T(8,128)(2,1)S(1)} async-done(((bf16[8,272,128]{2,1,0:T(8,128)(2,1)}), bf16[8,272,128]{2,1,0:T(8,128)(2,1)S(1)}, u32[]{:S(2)}, u32[]{:S(2)}) %all-to-all-start.1) | async-done | bytes 557088 | tf_op jit(solution)/shard_map/all_to_all | solution.py:411
  54.3 0.0 copy-done
  54.3 6.1 %backward_attention.1 = (bf16[128,1024]{1,0:T(8,128)(2,1)}, bf16[8,256,128]{2,1,0:T(8,128)(2,1)}, bf16[256,128]{1,0:T(8,128)(2,1)S(1)}, f32[256,128]{1,0:T(8,128)S(1)}) custom-call(bf16[2,32,1024]{2,1,0:T(8,128)(2,1)S(1)} %get-tuple-element.24.kept_ref, bf16[2,32,1024]{2,1,0:T(8,128)(2,1)S(1)} %collective-permute-done.6.near_ref, ...), custom_call_target="tpu_custom_call" | custom-call | flops 1000000 | tf_op jit(solution)/shard_map/backward_attention/pallas_call | solution.py:336
  60.4 5.2 %all-to-all-start.2 = ((bf16[8,256,128]{2,1,0:T(8,128)(2,1)}), bf16[8,256,128]{2,1,0:T(8,128)(2,1)S(1)}, u32[]{:S(2)}, u32[]{:S(2)}) async-start(bf16[8,256,128]{2,1,0:T(8,128)(2,1)} %get-tuple-element.29), calls=%async_computation.2 | async-start | bytes 1048576 | tf_op jit(solution)/shard_map/all_to_all | solution.py:422
  65.6 1.3 %collective-permute-start.4 = (bf16[2,272,128]{2,1,0:T(8,128)(2,1)S(1)}, bf16[2,272,128]{2,1,0:T(8,128)(2,1)S(1)}, u32[]{:S(2)}, u32[]{:S(2)}) collective-permute-start(bf16[2,272,128]{2,1,0:T(8,128)(2,1)S(1)} %get-tuple-element.22.pair_0_ref), channel_id=1, source_target_pairs={{0,32},{4,36},{8,40},{12,44},{16,48},{20,52},{24,56},{28,60},{1,33... | collective-permute-start | bytes 417800 | tf_op jit(solution)/shard_map/ppermute | solution.py:419
  66.9 4.6 %collective-permute-start.3 = (bf16[2,272,128]{2,1,0:T(8,128)(2,1)S(1)}, bf16[2,272,128]{2,1,0:T(8,128)(2,1)S(1)}, u32[]{:S(2)}, u32[]{:S(2)}) collective-permute-start(bf16[2,272,128]{2,1,0:T(8,128)(2,1)S(1)} %get-tuple-element.22.pair_0_ref), channel_id=1, source_target_pairs={{0,24},{4,28},{8,32},{12,36},{16,40},{20,44},{24,48},{28,52},{32,5... | collective-permute-start | bytes 417800 | tf_op jit(solution)/shard_map/ppermute | solution.py:419
  71.5 3.1 %collective-permute-start.2 = (bf16[2,272,128]{2,1,0:T(8,128)(2,1)S(1)}, bf16[2,272,128]{2,1,0:T(8,128)(2,1)S(1)}, u32[]{:S(2)}, u32[]{:S(2)}) collective-permute-start(bf16[2,272,128]{2,1,0:T(8,128)(2,1)S(1)} %get-tuple-element.22.pair_0_ref), channel_id=1, source_target_pairs={{0,16},{4,20},{8,24},{12,28},{16,32},{20,36},{24,40},{28,44},{32,4... | collective-permute-start | bytes 417800 | tf_op jit(solution)/shard_map/ppermute | solution.py:419
  74.6 2.5 %collective-permute-start.1 = (bf16[2,272,128]{2,1,0:T(8,128)(2,1)S(1)}, bf16[2,272,128]{2,1,0:T(8,128)(2,1)S(1)}, u32[]{:S(2)}, u32[]{:S(2)}) collective-permute-start(bf16[2,272,128]{2,1,0:T(8,128)(2,1)S(1)} %get-tuple-element.22.pair_0_ref), channel_id=1, source_target_pairs={{0,8},{4,12},{8,16},{12,20},{16,24},{20,28},{24,32},{28,36},{32,40... | collective-permute-start | bytes 417800 | tf_op jit(solution)/shard_map/ppermute | solution.py:419
  77.1 7.3 %collective-permute-start.10 = (bf16[256,128]{1,0:T(8,128)(2,1)S(1)}, bf16[256,128]{1,0:T(8,128)(2,1)S(1)}, u32[]{:S(2)}, u32[]{:S(2)}) collective-permute-start(bf16[256,128]{1,0:T(8,128)(2,1)S(1)} %get-tuple-element.33), channel_id=1, source_target_pairs={{0,36},{4,40},{8,44},{12,48},{16,52},{20,56},{24,60},{36,0},{40,4}... | collective-permute-start | bytes 196616 | tf_op jit(solution)/shard_map/ppermute | solution.py:425
  84.3 0.0 all-to-all-done.2.parts_ref
  84.4 0.0 copy-start.2
  84.4 0.2 reduce.1
  84.6 0.0 collective-permute-done.4.pair_8_ref
  84.6 3.4 %collective-permute-start.9 = (bf16[256,128]{1,0:T(8,128)(2,1)S(1)}, bf16[256,128]{1,0:T(8,128)(2,1)S(1)}, u32[]{:S(2)}, u32[]{:S(2)}) collective-permute-start(bf16[256,128]{1,0:T(8,128)(2,1)S(1)} %get-tuple-element.32), channel_id=1, source_target_pairs={{0,32},{4,36},{8,40},{12,44},{16,48},{20,52},{24,56},{28,60},{32,0... | collective-permute-start | bytes 196616 | tf_op jit(solution)/shard_map/ppermute | solution.py:437
  88.0 0.0 collective-permute-done.3.pair_6_ref
  88.0 7.0 %collective-permute-done.2.pair_4_ref = bf16[2,272,128]{2,1,0:T(8,128)(2,1)S(1)} collective-permute-done((bf16[2,272,128]{2,1,0:T(8,128)(2,1)S(1)}, bf16[2,272,128]{2,1,0:T(8,128)(2,1)S(1)}, u32[]{:S(2)}, u32[]{:S(2)}) %collective-permute-start.2) | collective-permute-done | bytes 139296 | tf_op jit(solution)/shard_map/ppermute | solution.py:419
  95.1 0.0 collective-permute-done.1.pair_2_ref
  95.1 0.0 copy-done.2
  95.1 3.5 %forward_attention.1 = (bf16[128,1024]{1,0:T(8,128)(2,1)}, f32[8,128]{1,0:T(8,128)}) custom-call(bf16[128,1024]{1,0:T(8,128)(2,1)S(1)} %bitcast.6, bf16[2,272,128]{2,1,0:T(8,128)(2,1)S(1)} %get-tuple-element.22.pair_0_ref, bf16[2,272,128]{2,1,0:T(8,128)(2,1)S(1)} %collective-permute-done.1.pair_2_ref, ...), custom_call_target="tpu_custom_call" | custom-call | flops 671088640 | bytes 3000000 | tf_op jit(solution)/shard_map/forward_attention/pallas_call | solution.py:313
  98.6 0.0 collective-permute-done.10.from_nine_ref
  98.6 0.0 collective-permute-done.9.from_upper_ref
  98.6 0.7 finish.1
  (2 shorter events, 0.0 us)
Async XLA Ops:
  0.6 15.9 %collective-permute-start.5 = (bf16[32,4096]{1,0:T(8,128)(2,1)}, bf16[32,4096]{1,0:T(8,128)(2,1)S(1)}, u32[]{:S(2)}, u32[]{:S(2)}) collective-permute-start(bf16[32,4096]{1,0:T(8,128)(2,1)} %bitcast.7), channel_id=1, source_target_pairs={{0,448},{64,384},{128,320},{192,256},{256,192},{320,128},{384,64},... | collective-permute-start | bytes 786440 | tf_op jit(solution)/shard_map/ppermute | solution.py:376
  6.3 21.5 %all-to-all-start = ((bf16[16,72,128]{2,1,0:T(8,128)(2,1)}), bf16[16,72,128]{2,1,0:T(8,128)(2,1)S(1)}, u32[]{:S(2)}, u32[]{:S(2)}) async-start(bf16[16,72,128]{2,1,0:T(8,128)(2,1)} %get-tuple-element.20), calls=%async_computation | async-start | bytes 589824 | tf_op jit(solution)/shard_map/all_to_all | solution.py:389
  16.5 4.3 %copy-start.1 = (bf16[272,128]{1,0:T(8,128)(2,1)S(1)}, bf16[272,128]{1,0:T(8,128)(2,1)}, u32[]{:S(2)}) copy-start(bf16[272,128]{1,0:T(8,128)(2,1)} %get-tuple-element.21.forward_ref) | copy-start | bytes 208900
  16.6 20.2 %collective-permute-start.6 = (bf16[2,32,1024]{2,1,0:T(8,128)(2,1)S(1)}, bf16[2,32,1024]{2,1,0:T(8,128)(2,1)S(1)}, u32[]{:S(2)}, u32[]{:S(2)}) collective-permute-start(bf16[2,32,1024]{2,1,0:T(8,128)(2,1)S(1)} %get-tuple-element.25), channel_id=1, source_target_pairs={{0,1},{1,0},{2,3},{3,2},{4,5},{5,4},{6,7},{7,6},{8,9},{9,8},{10,11... | collective-permute-start | bytes 393224 | tf_op jit(solution)/shard_map/ppermute | solution.py:401
  20.9 6.2 %collective-permute-start = (bf16[272,128]{1,0:T(8,128)(2,1)S(1)}, bf16[272,128]{1,0:T(8,128)(2,1)S(1)}, u32[]{:S(2)}, u32[]{:S(2)}) collective-permute-start(bf16[272,128]{1,0:T(8,128)(2,1)S(1)} %copy-done.1), channel_id=1, source_target_pairs={{0,4},{4,8},{8,12},{12,16},{16,20},{20,24},{24,28},{28,32},{32,36}... | collective-permute-start | bytes 208904 | tf_op jit(solution)/shard_map/ppermute | solution.py:397
  28.8 25.6 %all-to-all-start.1 = ((bf16[8,272,128]{2,1,0:T(8,128)(2,1)}), bf16[8,272,128]{2,1,0:T(8,128)(2,1)S(1)}, u32[]{:S(2)}, u32[]{:S(2)}) async-start(bf16[8,272,128]{2,1,0:T(8,128)(2,1)} %get-tuple-element.27), calls=%async_computation.1 | async-start | bytes 1114112 | tf_op jit(solution)/shard_map/all_to_all | solution.py:411
  36.7 17.6 %copy-start = (bf16[1,128,1024]{2,1,0:T(8,128)(2,1)S(1)}, bf16[1,128,1024]{2,1,0:T(8,128)(2,1)}, u32[]{:S(2)}) copy-start(bf16[1,128,1024]{2,1,0:T(8,128)(2,1)} %param.17) | copy-start | bytes 786436
  36.8 11.9 %collective-permute-start.7 = (bf16[2,32,1024]{2,1,0:T(8,128)(2,1)S(1)}, bf16[2,32,1024]{2,1,0:T(8,128)(2,1)S(1)}, u32[]{:S(2)}, u32[]{:S(2)}) collective-permute-start(bf16[2,32,1024]{2,1,0:T(8,128)(2,1)S(1)} %pass_on.1), channel_id=1, source_target_pairs={{0,2},{1,3},{2,0},{3,1},{4,6},{5,7},{6,4},{7,5},{8,10},{9,11},{10,... | collective-permute-start | bytes 393224 | tf_op jit(solution)/shard_map/ppermute | solution.py:417
  42.8 8.2 %collective-permute-start.8 = (bf16[272,128]{1,0:T(8,128)(2,1)S(1)}, bf16[272,128]{1,0:T(8,128)(2,1)S(1)}, u32[]{:S(2)}, u32[]{:S(2)}) collective-permute-start(bf16[272,128]{1,0:T(8,128)(2,1)S(1)} %get-tuple-element.26.own_ref), channel_id=1, source_target_pairs={{0,36},{4,40},{8,44},{12,48},{16,52},{20,56},{24,60},{36,0},{40,4}... | collective-permute-start | bytes 208904 | tf_op jit(solution)/shard_map/ppermute | solution.py:418
  60.4 23.9 %all-to-all-start.2 = ((bf16[8,256,128]{2,1,0:T(8,128)(2,1)}), bf16[8,256,128]{2,1,0:T(8,128)(2,1)S(1)}, u32[]{:S(2)}, u32[]{:S(2)}) async-start(bf16[8,256,128]{2,1,0:T(8,128)(2,1)} %get-tuple-element.29), calls=%async_computation.2 | async-start | bytes 1048576 | tf_op jit(solution)/shard_map/all_to_all | solution.py:422
  65.6 19.0 %collective-permute-start.4 = (bf16[2,272,128]{2,1,0:T(8,128)(2,1)S(1)}, bf16[2,272,128]{2,1,0:T(8,128)(2,1)S(1)}, u32[]{:S(2)}, u32[]{:S(2)}) collective-permute-start(bf16[2,272,128]{2,1,0:T(8,128)(2,1)S(1)} %get-tuple-element.22.pair_0_ref), channel_id=1, source_target_pairs={{0,32},{4,36},{8,40},{12,44},{16,48},{20,52},{24,56},{28,60},{1,33... | collective-permute-start | bytes 417800 | tf_op jit(solution)/shard_map/ppermute | solution.py:419
  66.9 21.1 %collective-permute-start.3 = (bf16[2,272,128]{2,1,0:T(8,128)(2,1)S(1)}, bf16[2,272,128]{2,1,0:T(8,128)(2,1)S(1)}, u32[]{:S(2)}, u32[]{:S(2)}) collective-permute-start(bf16[2,272,128]{2,1,0:T(8,128)(2,1)S(1)} %get-tuple-element.22.pair_0_ref), channel_id=1, source_target_pairs={{0,24},{4,28},{8,32},{12,36},{16,40},{20,44},{24,48},{28,52},{32,5... | collective-permute-start | bytes 417800 | tf_op jit(solution)/shard_map/ppermute | solution.py:419
  71.5 23.6 %collective-permute-start.2 = (bf16[2,272,128]{2,1,0:T(8,128)(2,1)S(1)}, bf16[2,272,128]{2,1,0:T(8,128)(2,1)S(1)}, u32[]{:S(2)}, u32[]{:S(2)}) collective-permute-start(bf16[2,272,128]{2,1,0:T(8,128)(2,1)S(1)} %get-tuple-element.22.pair_0_ref), channel_id=1, source_target_pairs={{0,16},{4,20},{8,24},{12,28},{16,32},{20,36},{24,40},{28,44},{32,4... | collective-permute-start | bytes 417800 | tf_op jit(solution)/shard_map/ppermute | solution.py:419
  74.6 20.5 %collective-permute-start.1 = (bf16[2,272,128]{2,1,0:T(8,128)(2,1)S(1)}, bf16[2,272,128]{2,1,0:T(8,128)(2,1)S(1)}, u32[]{:S(2)}, u32[]{:S(2)}) collective-permute-start(bf16[2,272,128]{2,1,0:T(8,128)(2,1)S(1)} %get-tuple-element.22.pair_0_ref), channel_id=1, source_target_pairs={{0,8},{4,12},{8,16},{12,20},{16,24},{20,28},{24,32},{28,36},{32,40... | collective-permute-start | bytes 417800 | tf_op jit(solution)/shard_map/ppermute | solution.py:419
  77.1 21.5 %collective-permute-start.10 = (bf16[256,128]{1,0:T(8,128)(2,1)S(1)}, bf16[256,128]{1,0:T(8,128)(2,1)S(1)}, u32[]{:S(2)}, u32[]{:S(2)}) collective-permute-start(bf16[256,128]{1,0:T(8,128)(2,1)S(1)} %get-tuple-element.33), channel_id=1, source_target_pairs={{0,36},{4,40},{8,44},{12,48},{16,52},{20,56},{24,60},{36,0},{40,4}... | collective-permute-start | bytes 196616 | tf_op jit(solution)/shard_map/ppermute | solution.py:425
  84.4 10.7 %copy-start.2 = (bf16[1,128,1024]{2,1,0:T(8,128)(2,1)S(1)}, bf16[1,128,1024]{2,1,0:T(8,128)(2,1)}, u32[]{:S(2)}) copy-start(bf16[1,128,1024]{2,1,0:T(8,128)(2,1)} %param.9) | copy-start | bytes 786436
  84.6 14.0 %collective-permute-start.9 = (bf16[256,128]{1,0:T(8,128)(2,1)S(1)}, bf16[256,128]{1,0:T(8,128)(2,1)S(1)}, u32[]{:S(2)}, u32[]{:S(2)}) collective-permute-start(bf16[256,128]{1,0:T(8,128)(2,1)S(1)} %get-tuple-element.32), channel_id=1, source_target_pairs={{0,32},{4,36},{8,40},{12,44},{16,48},{20,52},{24,56},{28,60},{32,0... | collective-permute-start | bytes 196616 | tf_op jit(solution)/shard_map/ppermute | solution.py:437

commit v5 on v4

--- a/solution.py
+++ b/solution.py
@@ -115,20 +115,23 @@
     slots_ref,
     nine_ref,
     grad_ref,
-    query_grad_ref,
-    send_ref,
-    send_nine_ref,
-    own_part_ref,
-    queries,
-    keys,
-    keys_t,
-    values,
-    bias,
-    scores,
-    prob_grads,
-    key_sum,
-    value_sum,
+    *refs,
 ):
+    (
+        query_grad_ref,
+        send_ref,
+        send_nine_ref,
+        own_part_ref,
+        queries,
+        keys,
+        keys_t,
+        values,
+        bias,
+        scores,
+        prob_grads,
+        key_sum,
+        value_sum,
+    ) = refs[1:]
     f, y, upper = fsdp_place()
     t = lax.axis_index("tp").astype(jnp.int32)
     for apart, piece in enumerate((kept_ref[0], near_ref[0], far_ref[0], far_ref[1])):
@@ -240,13 +243,14 @@
         ref[apart >> 1] = query_ref[:, pl.ds(lo, 1024)]
 
 
-def pass_on_kernel(kept_ref, near_ref, far_ref):
+def pass_on_kernel(kept_ref, near_ref, forward_ref, forward_before_ref, far_ref, forward_pair_ref):
     far_ref[0] = kept_ref[1]
     far_ref[1] = near_ref[1]
-
-
-def outgoing_kernel(cuts_ref, forward_ref, forward_before_ref, *refs):
-    own_ref, outgoing_ref, forward_pair_ref = refs[-3:]
+    forward_pair_ref[0] = forward_before_ref[...]
+    forward_pair_ref[1] = forward_ref[...]
+
+
+def outgoing_kernel(cuts_ref, own_ref, outgoing_ref):
     f, y, upper = fsdp_place()
     side = jnp.where(lax.axis_index("section") < 4, 2 * PIECES, 0)
     row = jnp.where(upper, PIECES, 0)
@@ -264,8 +268,6 @@
     own_ref[...] = own
     for target in range(SPAN):
         outgoing_ref[target] = jnp.where(upper & (target <= y), crossed, own)
-    forward_pair_ref[0] = forward_before_ref[...]
-    forward_pair_ref[1] = forward_ref[...]
 
 
 def reduce_kernel(parts_ref, own_part_ref, *refs):
@@ -332,7 +334,7 @@
     )(query, *pairs)
 
 
-def run_backward(queries, own, slots, nine, grad):
+def run_backward(queries, own, slots, nine, grad, *waits):
     return pl.pallas_call(
         backward_kernel,
         out_shape=(
@@ -341,7 +343,7 @@
             jax.ShapeDtypeStruct((2 * ROWS, HEAD_DIM), jnp.bfloat16),
             jax.ShapeDtypeStruct((2 * ROWS, HEAD_DIM), jnp.float32),
         ),
-        in_specs=[VMEM] * 7,
+        in_specs=[VMEM] * 7 + [ANY] * len(waits),
         out_specs=(VMEM, VMEM, VMEM, VMEM),
         scratch_shapes=[
             pltpu.VMEM((ROWS, 1024), jnp.bfloat16),
@@ -359,7 +361,7 @@
             flops=1_000_000, bytes_accessed=0, transcendentals=0
         ),
         name="backward_attention",
-    )(*queries, own, slots, nine, grad)
+    )(*queries, own, slots, nine, grad, *waits)
 
 
 def local(
@@ -399,26 +401,34 @@
         split_kernel, "split", SMALL_LIMIT, ((2, PIECE, 1024),) * 2, query_back, flops=3e10
     )
     near = lax.ppermute(near, "tp", TP_NEAR)
-    own, outgoing, forward_pair = run_small(
+    own, outgoing = run_small(
         outgoing_kernel,
         "outgoing",
         SMALL_LIMIT,
-        ((BLOCK, 128), (SPAN, BLOCK, 128), (2, BLOCK, 128)),
+        ((BLOCK, 128), (SPAN, BLOCK, 128)),
         cuts,
+    )
+    slots = lax.all_to_all(
+        outgoing, "fsdp", split_axis=0, concat_axis=0, tiled=False, axis_index_groups=ROW_GROUPS
+    )
+    far, forward_pair = run_small(
+        pass_on_kernel,
+        "pass_on",
+        SMALL_LIMIT,
+        ((2, PIECE, 1024), (2, BLOCK, 128)),
+        kept,
+        near,
         forward_part,
         forward_before,
-    )
-    slots = lax.all_to_all(
-        outgoing, "fsdp", split_axis=0, concat_axis=0, tiled=False, axis_index_groups=ROW_GROUPS
-    )
-    (far,) = run_small(
-        pass_on_kernel, "pass_on", SMALL_LIMIT, ((2, PIECE, 1024),), kept, near, flops=3e10
+        flops=3e10,
     )
     far = lax.ppermute(far, "tp", TP_FAR)
     nine = lax.ppermute(own, "fsdp", FSDP_NINE)
     pairs = {d: lax.ppermute(forward_pair, "fsdp", FSDP_UP[d]) for d in (8, 6, 4, 2)}
 
-    query_grad, send, send_nine, own_part = run_backward((kept, near, far), own, slots, nine, out_grad[0])
+    query_grad, send, send_nine, own_part = run_backward(
+        (kept, near, far), own, slots, nine, out_grad[0], pairs[4]
+    )
     parts = lax.all_to_all(
         send, "fsdp", split_axis=0, concat_axis=0, tiled=False, axis_index_groups=ROW_GROUPS
     )

time: 100 us -> 99.7 us (level)
  the two profiles are of different devices: /device:TPU:72 before, /device:TPU:1 now
where the time goes in v5:
time: 99.7 us; the launch traced here: 98.9 us
  starting transfers between devices  67.6 us (68%)
  waiting for transfers between devices  17.6 us (18%)
  Pallas kernels  13 us (13%)
    ppermute x4, starting transfers between devices, local(): lax.ppermute(forward_pair, 'fsdp', FSDP_UP[d])  18.7 us
    all_to_all x1, starting transfers between devices, local(): lax.all_to_all(cuts, ('section', 'fsdp', 'tp'), split_axis=0, concat_axis...  10.1 us
    all_to_all x1, starting transfers between devices, local(): lax.all_to_all(outgoing, 'fsdp', split_axis=0, concat_axis=0, tiled=False...  6.82 us
    pallas_call x1, Pallas kernels, run_backward(): pl.pallas_call(backward_kernel, out_shape=(jax.ShapeDtypeStruct((ROWS, 10...  6.06 us
    ppermute x1, starting transfers between devices, local(): query_back = lax.ppermute(held_queries[0], 'section', SECTION_PAIRS)  5.78 us
    all_to_all x1, waiting for transfers between devices, local(): lax.all_to_all(cuts, ('section', 'fsdp', 'tp'), split_axis=0, concat_axis...  5.62 us
    all_to_all x1, starting transfers between devices, local(): lax.all_to_all(send, 'fsdp', split_axis=0, concat_axis=0, tiled=False, ax...  5.58 us
    all_to_all x1, waiting for transfers between devices, local(): lax.all_to_all(send, 'fsdp', split_axis=0, concat_axis=0, tiled=False, ax...  5.01 us
  transfers between devices with their start and end apart: 14, of which 4 were waited for; matrix products, arithmetic and copies ran while one was open for 0% of the time, Pallas kernels for 6%

profile of v5, /device:TPU:1, one launch (start us, length us, event | category | flops | bytes accessed | tf_op | source)
XLA Modules:
  0.0 98.9 jit_solution(15258608768709297076)
XLA Ops:
  0.6 5.8 %collective-permute-start = (bf16[32,4096]{1,0:T(8,128)(2,1)}, bf16[32,4096]{1,0:T(8,128)(2,1)S(1)}, u32[]{:S(2)}, u32[]{:S(2)}) collective-permute-start(bf16[32,4096]{1,0:T(8,128)(2,1)} %bitcast.7), channel_id=1, source_target_pairs={{0,448},{64,384},{128,320},{192,256},{256,192},{320,128},{384,64},... | collective-permute-start | bytes 786440 | tf_op jit(solution)/shard_map/ppermute | solution.py:378
  6.4 1.6 %prepare.1 = (bf16[16,72,128]{2,1,0:T(8,128)(2,1)}, bf16[272,128]{1,0:T(8,128)(2,1)}) custom-call(bf16[1,32,512]{2,1,0:T(8,128)(2,1)} %held_key_ref.1, bf16[1,32,512]{2,1,0:T(8,128)(2,1)} %held_value_ref.1, s32[1,128]{1,0:T(1,128)} %held_ids_ref.1, bf16[1,128,128]{2,1,0:T(8,128)(2,1)} %key_ref.1, bf16[1,128,128]{2,1,0:T(8,128)(2,1)} %value_ref.1, ...), custom_call_target="tpu_custom_call" | custom-call | tf_op jit(solution)/shard_map/prepare/pallas_call | solution.py:296
  8.0 10.1 %all-to-all-start = ((bf16[16,72,128]{2,1,0:T(8,128)(2,1)}), bf16[16,72,128]{2,1,0:T(8,128)(2,1)S(1)}, u32[]{:S(2)}, u32[]{:S(2)}) async-start(bf16[16,72,128]{2,1,0:T(8,128)(2,1)} %get-tuple-element.27), calls=%async_computation | async-start | bytes 589824 | tf_op jit(solution)/shard_map/all_to_all | solution.py:391
  18.2 0.0 copy-start.2
  18.2 0.0 collective-permute-done.query_ref
  18.2 4.2 %collective-permute-start.1 = (bf16[2,32,1024]{2,1,0:T(8,128)(2,1)S(1)}, bf16[2,32,1024]{2,1,0:T(8,128)(2,1)S(1)}, u32[]{:S(2)}, u32[]{:S(2)}) collective-permute-start(bf16[2,32,1024]{2,1,0:T(8,128)(2,1)S(1)} %get-tuple-element.22), channel_id=1, source_target_pairs={{0,1},{1,0},{2,3},{3,2},{4,5},{5,4},{6,7},{7,6},{8,9},{9,8},{10,11... | collective-permute-start | bytes 393224 | tf_op jit(solution)/shard_map/ppermute | solution.py:403
  22.4 0.0 copy-done.2
  22.4 3.2 %collective-permute-start.2 = (bf16[272,128]{1,0:T(8,128)(2,1)S(1)}, bf16[272,128]{1,0:T(8,128)(2,1)S(1)}, u32[]{:S(2)}, u32[]{:S(2)}) collective-permute-start(bf16[272,128]{1,0:T(8,128)(2,1)S(1)} %copy-done.2), channel_id=1, source_target_pairs={{0,4},{4,8},{8,12},{12,16},{16,20},{20,24},{24,28},{28,32},{32,36}... | collective-permute-start | bytes 208904 | tf_op jit(solution)/shard_map/ppermute | solution.py:399
  25.6 5.6 %all-to-all-done.cuts_ref = bf16[16,72,128]{2,1,0:T(8,128)(2,1)S(1)} async-done(((bf16[16,72,128]{2,1,0:T(8,128)(2,1)}), bf16[16,72,128]{2,1,0:T(8,128)(2,1)S(1)}, u32[]{:S(2)}, u32[]{:S(2)}) %all-to-all-start) | async-done | bytes 294944 | tf_op jit(solution)/shard_map/all_to_all | solution.py:391
  31.2 0.9 outgoing.1
  32.2 6.8 %all-to-all-start.1 = ((bf16[8,272,128]{2,1,0:T(8,128)(2,1)}), bf16[8,272,128]{2,1,0:T(8,128)(2,1)S(1)}, u32[]{:S(2)}, u32[]{:S(2)}) async-start(bf16[8,272,128]{2,1,0:T(8,128)(2,1)} %get-tuple-element.29), calls=%async_computation.1 | async-start | bytes 1114112 | tf_op jit(solution)/shard_map/all_to_all | solution.py:411
  39.0 0.0 collective-permute-done.2.forward_before_ref
  39.0 0.0 collective-permute-done.1.near_ref
  39.0 0.0 copy-start
  39.0 7.4 %collective-permute-start.4 = (bf16[2,272,128]{2,1,0:T(8,128)(2,1)S(1)}, bf16[2,272,128]{2,1,0:T(8,128)(2,1)S(1)}, u32[]{:S(2)}, u32[]{:S(2)}) collective-permute-start(bf16[2,272,128]{2,1,0:T(8,128)(2,1)S(1)} %get-tuple-element.24.pair_0_ref), channel_id=1, source_target_pairs={{0,16},{4,20},{8,24},{12,28},{16,32},{20,36},{24,40},{28,44},{32,4... | collective-permute-start | bytes 417800 | tf_op jit(solution)/shard_map/ppermute | solution.py:427
  46.5 3.2 %collective-permute-start.7 = (bf16[2,32,1024]{2,1,0:T(8,128)(2,1)S(1)}, bf16[2,32,1024]{2,1,0:T(8,128)(2,1)S(1)}, u32[]{:S(2)}, u32[]{:S(2)}) collective-permute-start(bf16[2,32,1024]{2,1,0:T(8,128)(2,1)S(1)} %get-tuple-element.26), channel_id=1, source_target_pairs={{0,2},{1,3},{2,0},{3,1},{4,6},{5,7},{6,4},{7,5},{8,10},{9,11},{10,... | collective-permute-start | bytes 393224 | tf_op jit(solution)/shard_map/ppermute | solution.py:425
  49.7 3.6 %collective-permute-start.8 = (bf16[272,128]{1,0:T(8,128)(2,1)S(1)}, bf16[272,128]{1,0:T(8,128)(2,1)S(1)}, u32[]{:S(2)}, u32[]{:S(2)}) collective-permute-start(bf16[272,128]{1,0:T(8,128)(2,1)S(1)} %get-tuple-element.28.own_ref), channel_id=1, source_target_pairs={{0,36},{4,40},{8,44},{12,48},{16,52},{20,56},{24,60},{36,0},{40,4}... | collective-permute-start | bytes 208904 | tf_op jit(solution)/shard_map/ppermute | solution.py:426
  53.3 3.6 %collective-permute-done.7.far_ref = bf16[2,32,1024]{2,1,0:T(8,128)(2,1)S(1)} collective-permute-done((bf16[2,32,1024]{2,1,0:T(8,128)(2,1)S(1)}, bf16[2,32,1024]{2,1,0:T(8,128)(2,1)S(1)}, u32[]{:S(2)}, u32[]{:S(2)}) %collective-permute-start.7) | collective-permute-done | bytes 131104 | tf_op jit(solution)/shard_map/ppermute | solution.py:425
  56.9 0.0 collective-permute-done.4.pair_4_ref.refs_0_
  56.9 3.3 %collective-permute-done.8.nine_ref = bf16[272,128]{1,0:T(8,128)(2,1)S(1)} collective-permute-done((bf16[272,128]{1,0:T(8,128)(2,1)S(1)}, bf16[272,128]{1,0:T(8,128)(2,1)S(1)}, u32[]{:S(2)}, u32[]{:S(2)}) %collective-permute-start.8) | collective-permute-done | bytes 69664 | tf_op jit(solution)/shard_map/ppermute | solution.py:426
  60.2 0.0 all-to-all-done.1.slots_ref
  60.2 0.0 copy-done
  60.2 6.1 %backward_attention.1 = (bf16[128,1024]{1,0:T(8,128)(2,1)}, bf16[8,256,128]{2,1,0:T(8,128)(2,1)}, bf16[256,128]{1,0:T(8,128)(2,1)S(1)}, f32[256,128]{1,0:T(8,128)S(1)}) custom-call(bf16[2,32,1024]{2,1,0:T(8,128)(2,1)S(1)} %get-tuple-element.21.kept_ref, bf16[2,32,1024]{2,1,0:T(8,128)(2,1)S(1)} %collective-permute-done.1.near_ref, ...), custom_call_target="tpu_custom_call" | custom-call | flops 1000000 | tf_op jit(solution)/shard_map/backward_attention/pallas_call | solution.py:338
  66.3 5.6 %all-to-all-start.2 = ((bf16[8,256,128]{2,1,0:T(8,128)(2,1)}), bf16[8,256,128]{2,1,0:T(8,128)(2,1)S(1)}, u32[]{:S(2)}, u32[]{:S(2)}) async-start(bf16[8,256,128]{2,1,0:T(8,128)(2,1)} %get-tuple-element.31), calls=%async_computation.2 | async-start | bytes 1048576 | tf_op jit(solution)/shard_map/all_to_all | solution.py:432
  71.8 4.3 %collective-permute-start.3 = (bf16[2,272,128]{2,1,0:T(8,128)(2,1)S(1)}, bf16[2,272,128]{2,1,0:T(8,128)(2,1)S(1)}, u32[]{:S(2)}, u32[]{:S(2)}) collective-permute-start(bf16[2,272,128]{2,1,0:T(8,128)(2,1)S(1)} %get-tuple-element.24.pair_0_ref), channel_id=1, source_target_pairs={{0,8},{4,12},{8,16},{12,20},{16,24},{20,28},{24,32},{28,36},{32,40... | collective-permute-start | bytes 417800 | tf_op jit(solution)/shard_map/ppermute | solution.py:427
  76.1 5.5 %collective-permute-start.5 = (bf16[2,272,128]{2,1,0:T(8,128)(2,1)S(1)}, bf16[2,272,128]{2,1,0:T(8,128)(2,1)S(1)}, u32[]{:S(2)}, u32[]{:S(2)}) collective-permute-start(bf16[2,272,128]{2,1,0:T(8,128)(2,1)S(1)} %get-tuple-element.24.pair_0_ref), channel_id=1, source_target_pairs={{0,24},{4,28},{8,32},{12,36},{16,40},{20,44},{24,48},{28,52},{32,5... | collective-permute-start | bytes 417800 | tf_op jit(solution)/shard_map/ppermute | solution.py:427
  81.6 1.5 %collective-permute-start.6 = (bf16[2,272,128]{2,1,0:T(8,128)(2,1)S(1)}, bf16[2,272,128]{2,1,0:T(8,128)(2,1)S(1)}, u32[]{:S(2)}, u32[]{:S(2)}) collective-permute-start(bf16[2,272,128]{2,1,0:T(8,128)(2,1)S(1)} %get-tuple-element.24.pair_0_ref), channel_id=1, source_target_pairs={{0,32},{4,36},{8,40},{12,44},{16,48},{20,52},{24,56},{28,60},{1,33... | collective-permute-start | bytes 417800 | tf_op jit(solution)/shard_map/ppermute | solution.py:427
  83.1 1.9 %collective-permute-start.10 = (bf16[256,128]{1,0:T(8,128)(2,1)S(1)}, bf16[256,128]{1,0:T(8,128)(2,1)S(1)}, u32[]{:S(2)}, u32[]{:S(2)}) collective-permute-start(bf16[256,128]{1,0:T(8,128)(2,1)S(1)} %get-tuple-element.35), channel_id=1, source_target_pairs={{0,36},{4,40},{8,44},{12,48},{16,52},{20,56},{24,60},{36,0},{40,4}... | collective-permute-start | bytes 196616 | tf_op jit(solution)/shard_map/ppermute | solution.py:435
  85.1 5.0 %all-to-all-done.2.parts_ref = bf16[8,256,128]{2,1,0:T(8,128)(2,1)S(1)} async-done(((bf16[8,256,128]{2,1,0:T(8,128)(2,1)}), bf16[8,256,128]{2,1,0:T(8,128)(2,1)S(1)}, u32[]{:S(2)}, u32[]{:S(2)}) %all-to-all-start.2) | async-done | bytes 524320 | tf_op jit(solution)/shard_map/all_to_all | solution.py:432
  90.1 0.0 copy-start.1
  90.1 0.2 reduce.1
  90.3 4.5 %collective-permute-start.9 = (bf16[256,128]{1,0:T(8,128)(2,1)S(1)}, bf16[256,128]{1,0:T(8,128)(2,1)S(1)}, u32[]{:S(2)}, u32[]{:S(2)}) collective-permute-start(bf16[256,128]{1,0:T(8,128)(2,1)S(1)} %get-tuple-element.34), channel_id=1, source_target_pairs={{0,32},{4,36},{8,40},{12,44},{16,48},{20,52},{24,56},{28,60},{32,0... | collective-permute-start | bytes 196616 | tf_op jit(solution)/shard_map/ppermute | solution.py:447
  94.8 0.0 collective-permute-done.3.pair_2_ref
  94.8 0.0 collective-permute-done.5.pair_6_ref
  94.8 0.0 collective-permute-done.6.pair_8_ref
  94.8 0.0 copy-done.1
  94.8 3.5 %forward_attention.1 = (bf16[128,1024]{1,0:T(8,128)(2,1)}, f32[8,128]{1,0:T(8,128)}) custom-call(bf16[128,1024]{1,0:T(8,128)(2,1)S(1)} %bitcast.6, bf16[2,272,128]{2,1,0:T(8,128)(2,1)S(1)} %get-tuple-element.24.pair_0_ref, bf16[2,272,128]{2,1,0:T(8,128)(2,1)S(1)} %collective-permute-done.3.pair_2_ref, ...), custom_call_target="tpu_custom_call" | custom-call | flops 671088640 | bytes 3000000 | tf_op jit(solution)/shard_map/forward_attention/pallas_call | solution.py:315
  98.3 0.0 collective-permute-done.10.from_nine_ref
  98.3 0.0 collective-permute-done.9.from_upper_ref
  98.3 0.7 finish.1
  (2 shorter events, 0.0 us)
Async XLA Ops:
  0.6 17.5 %collective-permute-start = (bf16[32,4096]{1,0:T(8,128)(2,1)}, bf16[32,4096]{1,0:T(8,128)(2,1)S(1)}, u32[]{:S(2)}, u32[]{:S(2)}) collective-permute-start(bf16[32,4096]{1,0:T(8,128)(2,1)} %bitcast.7), channel_id=1, source_target_pairs={{0,448},{64,384},{128,320},{192,256},{256,192},{320,128},{384,64},... | collective-permute-start | bytes 786440 | tf_op jit(solution)/shard_map/ppermute | solution.py:378
  8.0 23.2 %all-to-all-start = ((bf16[16,72,128]{2,1,0:T(8,128)(2,1)}), bf16[16,72,128]{2,1,0:T(8,128)(2,1)S(1)}, u32[]{:S(2)}, u32[]{:S(2)}) async-start(bf16[16,72,128]{2,1,0:T(8,128)(2,1)} %get-tuple-element.27), calls=%async_computation | async-start | bytes 589824 | tf_op jit(solution)/shard_map/all_to_all | solution.py:391
  18.2 4.2 %copy-start.2 = (bf16[272,128]{1,0:T(8,128)(2,1)S(1)}, bf16[272,128]{1,0:T(8,128)(2,1)}, u32[]{:S(2)}) copy-start(bf16[272,128]{1,0:T(8,128)(2,1)} %get-tuple-element.23.forward_ref) | copy-start | bytes 208900
  18.2 20.8 %collective-permute-start.1 = (bf16[2,32,1024]{2,1,0:T(8,128)(2,1)S(1)}, bf16[2,32,1024]{2,1,0:T(8,128)(2,1)S(1)}, u32[]{:S(2)}, u32[]{:S(2)}) collective-permute-start(bf16[2,32,1024]{2,1,0:T(8,128)(2,1)S(1)} %get-tuple-element.22), channel_id=1, source_target_pairs={{0,1},{1,0},{2,3},{3,2},{4,5},{5,4},{6,7},{7,6},{8,9},{9,8},{10,11... | collective-permute-start | bytes 393224 | tf_op jit(solution)/shard_map/ppermute | solution.py:403
  22.4 16.6 %collective-permute-start.2 = (bf16[272,128]{1,0:T(8,128)(2,1)S(1)}, bf16[272,128]{1,0:T(8,128)(2,1)S(1)}, u32[]{:S(2)}, u32[]{:S(2)}) collective-permute-start(bf16[272,128]{1,0:T(8,128)(2,1)S(1)} %copy-done.2), channel_id=1, source_target_pairs={{0,4},{4,8},{8,12},{12,16},{16,20},{20,24},{24,28},{28,32},{32,36}... | collective-permute-start | bytes 208904 | tf_op jit(solution)/shard_map/ppermute | solution.py:399
  32.2 28.0 %all-to-all-start.1 = ((bf16[8,272,128]{2,1,0:T(8,128)(2,1)}), bf16[8,272,128]{2,1,0:T(8,128)(2,1)S(1)}, u32[]{:S(2)}, u32[]{:S(2)}) async-start(bf16[8,272,128]{2,1,0:T(8,128)(2,1)} %get-tuple-element.29), calls=%async_computation.1 | async-start | bytes 1114112 | tf_op jit(solution)/shard_map/all_to_all | solution.py:411
  39.0 21.2 %copy-start = (bf16[1,128,1024]{2,1,0:T(8,128)(2,1)S(1)}, bf16[1,128,1024]{2,1,0:T(8,128)(2,1)}, u32[]{:S(2)}) copy-start(bf16[1,128,1024]{2,1,0:T(8,128)(2,1)} %param.17) | copy-start | bytes 786436
  39.0 17.9 %collective-permute-start.4 = (bf16[2,272,128]{2,1,0:T(8,128)(2,1)S(1)}, bf16[2,272,128]{2,1,0:T(8,128)(2,1)S(1)}, u32[]{:S(2)}, u32[]{:S(2)}) collective-permute-start(bf16[2,272,128]{2,1,0:T(8,128)(2,1)S(1)} %get-tuple-element.24.pair_0_ref), channel_id=1, source_target_pairs={{0,16},{4,20},{8,24},{12,28},{16,32},{20,36},{24,40},{28,44},{32,4... | collective-permute-start | bytes 417800 | tf_op jit(solution)/shard_map/ppermute | solution.py:427
  46.5 10.4 %collective-permute-start.7 = (bf16[2,32,1024]{2,1,0:T(8,128)(2,1)S(1)}, bf16[2,32,1024]{2,1,0:T(8,128)(2,1)S(1)}, u32[]{:S(2)}, u32[]{:S(2)}) collective-permute-start(bf16[2,32,1024]{2,1,0:T(8,128)(2,1)S(1)} %get-tuple-element.26), channel_id=1, source_target_pairs={{0,2},{1,3},{2,0},{3,1},{4,6},{5,7},{6,4},{7,5},{8,10},{9,11},{10,... | collective-permute-start | bytes 393224 | tf_op jit(solution)/shard_map/ppermute | solution.py:425
  49.7 10.5 %collective-permute-start.8 = (bf16[272,128]{1,0:T(8,128)(2,1)S(1)}, bf16[272,128]{1,0:T(8,128)(2,1)S(1)}, u32[]{:S(2)}, u32[]{:S(2)}) collective-permute-start(bf16[272,128]{1,0:T(8,128)(2,1)S(1)} %get-tuple-element.28.own_ref), channel_id=1, source_target_pairs={{0,36},{4,40},{8,44},{12,48},{16,52},{20,56},{24,60},{36,0},{40,4}... | collective-permute-start | bytes 208904 | tf_op jit(solution)/shard_map/ppermute | solution.py:426
  66.3 23.8 %all-to-all-start.2 = ((bf16[8,256,128]{2,1,0:T(8,128)(2,1)}), bf16[8,256,128]{2,1,0:T(8,128)(2,1)S(1)}, u32[]{:S(2)}, u32[]{:S(2)}) async-start(bf16[8,256,128]{2,1,0:T(8,128)(2,1)} %get-tuple-element.31), calls=%async_computation.2 | async-start | bytes 1048576 | tf_op jit(solution)/shard_map/all_to_all | solution.py:432
  71.8 22.9 %collective-permute-start.3 = (bf16[2,272,128]{2,1,0:T(8,128)(2,1)S(1)}, bf16[2,272,128]{2,1,0:T(8,128)(2,1)S(1)}, u32[]{:S(2)}, u32[]{:S(2)}) collective-permute-start(bf16[2,272,128]{2,1,0:T(8,128)(2,1)S(1)} %get-tuple-element.24.pair_0_ref), channel_id=1, source_target_pairs={{0,8},{4,12},{8,16},{12,20},{16,24},{20,28},{24,32},{28,36},{32,40... | collective-permute-start | bytes 417800 | tf_op jit(solution)/shard_map/ppermute | solution.py:427
  76.1 18.7 %collective-permute-start.5 = (bf16[2,272,128]{2,1,0:T(8,128)(2,1)S(1)}, bf16[2,272,128]{2,1,0:T(8,128)(2,1)S(1)}, u32[]{:S(2)}, u32[]{:S(2)}) collective-permute-start(bf16[2,272,128]{2,1,0:T(8,128)(2,1)S(1)} %get-tuple-element.24.pair_0_ref), channel_id=1, source_target_pairs={{0,24},{4,28},{8,32},{12,36},{16,40},{20,44},{24,48},{28,52},{32,5... | collective-permute-start | bytes 417800 | tf_op jit(solution)/shard_map/ppermute | solution.py:427
  81.6 13.1 %collective-permute-start.6 = (bf16[2,272,128]{2,1,0:T(8,128)(2,1)S(1)}, bf16[2,272,128]{2,1,0:T(8,128)(2,1)S(1)}, u32[]{:S(2)}, u32[]{:S(2)}) collective-permute-start(bf16[2,272,128]{2,1,0:T(8,128)(2,1)S(1)} %get-tuple-element.24.pair_0_ref), channel_id=1, source_target_pairs={{0,32},{4,36},{8,40},{12,44},{16,48},{20,52},{24,56},{28,60},{1,33... | collective-permute-start | bytes 417800 | tf_op jit(solution)/shard_map/ppermute | solution.py:427
  83.1 15.1 %collective-permute-start.10 = (bf16[256,128]{1,0:T(8,128)(2,1)S(1)}, bf16[256,128]{1,0:T(8,128)(2,1)S(1)}, u32[]{:S(2)}, u32[]{:S(2)}) collective-permute-start(bf16[256,128]{1,0:T(8,128)(2,1)S(1)} %get-tuple-element.35), channel_id=1, source_target_pairs={{0,36},{4,40},{8,44},{12,48},{16,52},{20,56},{24,60},{36,0},{40,4}... | collective-permute-start | bytes 196616 | tf_op jit(solution)/shard_map/ppermute | solution.py:435
  90.1 4.7 %copy-start.1 = (bf16[1,128,1024]{2,1,0:T(8,128)(2,1)S(1)}, bf16[1,128,1024]{2,1,0:T(8,128)(2,1)}, u32[]{:S(2)}) copy-start(bf16[1,128,1024]{2,1,0:T(8,128)(2,1)} %param.9) | copy-start | bytes 786436
  90.3 8.0 %collective-permute-start.9 = (bf16[256,128]{1,0:T(8,128)(2,1)S(1)}, bf16[256,128]{1,0:T(8,128)(2,1)S(1)}, u32[]{:S(2)}, u32[]{:S(2)}) collective-permute-start(bf16[256,128]{1,0:T(8,128)(2,1)S(1)} %get-tuple-element.34), channel_id=1, source_target_pairs={{0,32},{4,36},{8,40},{12,44},{16,48},{20,52},{24,56},{28,60},{32,0... | collective-permute-start | bytes 196616 | tf_op jit(solution)/shard_map/ppermute | solution.py:447

commit v6 on v5

--- a/solution.py
+++ b/solution.py
@@ -21,7 +21,7 @@
 VMEM_LIMIT = 24 * 1024 * 1024
 SMALL_LIMIT = 8 * 1024 * 1024
 
-BLOCK = 2 * ROWS + 16
+BLOCK = 2 * ROWS + 8
 CUT = 2 * PIECE + 8
 
 FSDP_UP = {d: [(f, f + d) for f in range(16 - d)] for d in (1, 2, 4, 6, 8)}
@@ -212,13 +212,13 @@
 
 
 def wide_ids(ids_ref):
-    return jnp.broadcast_to(ids_ref[...].astype(jnp.float32), (16, 128)).astype(jnp.bfloat16)
+    return jnp.broadcast_to(ids_ref[...].astype(jnp.float32), (8, 128)).astype(jnp.bfloat16)
 
 
 def prepare_kernel(
     held_key_ref, held_value_ref, held_ids_ref, key_ref, value_ref, ids_ref, cut_ref, forward_ref
 ):
-    held_ids = wide_ids(held_ids_ref)[0:8]
+    held_ids = wide_ids(held_ids_ref)
     for t in range(PIECES):
         cut = jnp.concatenate(
             [
@@ -259,7 +259,7 @@
         cuts = [cuts_ref[first + piece] for piece in range(PIECES)]
         ids = cuts[0][2 * PIECE :]
         return jnp.concatenate(
-            [cut[:PIECE] for cut in cuts] + [cut[PIECE : 2 * PIECE] for cut in cuts] + [ids, ids],
+            [cut[:PIECE] for cut in cuts] + [cut[PIECE : 2 * PIECE] for cut in cuts] + [ids],
             axis=0,
         )
 

time: 99.7 us -> 99.2 us (level)
  waiting for transfers between devices: 17.6 us -> 13.8 us
  starting transfers between devices: 67.6 us -> 70.8 us
    ppermute x1, starting transfers between devices: 4.46 us -> 7.62 us  [local(): from_upper = lax.ppermute(other_row, 'fsdp', FSDP_SWAP)]
    all_to_all x1, waiting for transfers between devices: 5.01 us -> 1.87 us  [local(): lax.all_to_all(send, 'fsdp', split_axis=0, concat_axis=0, tiled=False, ax...]
where the time goes in v6:
time: 99.2 us; the launch traced here: 98.4 us
  starting transfers between devices  70.8 us (71%)
  waiting for transfers between devices  13.8 us (14%)
  Pallas kernels  12.9 us (13%)
    ppermute x4, starting transfers between devices, local(): lax.ppermute(forward_pair, 'fsdp', FSDP_UP[d])  18.7 us
    all_to_all x1, starting transfers between devices, local(): lax.all_to_all(cuts, ('section', 'fsdp', 'tp'), split_axis=0, concat_axis...  10.1 us
    ppermute x1, starting transfers between devices, local(): from_upper = lax.ppermute(other_row, 'fsdp', FSDP_SWAP)  7.62 us
    all_to_all x1, starting transfers between devices, local(): lax.all_to_all(outgoing, 'fsdp', split_axis=0, concat_axis=0, tiled=False...  6.82 us
    pallas_call x1, Pallas kernels, run_backward(): pl.pallas_call(backward_kernel, out_shape=(jax.ShapeDtypeStruct((ROWS, 10...  6.06 us
    ppermute x1, starting transfers between devices, local(): query_back = lax.ppermute(held_queries[0], 'section', SECTION_PAIRS)  5.78 us
    all_to_all x1, waiting for transfers between devices, local(): lax.all_to_all(cuts, ('section', 'fsdp', 'tp'), split_axis=0, concat_axis...  5.62 us
    all_to_all x1, starting transfers between devices, local(): lax.all_to_all(send, 'fsdp', split_axis=0, concat_axis=0, tiled=False, ax...  5.62 us
  transfers between devices with their start and end apart: 14, of which 4 were waited for; matrix products, arithmetic and copies ran while one was open for 0% of the time, Pallas kernels for 6%

profile of v6, /device:TPU:1, one launch (start us, length us, event | category | flops | bytes accessed | tf_op | source)
XLA Modules:
  0.0 98.4 jit_solution(1518749001253442159)
XLA Ops:
  0.6 5.8 %collective-permute-start = (bf16[32,4096]{1,0:T(8,128)(2,1)}, bf16[32,4096]{1,0:T(8,128)(2,1)S(1)}, u32[]{:S(2)}, u32[]{:S(2)}) collective-permute-start(bf16[32,4096]{1,0:T(8,128)(2,1)} %bitcast.7), channel_id=1, source_target_pairs={{0,448},{64,384},{128,320},{192,256},{256,192},{320,128},{384,64},... | collective-permute-start | bytes 786440 | tf_op jit(solution)/shard_map/ppermute | solution.py:378
  6.4 1.6 %prepare.1 = (bf16[16,72,128]{2,1,0:T(8,128)(2,1)}, bf16[264,128]{1,0:T(8,128)(2,1)}) custom-call(bf16[1,32,512]{2,1,0:T(8,128)(2,1)} %held_key_ref.1, bf16[1,32,512]{2,1,0:T(8,128)(2,1)} %held_value_ref.1, s32[1,128]{1,0:T(1,128)} %held_ids_ref.1, bf16[1,128,128]{2,1,0:T(8,128)(2,1)} %key_ref.1, bf16[1,128,128]{2,1,0:T(8,128)(2,1)} %value_ref.1, ...), custom_call_target="tpu_custom_call" | custom-call | tf_op jit(solution)/shard_map/prepare/pallas_call | solution.py:296
  8.0 10.1 %all-to-all-start = ((bf16[16,72,128]{2,1,0:T(8,128)(2,1)}), bf16[16,72,128]{2,1,0:T(8,128)(2,1)S(1)}, u32[]{:S(2)}, u32[]{:S(2)}) async-start(bf16[16,72,128]{2,1,0:T(8,128)(2,1)} %get-tuple-element.27), calls=%async_computation | async-start | bytes 589824 | tf_op jit(solution)/shard_map/all_to_all | solution.py:391
  18.2 0.0 copy-start.2
  18.2 0.0 collective-permute-done.query_ref
  18.2 4.2 %collective-permute-start.1 = (bf16[2,32,1024]{2,1,0:T(8,128)(2,1)S(1)}, bf16[2,32,1024]{2,1,0:T(8,128)(2,1)S(1)}, u32[]{:S(2)}, u32[]{:S(2)}) collective-permute-start(bf16[2,32,1024]{2,1,0:T(8,128)(2,1)S(1)} %get-tuple-element.22), channel_id=1, source_target_pairs={{0,1},{1,0},{2,3},{3,2},{4,5},{5,4},{6,7},{7,6},{8,9},{9,8},{10,11... | collective-permute-start | bytes 393224 | tf_op jit(solution)/shard_map/ppermute | solution.py:403
  22.4 0.0 copy-done.2
  22.4 3.2 %collective-permute-start.2 = (bf16[264,128]{1,0:T(8,128)(2,1)S(1)}, bf16[264,128]{1,0:T(8,128)(2,1)S(1)}, u32[]{:S(2)}, u32[]{:S(2)}) collective-permute-start(bf16[264,128]{1,0:T(8,128)(2,1)S(1)} %copy-done.2), channel_id=1, source_target_pairs={{0,4},{4,8},{8,12},{12,16},{16,20},{20,24},{24,28},{28,32},{32,36}... | collective-permute-start | bytes 202760 | tf_op jit(solution)/shard_map/ppermute | solution.py:399
  25.6 5.6 %all-to-all-done.cuts_ref = bf16[16,72,128]{2,1,0:T(8,128)(2,1)S(1)} async-done(((bf16[16,72,128]{2,1,0:T(8,128)(2,1)}), bf16[16,72,128]{2,1,0:T(8,128)(2,1)S(1)}, u32[]{:S(2)}, u32[]{:S(2)}) %all-to-all-start) | async-done | bytes 294944 | tf_op jit(solution)/shard_map/all_to_all | solution.py:391
  31.2 0.9 outgoing.1
  32.1 6.8 %all-to-all-start.1 = ((bf16[8,264,128]{2,1,0:T(8,128)(2,1)}), bf16[8,264,128]{2,1,0:T(8,128)(2,1)S(1)}, u32[]{:S(2)}, u32[]{:S(2)}) async-start(bf16[8,264,128]{2,1,0:T(8,128)(2,1)} %get-tuple-element.29), calls=%async_computation.1 | async-start | bytes 1081344 | tf_op jit(solution)/shard_map/all_to_all | solution.py:411
  39.0 0.0 collective-permute-done.2.forward_before_ref
  39.0 0.0 collective-permute-done.1.near_ref
  39.0 0.0 copy-start
  39.0 7.4 %collective-permute-start.4 = (bf16[2,264,128]{2,1,0:T(8,128)(2,1)S(1)}, bf16[2,264,128]{2,1,0:T(8,128)(2,1)S(1)}, u32[]{:S(2)}, u32[]{:S(2)}) collective-permute-start(bf16[2,264,128]{2,1,0:T(8,128)(2,1)S(1)} %get-tuple-element.24.pair_0_ref), channel_id=1, source_target_pairs={{0,16},{4,20},{8,24},{12,28},{16,32},{20,36},{24,40},{28,44},{32,4... | collective-permute-start | bytes 405512 | tf_op jit(solution)/shard_map/ppermute | solution.py:427
  46.4 3.2 %collective-permute-start.7 = (bf16[2,32,1024]{2,1,0:T(8,128)(2,1)S(1)}, bf16[2,32,1024]{2,1,0:T(8,128)(2,1)S(1)}, u32[]{:S(2)}, u32[]{:S(2)}) collective-permute-start(bf16[2,32,1024]{2,1,0:T(8,128)(2,1)S(1)} %get-tuple-element.26), channel_id=1, source_target_pairs={{0,2},{1,3},{2,0},{3,1},{4,6},{5,7},{6,4},{7,5},{8,10},{9,11},{10,... | collective-permute-start | bytes 393224 | tf_op jit(solution)/shard_map/ppermute | solution.py:425
  49.6 3.6 %collective-permute-start.8 = (bf16[264,128]{1,0:T(8,128)(2,1)S(1)}, bf16[264,128]{1,0:T(8,128)(2,1)S(1)}, u32[]{:S(2)}, u32[]{:S(2)}) collective-permute-start(bf16[264,128]{1,0:T(8,128)(2,1)S(1)} %get-tuple-element.28.own_ref), channel_id=1, source_target_pairs={{0,36},{4,40},{8,44},{12,48},{16,52},{20,56},{24,60},{36,0},{40,4}... | collective-permute-start | bytes 202760 | tf_op jit(solution)/shard_map/ppermute | solution.py:426
  53.3 3.6 %collective-permute-done.7.far_ref = bf16[2,32,1024]{2,1,0:T(8,128)(2,1)S(1)} collective-permute-done((bf16[2,32,1024]{2,1,0:T(8,128)(2,1)S(1)}, bf16[2,32,1024]{2,1,0:T(8,128)(2,1)S(1)}, u32[]{:S(2)}, u32[]{:S(2)}) %collective-permute-start.7) | collective-permute-done | bytes 131104 | tf_op jit(solution)/shard_map/ppermute | solution.py:425
  56.9 0.0 collective-permute-done.4.pair_4_ref.refs_0_
  56.9 2.7 %collective-permute-done.8.nine_ref = bf16[264,128]{1,0:T(8,128)(2,1)S(1)} collective-permute-done((bf16[264,128]{1,0:T(8,128)(2,1)S(1)}, bf16[264,128]{1,0:T(8,128)(2,1)S(1)}, u32[]{:S(2)}, u32[]{:S(2)}) %collective-permute-start.8) | collective-permute-done | bytes 67616 | tf_op jit(solution)/shard_map/ppermute | solution.py:426
  59.6 0.0 all-to-all-done.1.slots_ref
  59.6 0.0 copy-done
  59.6 6.1 %backward_attention.1 = (bf16[128,1024]{1,0:T(8,128)(2,1)}, bf16[8,256,128]{2,1,0:T(8,128)(2,1)}, bf16[256,128]{1,0:T(8,128)(2,1)S(1)}, f32[256,128]{1,0:T(8,128)S(1)}) custom-call(bf16[2,32,1024]{2,1,0:T(8,128)(2,1)S(1)} %get-tuple-element.21.kept_ref, bf16[2,32,1024]{2,1,0:T(8,128)(2,1)S(1)} %collective-permute-done.1.near_ref, ...), custom_call_target="tpu_custom_call" | custom-call | flops 1000000 | tf_op jit(solution)/shard_map/backward_attention/pallas_call | solution.py:338
  65.7 5.6 %all-to-all-start.2 = ((bf16[8,256,128]{2,1,0:T(8,128)(2,1)}), bf16[8,256,128]{2,1,0:T(8,128)(2,1)S(1)}, u32[]{:S(2)}, u32[]{:S(2)}) async-start(bf16[8,256,128]{2,1,0:T(8,128)(2,1)} %get-tuple-element.31), calls=%async_computation.2 | async-start | bytes 1048576 | tf_op jit(solution)/shard_map/all_to_all | solution.py:432
  71.3 4.3 %collective-permute-start.3 = (bf16[2,264,128]{2,1,0:T(8,128)(2,1)S(1)}, bf16[2,264,128]{2,1,0:T(8,128)(2,1)S(1)}, u32[]{:S(2)}, u32[]{:S(2)}) collective-permute-start(bf16[2,264,128]{2,1,0:T(8,128)(2,1)S(1)} %get-tuple-element.24.pair_0_ref), channel_id=1, source_target_pairs={{0,8},{4,12},{8,16},{12,20},{16,24},{20,28},{24,32},{28,36},{32,40... | collective-permute-start | bytes 405512 | tf_op jit(solution)/shard_map/ppermute | solution.py:427
  75.6 5.5 %collective-permute-start.5 = (bf16[2,264,128]{2,1,0:T(8,128)(2,1)S(1)}, bf16[2,264,128]{2,1,0:T(8,128)(2,1)S(1)}, u32[]{:S(2)}, u32[]{:S(2)}) collective-permute-start(bf16[2,264,128]{2,1,0:T(8,128)(2,1)S(1)} %get-tuple-element.24.pair_0_ref), channel_id=1, source_target_pairs={{0,24},{4,28},{8,32},{12,36},{16,40},{20,44},{24,48},{28,52},{32,5... | collective-permute-start | bytes 405512 | tf_op jit(solution)/shard_map/ppermute | solution.py:427
  81.1 1.5 %collective-permute-start.6 = (bf16[2,264,128]{2,1,0:T(8,128)(2,1)S(1)}, bf16[2,264,128]{2,1,0:T(8,128)(2,1)S(1)}, u32[]{:S(2)}, u32[]{:S(2)}) collective-permute-start(bf16[2,264,128]{2,1,0:T(8,128)(2,1)S(1)} %get-tuple-element.24.pair_0_ref), channel_id=1, source_target_pairs={{0,32},{4,36},{8,40},{12,44},{16,48},{20,52},{24,56},{28,60},{1,33... | collective-permute-start | bytes 405512 | tf_op jit(solution)/shard_map/ppermute | solution.py:427
  82.6 1.9 %collective-permute-start.10 = (bf16[256,128]{1,0:T(8,128)(2,1)S(1)}, bf16[256,128]{1,0:T(8,128)(2,1)S(1)}, u32[]{:S(2)}, u32[]{:S(2)}) collective-permute-start(bf16[256,128]{1,0:T(8,128)(2,1)S(1)} %get-tuple-element.35), channel_id=1, source_target_pairs={{0,36},{4,40},{8,44},{12,48},{16,52},{20,56},{24,60},{36,0},{40,4}... | collective-permute-start | bytes 196616 | tf_op jit(solution)/shard_map/ppermute | solution.py:435
  84.5 1.9 %all-to-all-done.2.parts_ref = bf16[8,256,128]{2,1,0:T(8,128)(2,1)S(1)} async-done(((bf16[8,256,128]{2,1,0:T(8,128)(2,1)}), bf16[8,256,128]{2,1,0:T(8,128)(2,1)S(1)}, u32[]{:S(2)}, u32[]{:S(2)}) %all-to-all-start.2) | async-done | bytes 524320 | tf_op jit(solution)/shard_map/all_to_all | solution.py:432
  86.4 0.0 copy-start.1
  86.4 0.2 reduce.1
  86.6 7.6 %collective-permute-start.9 = (bf16[256,128]{1,0:T(8,128)(2,1)S(1)}, bf16[256,128]{1,0:T(8,128)(2,1)S(1)}, u32[]{:S(2)}, u32[]{:S(2)}) collective-permute-start(bf16[256,128]{1,0:T(8,128)(2,1)S(1)} %get-tuple-element.34), channel_id=1, source_target_pairs={{0,32},{4,36},{8,40},{12,44},{16,48},{20,52},{24,56},{28,60},{32,0... | collective-permute-start | bytes 196616 | tf_op jit(solution)/shard_map/ppermute | solution.py:447
  94.2 0.0 collective-permute-done.3.pair_2_ref
  94.2 0.0 collective-permute-done.5.pair_6_ref
  94.3 0.0 collective-permute-done.6.pair_8_ref
  94.3 0.0 copy-done.1
  94.3 3.5 %forward_attention.1 = (bf16[128,1024]{1,0:T(8,128)(2,1)}, f32[8,128]{1,0:T(8,128)}) custom-call(bf16[128,1024]{1,0:T(8,128)(2,1)S(1)} %bitcast.6, bf16[2,264,128]{2,1,0:T(8,128)(2,1)S(1)} %get-tuple-element.24.pair_0_ref, bf16[2,264,128]{2,1,0:T(8,128)(2,1)S(1)} %collective-permute-done.3.pair_2_ref, ...), custom_call_target="tpu_custom_call" | custom-call | flops 671088640 | bytes 3000000 | tf_op jit(solution)/shard_map/forward_attention/pallas_call | solution.py:315
  97.8 0.0 collective-permute-done.10.from_nine_ref
  97.8 0.0 collective-permute-done.9.from_upper_ref
  97.8 0.7 finish.1
  (2 shorter events, 0.0 us)
Async XLA Ops:
  0.6 17.5 %collective-permute-start = (bf16[32,4096]{1,0:T(8,128)(2,1)}, bf16[32,4096]{1,0:T(8,128)(2,1)S(1)}, u32[]{:S(2)}, u32[]{:S(2)}) collective-permute-start(bf16[32,4096]{1,0:T(8,128)(2,1)} %bitcast.7), channel_id=1, source_target_pairs={{0,448},{64,384},{128,320},{192,256},{256,192},{320,128},{384,64},... | collective-permute-start | bytes 786440 | tf_op jit(solution)/shard_map/ppermute | solution.py:378
  8.0 23.2 %all-to-all-start = ((bf16[16,72,128]{2,1,0:T(8,128)(2,1)}), bf16[16,72,128]{2,1,0:T(8,128)(2,1)S(1)}, u32[]{:S(2)}, u32[]{:S(2)}) async-start(bf16[16,72,128]{2,1,0:T(8,128)(2,1)} %get-tuple-element.27), calls=%async_computation | async-start | bytes 589824 | tf_op jit(solution)/shard_map/all_to_all | solution.py:391
  18.2 4.2 %copy-start.2 = (bf16[264,128]{1,0:T(8,128)(2,1)S(1)}, bf16[264,128]{1,0:T(8,128)(2,1)}, u32[]{:S(2)}) copy-start(bf16[264,128]{1,0:T(8,128)(2,1)} %get-tuple-element.23.forward_ref) | copy-start | bytes 202756
  18.2 20.7 %collective-permute-start.1 = (bf16[2,32,1024]{2,1,0:T(8,128)(2,1)S(1)}, bf16[2,32,1024]{2,1,0:T(8,128)(2,1)S(1)}, u32[]{:S(2)}, u32[]{:S(2)}) collective-permute-start(bf16[2,32,1024]{2,1,0:T(8,128)(2,1)S(1)} %get-tuple-element.22), channel_id=1, source_target_pairs={{0,1},{1,0},{2,3},{3,2},{4,5},{5,4},{6,7},{7,6},{8,9},{9,8},{10,11... | collective-permute-start | bytes 393224 | tf_op jit(solution)/shard_map/ppermute | solution.py:403
  22.4 16.6 %collective-permute-start.2 = (bf16[264,128]{1,0:T(8,128)(2,1)S(1)}, bf16[264,128]{1,0:T(8,128)(2,1)S(1)}, u32[]{:S(2)}, u32[]{:S(2)}) collective-permute-start(bf16[264,128]{1,0:T(8,128)(2,1)S(1)} %copy-done.2), channel_id=1, source_target_pairs={{0,4},{4,8},{8,12},{12,16},{16,20},{20,24},{24,28},{28,32},{32,36}... | collective-permute-start | bytes 202760 | tf_op jit(solution)/shard_map/ppermute | solution.py:399
  32.1 27.5 %all-to-all-start.1 = ((bf16[8,264,128]{2,1,0:T(8,128)(2,1)}), bf16[8,264,128]{2,1,0:T(8,128)(2,1)S(1)}, u32[]{:S(2)}, u32[]{:S(2)}) async-start(bf16[8,264,128]{2,1,0:T(8,128)(2,1)} %get-tuple-element.29), calls=%async_computation.1 | async-start | bytes 1081344 | tf_op jit(solution)/shard_map/all_to_all | solution.py:411
  39.0 20.6 %copy-start = (bf16[1,128,1024]{2,1,0:T(8,128)(2,1)S(1)}, bf16[1,128,1024]{2,1,0:T(8,128)(2,1)}, u32[]{:S(2)}) copy-start(bf16[1,128,1024]{2,1,0:T(8,128)(2,1)} %param.17) | copy-start | bytes 786436
  39.0 17.9 %collective-permute-start.4 = (bf16[2,264,128]{2,1,0:T(8,128)(2,1)S(1)}, bf16[2,264,128]{2,1,0:T(8,128)(2,1)S(1)}, u32[]{:S(2)}, u32[]{:S(2)}) collective-permute-start(bf16[2,264,128]{2,1,0:T(8,128)(2,1)S(1)} %get-tuple-element.24.pair_0_ref), channel_id=1, source_target_pairs={{0,16},{4,20},{8,24},{12,28},{16,32},{20,36},{24,40},{28,44},{32,4... | collective-permute-start | bytes 405512 | tf_op jit(solution)/shard_map/ppermute | solution.py:427
  46.4 10.4 %collective-permute-start.7 = (bf16[2,32,1024]{2,1,0:T(8,128)(2,1)S(1)}, bf16[2,32,1024]{2,1,0:T(8,128)(2,1)S(1)}, u32[]{:S(2)}, u32[]{:S(2)}) collective-permute-start(bf16[2,32,1024]{2,1,0:T(8,128)(2,1)S(1)} %get-tuple-element.26), channel_id=1, source_target_pairs={{0,2},{1,3},{2,0},{3,1},{4,6},{5,7},{6,4},{7,5},{8,10},{9,11},{10,... | collective-permute-start | bytes 393224 | tf_op jit(solution)/shard_map/ppermute | solution.py:425
  49.6 10.0 %collective-permute-start.8 = (bf16[264,128]{1,0:T(8,128)(2,1)S(1)}, bf16[264,128]{1,0:T(8,128)(2,1)S(1)}, u32[]{:S(2)}, u32[]{:S(2)}) collective-permute-start(bf16[264,128]{1,0:T(8,128)(2,1)S(1)} %get-tuple-element.28.own_ref), channel_id=1, source_target_pairs={{0,36},{4,40},{8,44},{12,48},{16,52},{20,56},{24,60},{36,0},{40,4}... | collective-permute-start | bytes 202760 | tf_op jit(solution)/shard_map/ppermute | solution.py:426
  65.7 20.7 %all-to-all-start.2 = ((bf16[8,256,128]{2,1,0:T(8,128)(2,1)}), bf16[8,256,128]{2,1,0:T(8,128)(2,1)S(1)}, u32[]{:S(2)}, u32[]{:S(2)}) async-start(bf16[8,256,128]{2,1,0:T(8,128)(2,1)} %get-tuple-element.31), calls=%async_computation.2 | async-start | bytes 1048576 | tf_op jit(solution)/shard_map/all_to_all | solution.py:432
  71.3 22.9 %collective-permute-start.3 = (bf16[2,264,128]{2,1,0:T(8,128)(2,1)S(1)}, bf16[2,264,128]{2,1,0:T(8,128)(2,1)S(1)}, u32[]{:S(2)}, u32[]{:S(2)}) collective-permute-start(bf16[2,264,128]{2,1,0:T(8,128)(2,1)S(1)} %get-tuple-element.24.pair_0_ref), channel_id=1, source_target_pairs={{0,8},{4,12},{8,16},{12,20},{16,24},{20,28},{24,32},{28,36},{32,40... | collective-permute-start | bytes 405512 | tf_op jit(solution)/shard_map/ppermute | solution.py:427
  75.6 18.7 %collective-permute-start.5 = (bf16[2,264,128]{2,1,0:T(8,128)(2,1)S(1)}, bf16[2,264,128]{2,1,0:T(8,128)(2,1)S(1)}, u32[]{:S(2)}, u32[]{:S(2)}) collective-permute-start(bf16[2,264,128]{2,1,0:T(8,128)(2,1)S(1)} %get-tuple-element.24.pair_0_ref), channel_id=1, source_target_pairs={{0,24},{4,28},{8,32},{12,36},{16,40},{20,44},{24,48},{28,52},{32,5... | collective-permute-start | bytes 405512 | tf_op jit(solution)/shard_map/ppermute | solution.py:427
  81.1 13.2 %collective-permute-start.6 = (bf16[2,264,128]{2,1,0:T(8,128)(2,1)S(1)}, bf16[2,264,128]{2,1,0:T(8,128)(2,1)S(1)}, u32[]{:S(2)}, u32[]{:S(2)}) collective-permute-start(bf16[2,264,128]{2,1,0:T(8,128)(2,1)S(1)} %get-tuple-element.24.pair_0_ref), channel_id=1, source_target_pairs={{0,32},{4,36},{8,40},{12,44},{16,48},{20,52},{24,56},{28,60},{1,33... | collective-permute-start | bytes 405512 | tf_op jit(solution)/shard_map/ppermute | solution.py:427
  82.6 15.2 %collective-permute-start.10 = (bf16[256,128]{1,0:T(8,128)(2,1)S(1)}, bf16[256,128]{1,0:T(8,128)(2,1)S(1)}, u32[]{:S(2)}, u32[]{:S(2)}) collective-permute-start(bf16[256,128]{1,0:T(8,128)(2,1)S(1)} %get-tuple-element.35), channel_id=1, source_target_pairs={{0,36},{4,40},{8,44},{12,48},{16,52},{20,56},{24,60},{36,0},{40,4}... | collective-permute-start | bytes 196616 | tf_op jit(solution)/shard_map/ppermute | solution.py:435
  86.4 7.9 %copy-start.1 = (bf16[1,128,1024]{2,1,0:T(8,128)(2,1)S(1)}, bf16[1,128,1024]{2,1,0:T(8,128)(2,1)}, u32[]{:S(2)}) copy-start(bf16[1,128,1024]{2,1,0:T(8,128)(2,1)} %param.9) | copy-start | bytes 786436
  86.6 11.2 %collective-permute-start.9 = (bf16[256,128]{1,0:T(8,128)(2,1)S(1)}, bf16[256,128]{1,0:T(8,128)(2,1)S(1)}, u32[]{:S(2)}, u32[]{:S(2)}) collective-permute-start(bf16[256,128]{1,0:T(8,128)(2,1)S(1)} %get-tuple-element.34), channel_id=1, source_target_pairs={{0,32},{4,36},{8,40},{12,44},{16,48},{20,52},{24,56},{28,60},{32,0... | collective-permute-start | bytes 196616 | tf_op jit(solution)/shard_map/ppermute | solution.py:447
